TPU v7x, 32 devices: a whole 2x2x4 slice. The times are simulated.
32 devices in a mesh: groups: 2 (over x), tensor: 8 (over z, y), expert: 2 (over core).
Axes of the slice: x: 2, y: 2, z: 4, core: 2. Of those that a mesh axis runs over, the one named last changes fastest.
Arguments:
- tokens: bfloat16 [1024, 6144], P(('groups', 'tensor', 'expert')), parts along dimension 0, may hold values from -6 to 6
- expert_ids: int32 [1024, 2], P(('groups', 'tensor', 'expert')), parts along dimension 0, may hold values from 0 to 7, as said below
- gates: float32 [1024, 2], P(('groups', 'tensor', 'expert')), parts along dimension 0, may hold values from 0.1 to 0.9
- w_gate: bfloat16 [2, 6144, 8192], P('expert', None, 'tensor'), may hold values from -0.078125 to 0.078125
- w_up: bfloat16 [2, 6144, 8192], P('expert', None, 'tensor'), may hold values from -0.078125 to 0.078125
- w_down: bfloat16 [2, 8192, 6144], P('expert', 'tensor'), may hold values from -0.0625 to 0.0625
Outputs:
- layer_out: bfloat16 [1024, 6144], P(('groups', 'tensor', 'expert')), parts along dimension 0
There are 2 independent parts, one for each index of `groups`. A program takes and returns all parts, laid end to end along the dimension named above; an argument that names none is the same for every part. Nothing has to cross between parts.
Inputs may be any that keep to these rules, and one draw needn't show every extreme that they name: `expert_ids`: the 2 ids of a token differ. Among the 32 tokens of one device, each of the experts 0 to 1 is picked by at most 8 tokens, and in every draw one of them is picked by exactly 8 tokens on every device.
All inputs are finite; a program needn't handle non-finite values.
Results may differ from a plain program's by a relative error of at most 0.013.
Values may be sent and summed in bfloat16 or wider, within the bound.
No kernel may reach another device: no remote copies, remote signals or barrier semaphores. Data moves between devices by JAX's collectives and lax.ppermute only.
A program may use at most 128 MiB of HBM per device.

v0:
```python
import jax
import jax.numpy as jnp
from jax import lax
from jax.sharding import PartitionSpec as P


def per_device(tokens, expert_ids, gates, w_gate, w_up, w_down):
    expert_count = lax.axis_size("expert")
    tensor_count = lax.axis_size("tensor")
    rows_here = tokens.shape[0]
    model_width = tokens.shape[1]
    capacity = rows_here // 4
    experts = jnp.arange(expert_count, dtype=jnp.int32)
    matches = expert_ids[:, :, None] == experts
    picked = jnp.any(matches, axis=1).astype(jnp.int32)
    weight = jnp.sum(jnp.where(matches, gates[:, :, None], jnp.float32(0.0)), axis=1)
    slot_of = jnp.cumsum(picked, axis=0) - picked
    onehot = (
        (picked[..., None] == 1) & (slot_of[..., None] == jnp.arange(capacity, dtype=jnp.int32))
    ).astype(jnp.bfloat16)
    routed = jnp.einsum("tec,td->ecd", onehot, tokens, preferred_element_type=jnp.float32).astype(
        jnp.bfloat16
    )
    gate_local = w_gate[0]
    up_local = w_up[0]
    down_local = w_down[0]
    unit_share = gate_local.shape[1]
    spread = lax.all_gather(routed[None], "tensor", axis=0, tiled=True)
    portion = lax.all_to_all(spread, "expert", split_axis=1, concat_axis=1, tiled=True)
    flattened = portion.reshape(-1, model_width)
    gate_proj = jnp.dot(flattened, gate_local, preferred_element_type=jnp.float32)
    up_proj = jnp.dot(flattened, up_local, preferred_element_type=jnp.float32)
    hidden_rows = (jax.nn.silu(gate_proj) * up_proj).astype(jnp.bfloat16)
    hidden = hidden_rows.reshape(portion.shape[:-1] + (unit_share,))
    hidden_flat = hidden.reshape(tensor_count, expert_count * capacity, unit_share)
    portion = hidden_flat
    summed = lax.psum_scatter(
        jnp.einsum("rcf,fd->rcd", portion, down_local, preferred_element_type=jnp.float32).astype(
            jnp.bfloat16
        ),
        "tensor",
        scatter_dimension=0,
        tiled=True,
    )
    reduced = summed.reshape(expert_count, capacity, model_width)
    returned = lax.all_to_all(reduced, "expert", split_axis=0, concat_axis=0, tiled=True)
    coefficient = onehot.astype(jnp.float32) * weight[:, :, None]
    layer_out = jnp.einsum(
        "tec,ecd->td", coefficient, returned.astype(jnp.float32), precision=lax.Precision.HIGHEST
    )
    return layer_out.astype(jnp.bfloat16)


def solution(mesh):
    placed = (
        P(("groups", "tensor", "expert"), None),
        P(("groups", "tensor", "expert"), None),
        P(("groups", "tensor", "expert"), None),
        P("expert", None, "tensor"),
        P("expert", None, "tensor"),
        P("expert", "tensor", None),
    )
    return jax.shard_map(
        per_device,
        mesh=mesh,
        in_specs=placed,
        out_specs=P(("groups", "tensor", "expert"), None),
        check_vma=False,
    )
```

profile of v0, /device:TPU:0, one launch (start us, length us, event | category | flops | bytes accessed | tf_op | source)
XLA Modules:
  0.0 155.0 jit_solution(8736896650342397636)
XLA Ops:
  6.5 0.7 fusion.28
  7.3 0.1 copy.22
  7.4 0.1 reduce_window_sum.11
  7.5 0.1 copy.24
  7.5 0.1 copy.23
  7.6 0.9 convolution_convert_fusion
  8.5 0.0 all-gather.3.cloned.1.call-update
  8.5 0.0 reduce-scatter.2.cloned.1.call-start
  8.6 47.9 %all-gather.3.cloned.1.call-done = bf16[16,8,6144]{2,1,0:T(8,128)(2,1)} async-done(((bf16[2,8,6144]{2,1,0:T(8,128)(2,1)}), bf16[16,8,6144]{2,1,0:T(8,128)(2,1)}) %all-gather.3.cloned.1.call-update) | async-done | bytes 1572880 | tf_op jit(solution)/shard_map/all_gather | solution.py:28
  56.5 1.5 copy.25
  58.0 5.0 %all_to_all.10 = bf16[8,2,8,6144]{3,2,0,1:T(8,128)(2,1)S(1)} all-to-all(bf16[8,2,8,6144]{3,2,0,1:T(8,128)(2,1)S(1)} %copy.25), channel_id=1, replica_groups=mesh['groups'=2,'tensor'=8,'expert'=2] {'expert'}, dimensions={1} | all-to-all | bytes 3145728 | tf_op jit(solution)/shard_map/all_to_all | solution.py:29
  63.0 0.1 copy.26
  63.1 0.0 copy-start.3
  63.1 0.0 slice-start
  63.1 6.5 %fusion.4 = f32[128,1024]{1,0:T(8,128)S(1)} fusion(bf16[128,6144]{1,0:T(8,128)(2,1)S(1)} %bitcast.33, bf16[1,6144,1024]{2,1,0:T(8,128)(2,1)} %param.9), kind=kOutput, calls=%fused_computation.4 | convolution fusion | flops 1610612736 | bytes 14680064 | tf_op jit(solution)/shard_map/dot_general | solution.py:31
  69.6 1.6 %copy-done.3 = bf16[1,6144,1024]{2,1,0:T(8,128)(2,1)S(1)} copy-done((bf16[1,6144,1024]{2,1,0:T(8,128)(2,1)S(1)}, bf16[1,6144,1024]{2,1,0:T(8,128)(2,1)}, u32[]{:S(2)}) %copy-start.3) | copy-done | bytes 12582936
  71.2 2.0 %fusion.13 = bf16[128,1024]{1,0:T(8,128)(2,1)S(1)} fusion(bf16[128,6144]{1,0:T(8,128)(2,1)S(1)} %bitcast.34, bf16[1,6144,1024]{2,1,0:T(8,128)(2,1)S(1)} %copy-done.3, f32[128,1024]{1,0:T(8,128)S(1)} %fusion.4), kind=kOutput, calls=%fused_computation.11 | convolution fusion | flops 1611399168 | bytes 14942208 | tf_op jit(solution)/shard_map/dot_general | solution.py:32
  73.3 0.3 slice-done.1
  73.6 1.4 slice-done.2
  75.1 3.0 %fusion.6 = bf16[8,16,6144]{2,1,0:T(8,128)(2,1)} fusion(bf16[8,16,1024]{2,1,0:T(8,128)(2,1)S(1)} %bitcast.36, bf16[1,1024,6144]{2,1,0:T(8,128)(2,1)S(1)} %bitcast.32), kind=kOutput, calls=%fused_computation.6 | convolution fusion | flops 1611399168 | bytes 14417920 | tf_op jit(solution)/shard_map/rcf,fd->rcd/dot_general | solution.py:38
  78.1 0.0 reduce-scatter.2.cloned.1.call-update
  78.1 63.8 %reduce-scatter.2.cloned.1.call-done = bf16[1,16,6144]{2,1,0:T(8,128)(2,1)} async-done(((bf16[8,16,6144]{2,1,0:T(8,128)(2,1)}), bf16[1,16,6144]{2,1,0:T(8,128)(2,1)}) %reduce-scatter.2.cloned.1.call-update) | async-done | bytes 196624 | tf_op jit(solution)/shard_map/reduce_scatter | solution.py:37
  142.0 4.9 %all_to_all.11 = bf16[2,8,6144]{2,1,0:T(8,128)(2,1)S(1)} all-to-all(bf16[2,8,6144]{2,1,0:T(8,128)(2,1)} %bitcast.37), channel_id=1, replica_groups=mesh['groups'=2,'tensor'=8,'expert'=2] {'expert'}, dimensions={0} | all-to-all | bytes 393216 | tf_op jit(solution)/shard_map/all_to_all | solution.py:46
  146.9 1.3 fusion.9
  (14 shorter events, 0.1 us)
Async XLA Ops:
  6.5 1.1 copy-start
  6.5 49.9 %all-gather.3.cloned.1.call-start = ((), (), s32[]{:S(2)}) async-start(), calls=%async_computation.4 | async-start | bytes 1769472 | tf_op jit(solution)/shard_map/all_gather | solution.py:28
  8.5 133.4 %reduce-scatter.2.cloned.1.call-start = ((), (), s32[]{:S(2)}) async-start(), calls=%async_computation.3 | async-start | bytes 1769472 | tf_op jit(solution)/shard_map/reduce_scatter | solution.py:37
  63.1 8.2 %copy-start.3 = (bf16[1,6144,1024]{2,1,0:T(8,128)(2,1)S(1)}, bf16[1,6144,1024]{2,1,0:T(8,128)(2,1)}, u32[]{:S(2)}) copy-start(bf16[1,6144,1024]{2,1,0:T(8,128)(2,1)} %param.10) | copy-start | bytes 37748740
  63.1 10.2 %slice-start = ((s8[12582912]{0:T(1024)(128)(4,1)}), s8[4194304]{0:T(1024)(128)(4,1)S(1)}, s32[]{:S(2)}) async-start(s8[12582912]{0:T(1024)(128)(4,1)} %bitcast.31), calls=%async_computation.5 | async-start | bytes 8388608
  63.1 10.5 %slice-start.1 = ((s8[12582912]{0:T(1024)(128)(4,1)}), s8[4194304]{0:T(1024)(128)(4,1)S(1)}, s32[]{:S(2)}) async-start(s8[12582912]{0:T(1024)(128)(4,1)} %bitcast.31), calls=%async_computation.6 | async-start | bytes 8388608
  71.2 3.8 %slice-start.2 = ((s8[12582912]{0:T(1024)(128)(4,1)}), s8[4194304]{0:T(1024)(128)(4,1)S(1)}, s32[]{:S(2)}) async-start(s8[12582912]{0:T(1024)(128)(4,1)} %bitcast.31), calls=%async_computation.7 | async-start | bytes 8388608
  75.1 3.0 %copy-start.1 = (s32[32,2]{0,1:T(2,128)S(1)}, s32[32,2]{0,1:T(2,128)}, u32[]{:S(2)}) copy-start(s32[32,2]{0,1:T(2,128)} %param.7) | copy-start | bytes 772
  75.1 3.0 %copy-start.2 = (f32[32,2]{0,1:T(2,128)S(1)}, f32[32,2]{0,1:T(2,128)}, u32[]{:S(2)}) copy-start(f32[32,2]{0,1:T(2,128)} %param.8) | copy-start | bytes 772
Sparse Core Ops, SparseCore 0:
  9.5 46.8 all-gather.2
  78.2 63.6 reduce-scatter.1
where the time goes:
time: 155 us
  waiting for transfers between devices  112 us (72%)
  matrix products  13.7 us (9%)
  between operations  13.5 us (9%)
  blocking collectives  9.92 us (6%)
  local copies, waits for them, and re-layouts  5.29 us (3%)
    reduce_scatter x1, waiting for transfers between devices, per_device(): lax.psum_scatter(jnp.einsum('rcf,fd->rcd', portion, down_local, preferred...  63.8 us
    all_gather x1, waiting for transfers between devices, per_device(): spread = lax.all_gather(routed[None], 'tensor', axis=0, tiled=True)  47.9 us
    dot_general x1, matrix products, per_device(): jnp.dot(flattened, gate_local, preferred_element_type=jnp.float32)  6.52 us
    all_to_all x1, blocking collectives, per_device(): lax.all_to_all(spread, 'expert', split_axis=1, concat_axis=1, tiled=True)  5 us
    all_to_all x1, blocking collectives, per_device(): lax.all_to_all(reduced, 'expert', split_axis=0, concat_axis=0, tiled=True)  4.92 us
    unnamed x14, local copies, waits for them, and re-layouts  3.4 us
  transfers between devices with their start and end apart: 2, of which 2 were waited for; matrix products, arithmetic and copies ran while one was open for 0% of the time, Pallas kernels for 0%

commit v1 on v0

v1 whole, which is shorter than its diff:
```python
import jax
import jax.numpy as jnp
import numpy as np
from jax import lax
from jax.sharding import PartitionSpec as P


def ring_order(mesh):
    count = mesh.shape["tensor"]
    names = list(mesh.axis_names)
    line = np.moveaxis(mesh.devices, names.index("tensor"), 0).reshape(count, -1)[:, 0]
    natural = list(range(count))
    places = [tuple(getattr(device, "coords", ()) or ()) for device in line]
    if not all(len(place) == 3 for place in places):
        return natural
    varying = [d for d in range(3) if len({place[d] for place in places}) > 1]
    if len(varying) != 2:
        return natural
    inner = [d for d in varying if len({place[d] for place in places}) == 2]
    if not inner:
        return natural
    side = inner[-1]
    along = varying[0] if varying[1] == side else varying[1]
    low = min(place[side] for place in places)
    up = sorted((i for i in natural if places[i][side] == low), key=lambda i: places[i][along])
    down = sorted((i for i in natural if places[i][side] != low), key=lambda i: -places[i][along])
    return up + down


def make_per_device(ring):
    count = len(ring)
    forward = [(ring[i], ring[(i + 1) % count]) for i in range(count)]
    backward = [(b, a) for a, b in forward]
    swap = [(0, 1), (1, 0)]
    longer, shorter = count // 2, (count - 1) // 2

    def gather(block, forward_steps, backward_steps):
        held = {0: block}
        ahead = behind = block
        for step in range(1, max(forward_steps, backward_steps) + 1):
            if step <= forward_steps:
                behind = lax.ppermute(behind, "tensor", forward)
                held[-step] = behind
            if step <= backward_steps:
                ahead = lax.ppermute(ahead, "tensor", backward)
                held[step] = ahead
        return held

    def scatter_sum(terms, forward_steps, backward_steps):
        def flow(steps, sign, perm):
            running = None
            for step in range(steps, 0, -1):
                distance = sign * step
                term = terms[distance] if distance in terms else terms[distance - sign * count]
                total = term if running is None else term + running.astype(jnp.float32)
                running = lax.ppermute(total.astype(jnp.bfloat16), "tensor", perm)
            return running

        total = terms[0]
        for part in (flow(forward_steps, 1, forward), flow(backward_steps, -1, backward)):
            if part is not None:
                total = total + part.astype(jnp.float32)
        return total

    def per_device(tokens, expert_ids, gates, w_gate, w_up, w_down):
        expert_count = lax.axis_size("expert")
        rows_here = tokens.shape[0]
        capacity = rows_here // 4
        own = lax.axis_index("expert")
        experts = (own + jnp.arange(expert_count, dtype=jnp.int32)) % expert_count
        matches = expert_ids[:, :, None] == experts
        picked = jnp.any(matches, axis=1).astype(jnp.int32)
        weight = jnp.sum(jnp.where(matches, gates[:, :, None], jnp.float32(0.0)), axis=1)
        slot_of = jnp.cumsum(picked, axis=0) - picked
        onehot = (
            (picked[..., None] == 1) & (slot_of[..., None] == jnp.arange(capacity, dtype=jnp.int32))
        ).astype(jnp.bfloat16)
        routed = jnp.einsum("tec,td->ecd", onehot, tokens, preferred_element_type=jnp.float32).astype(
            jnp.bfloat16
        )
        sibling = lax.ppermute(routed[1], "expert", swap)
        held_a = gather(routed[0], longer, shorter)
        held_b = gather(sibling, shorter, longer)
        keys = [("a", k) for k in held_a] + [("b", k) for k in held_b]
        rows = jnp.concatenate(list(held_a.values()) + list(held_b.values()), axis=0)
        gate_proj = jnp.dot(rows, w_gate[0], preferred_element_type=jnp.float32)
        up_proj = jnp.dot(rows, w_up[0], preferred_element_type=jnp.float32)
        hidden = (jax.nn.silu(gate_proj) * up_proj).astype(jnp.bfloat16)
        parts = jnp.dot(hidden, w_down[0], preferred_element_type=jnp.float32)
        terms = {"a": {}, "b": {}}
        for i, (chain, distance) in enumerate(keys):
            terms[chain][distance] = parts[i * capacity : (i + 1) * capacity]
        sum_b = scatter_sum(terms["b"], shorter, longer)
        other = lax.ppermute(sum_b.astype(jnp.bfloat16), "expert", swap)
        sum_a = scatter_sum(terms["a"], longer, shorter).astype(jnp.bfloat16)
        returned = jnp.stack([sum_a, other]).astype(jnp.float32)
        coefficient = onehot.astype(jnp.float32) * weight[:, :, None]
        layer_out = jnp.einsum(
            "tec,ecd->td", coefficient, returned, precision=lax.Precision.HIGHEST
        )
        return layer_out.astype(jnp.bfloat16)

    return per_device


def solution(mesh):
    placed = (
        P(("groups", "tensor", "expert"), None),
        P(("groups", "tensor", "expert"), None),
        P(("groups", "tensor", "expert"), None),
        P("expert", None, "tensor"),
        P("expert", None, "tensor"),
        P("expert", "tensor", None),
    )
    return jax.shard_map(
        make_per_device(ring_order(mesh)),
        mesh=mesh,
        in_specs=placed,
        out_specs=P(("groups", "tensor", "expert"), None),
        check_vma=False,
    )
```

time: 155 us -> 104 us (0.67)
  waiting for transfers between devices: 112 us -> 40.5 us
  starting transfers between devices: 0.04 us -> 30.7 us
  between operations: 13.5 us -> 0.21 us
  blocking collectives: 9.92 us -> 0 us
  matrix products: 13.7 us -> 22.2 us
  other arithmetic: 0.83 us -> 9.07 us
  local copies, waits for them, and re-layouts: 5.29 us -> 0.46 us
    reduce_scatter x1 -> x0, waiting for transfers between devices: 63.8 us -> none  [per_device(): lax.psum_scatter(jnp.einsum('rcf,fd->rcd', portion, down_local, preferred...]
    all_gather x1 -> x0, waiting for transfers between devices: 47.9 us -> none  [per_device(): spread = lax.all_gather(routed[None], 'tensor', axis=0, tiled=True)]
    ppermute x0 -> x30, waiting for transfers between devices: none -> 40.5 us  [the longest x14 23.7 us: flow(): running = lax.ppermute(total.astype(jnp.bfloat16), 'tensor', perm)]
    ppermute x0 -> x30, starting transfers between devices: none -> 30.7 us  [the longest x14 15.3 us: flow(): running = lax.ppermute(total.astype(jnp.bfloat16), 'tensor', perm)]
    all_to_all x2 -> x0, blocking collectives: 9.92 us -> none  [the longest x1 5 us: per_device(): lax.all_to_all(spread, 'expert', split_axis=1, concat_axis=1, tiled=True)]
    dot_general x4 -> x3, matrix products: 12.8 us -> 22 us  [the longest x1 13.6 us: per_device(): parts = jnp.dot(hidden, w_down[0], preferred_element_type=jnp.float32)]
    convert_element_type x0 -> x7, other arithmetic: none -> 6.9 us  [the longest x6 5.94 us: flow(): running = lax.ppermute(total.astype(jnp.bfloat16), 'tensor', perm)]
    unnamed x14 -> x21, local copies, waits for them, and re-layouts: 3.4 us -> 0.14 us
  transfers between devices with their start and end apart: 2 -> 30, of which waited for: 2 -> 19; matrix products, arithmetic and copies ran while one was open for 0% -> 3% of each run, Pallas kernels for 0% -> 0%
where the time goes in v1:
time: 104 us; the launch traced here: 103 us
  waiting for transfers between devices  40.5 us (39%)
  starting transfers between devices  30.7 us (30%)
  matrix products  22.2 us (21%)
  other arithmetic  9.07 us (9%)
    ppermute x14, waiting for transfers between devices, flow(): running = lax.ppermute(total.astype(jnp.bfloat16), 'tensor', perm)  23.7 us
    ppermute x14, starting transfers between devices, flow(): running = lax.ppermute(total.astype(jnp.bfloat16), 'tensor', perm)  15.3 us
    ppermute x7, starting transfers between devices, gather(): behind = lax.ppermute(behind, 'tensor', forward)  14.5 us
    dot_general x1, matrix products, per_device(): parts = jnp.dot(hidden, w_down[0], preferred_element_type=jnp.float32)  13.6 us
    ppermute x7, waiting for transfers between devices, gather(): ahead = lax.ppermute(ahead, 'tensor', backward)  9.04 us
    dot_general x1, matrix products, per_device(): up_proj = jnp.dot(rows, w_up[0], preferred_element_type=jnp.float32)  7.18 us
    convert_element_type x6, other arithmetic, flow(): running = lax.ppermute(total.astype(jnp.bfloat16), 'tensor', perm)  5.94 us
    ppermute x7, waiting for transfers between devices, gather(): behind = lax.ppermute(behind, 'tensor', forward)  5.28 us
  transfers between devices with their start and end apart: 30, of which 19 were waited for; matrix products, arithmetic and copies ran while one was open for 3% of the time, Pallas kernels for 0%

profile of v1, /device:TPU:0, one launch (start us, length us, event | category | flops | bytes accessed | tf_op | source)
XLA Modules:
  0.0 103.2 jit_solution(9961274508508714484)
XLA Ops:
  1.4 3.1 %collective-permute-start = (bf16[8,6144]{1,0:T(8,128)(2,1)S(1)}, bf16[8,6144]{1,0:T(8,128)(2,1)S(1)}, u32[]{:S(2)}, u32[]{:S(2)}) collective-permute-start(bf16[8,6144]{1,0:T(8,128)(2,1)S(1)} %get-tuple-element.17), channel_id=1, source_target_pairs={{0,4},{4,8},{8,12},{12,14},{14,10},{10,6},{6,2},{2,0},{1,5},{5,9},... | collective-permute-start | bytes 294920 | tf_op jit(solution)/shard_map/ppermute | solution.py:42
  5.8 2.0 %collective-permute-start.8 = (bf16[8,6144]{1,0:T(8,128)(2,1)S(1)}, bf16[8,6144]{1,0:T(8,128)(2,1)S(1)}, u32[]{:S(2)}, u32[]{:S(2)}) collective-permute-start(bf16[8,6144]{1,0:T(8,128)(2,1)S(1)} %collective-permute-done.7), channel_id=1, source_target_pairs={{0,4},{4,8},{8,12},{12,14},{14,10},{10,6},{6,2},{2,0},{1,5},{5,9},... | collective-permute-start | bytes 294920 | tf_op jit(solution)/shard_map/ppermute | solution.py:42
  7.8 2.0 %collective-permute-start.2 = (bf16[8,6144]{1,0:T(8,128)(2,1)S(1)}, bf16[8,6144]{1,0:T(8,128)(2,1)S(1)}, u32[]{:S(2)}, u32[]{:S(2)}) collective-permute-start(bf16[8,6144]{1,0:T(8,128)(2,1)S(1)} %collective-permute-done), channel_id=1, source_target_pairs={{0,4},{4,8},{8,12},{12,14},{14,10},{10,6},{6,2},{2,0},{1,5},{5,9},... | collective-permute-start | bytes 294920 | tf_op jit(solution)/shard_map/ppermute | solution.py:42
  9.9 3.0 %collective-permute-done.2 = bf16[8,6144]{1,0:T(8,128)(2,1)S(1)} collective-permute-done((bf16[8,6144]{1,0:T(8,128)(2,1)S(1)}, bf16[8,6144]{1,0:T(8,128)(2,1)S(1)}, u32[]{:S(2)}, u32[]{:S(2)}) %collective-permute-start.2) | collective-permute-done | bytes 98336 | tf_op jit(solution)/shard_map/ppermute | solution.py:42
  13.0 1.8 %collective-permute-start.4 = (bf16[8,6144]{1,0:T(8,128)(2,1)S(1)}, bf16[8,6144]{1,0:T(8,128)(2,1)S(1)}, u32[]{:S(2)}, u32[]{:S(2)}) collective-permute-start(bf16[8,6144]{1,0:T(8,128)(2,1)S(1)} %collective-permute-done.2), channel_id=1, source_target_pairs={{0,4},{4,8},{8,12},{12,14},{14,10},{10,6},{6,2},{2,0},{1,5},{5,9},... | collective-permute-start | bytes 294920 | tf_op jit(solution)/shard_map/ppermute | solution.py:42
  15.1 1.9 %collective-permute-start.10 = (bf16[8,6144]{1,0:T(8,128)(2,1)S(1)}, bf16[8,6144]{1,0:T(8,128)(2,1)S(1)}, u32[]{:S(2)}, u32[]{:S(2)}) collective-permute-start(bf16[8,6144]{1,0:T(8,128)(2,1)S(1)} %collective-permute-done.8), channel_id=1, source_target_pairs={{0,4},{4,8},{8,12},{12,14},{14,10},{10,6},{6,2},{2,0},{1,5},{5,9},... | collective-permute-start | bytes 294920 | tf_op jit(solution)/shard_map/ppermute | solution.py:42
  18.4 2.0 %collective-permute-start.6 = (bf16[8,6144]{1,0:T(8,128)(2,1)S(1)}, bf16[8,6144]{1,0:T(8,128)(2,1)S(1)}, u32[]{:S(2)}, u32[]{:S(2)}) collective-permute-start(bf16[8,6144]{1,0:T(8,128)(2,1)S(1)} %collective-permute-done.4), channel_id=1, source_target_pairs={{0,4},{4,8},{8,12},{12,14},{14,10},{10,6},{6,2},{2,0},{1,5},{5,9},... | collective-permute-start | bytes 294920 | tf_op jit(solution)/shard_map/ppermute | solution.py:42
  20.7 1.7 %collective-permute-start.12 = (bf16[8,6144]{1,0:T(8,128)(2,1)S(1)}, bf16[8,6144]{1,0:T(8,128)(2,1)S(1)}, u32[]{:S(2)}, u32[]{:S(2)}) collective-permute-start(bf16[8,6144]{1,0:T(8,128)(2,1)S(1)} %collective-permute-done.10), channel_id=1, source_target_pairs={{0,4},{4,8},{8,12},{12,14},{14,10},{10,6},{6,2},{2,0},{1,5},{5,9},... | collective-permute-start | bytes 294920 | tf_op jit(solution)/shard_map/ppermute | solution.py:42
  23.6 4.4 %collective-permute-done.13 = bf16[8,6144]{1,0:T(8,128)(2,1)S(1)} collective-permute-done((bf16[8,6144]{1,0:T(8,128)(2,1)S(1)}, bf16[8,6144]{1,0:T(8,128)(2,1)S(1)}, u32[]{:S(2)}, u32[]{:S(2)}) %collective-permute-start.13) | collective-permute-done | bytes 98336 | tf_op jit(solution)/shard_map/ppermute | solution.py:45
  28.0 4.6 %collective-permute-done.14 = bf16[8,6144]{1,0:T(8,128)(2,1)S(1)} collective-permute-done((bf16[8,6144]{1,0:T(8,128)(2,1)S(1)}, bf16[8,6144]{1,0:T(8,128)(2,1)S(1)}, u32[]{:S(2)}, u32[]{:S(2)}) %collective-permute-start.14) | collective-permute-done | bytes 98336 | tf_op jit(solution)/shard_map/ppermute | solution.py:45
  32.6 7.2 %fusion.2 = f32[128,1024]{1,0:T(8,128)} fusion(bf16[128,6144]{1,0:T(8,128)(2,1)S(1)} %constant_dynamic-update-slice_fusion, bf16[1,6144,1024]{2,1,0:T(8,128)(2,1)} %param.10), kind=kOutput, calls=%fused_computation.2 | convolution fusion | flops 1610612736 | bytes 14680064 | tf_op jit(solution)/shard_map/dot_general | solution.py:87
  39.8 13.6 %fusion.47 = (bf16[128,6144]{1,0:T(8,128)(2,1)S(1)}, f32[128,6144]{1,0:T(8,128)}) fusion(bf16[1,1024,6144]{2,1,0:T(8,128)(2,1)} %param.11, f32[128,1024]{1,0:T(8,128)} %fusion.2, bf16[128,6144]{1,0:T(8,128)(2,1)S(1)} %constant_dynamic-update-slice_fusion, bf16[1,6144,1024]{2,1,0:T(8,128)(2,1)} %param.9), kind=kOutput, calls=%fused_computation.82 | convolution fusion | flops 3222798336 | bytes 31981568 | tf_op jit(solution)/shard_map/dot_general | solution.py:89
  53.4 1.6 %collective-permute-start.15 = (bf16[8,6144]{1,0:T(8,128)(2,1)S(1)}, bf16[8,6144]{1,0:T(8,128)(2,1)S(1)}, u32[]{:S(2)}, u32[]{:S(2)}) collective-permute-start(bf16[8,6144]{1,0:T(8,128)(2,1)S(1)} %get-tuple-element.12), channel_id=1, source_target_pairs={{0,4},{4,8},{8,12},{12,14},{14,10},{10,6},{6,2},{2,0},{1,5},{5,9},... | collective-permute-start | bytes 294920 | tf_op jit(solution)/shard_map/ppermute | solution.py:56
  55.0 3.1 %collective-permute-done.15 = bf16[8,6144]{1,0:T(8,128)(2,1)S(1)} collective-permute-done((bf16[8,6144]{1,0:T(8,128)(2,1)S(1)}, bf16[8,6144]{1,0:T(8,128)(2,1)S(1)}, u32[]{:S(2)}, u32[]{:S(2)}) %collective-permute-start.15) | collective-permute-done | bytes 98336 | tf_op jit(solution)/shard_map/ppermute | solution.py:56
  59.1 1.6 %collective-permute-start.16 = (bf16[8,6144]{1,0:T(8,128)(2,1)S(1)}, bf16[8,6144]{1,0:T(8,128)(2,1)S(1)}, u32[]{:S(2)}, u32[]{:S(2)}) collective-permute-start(bf16[8,6144]{1,0:T(8,128)(2,1)S(1)} %fusion.22), channel_id=1, source_target_pairs={{0,4},{4,8},{8,12},{12,14},{14,10},{10,6},{6,2},{2,0},{1,5},{5,9},... | collective-permute-start | bytes 294920 | tf_op jit(solution)/shard_map/ppermute | solution.py:56
  61.2 2.6 %collective-permute-done.16 = bf16[8,6144]{1,0:T(8,128)(2,1)S(1)} collective-permute-done((bf16[8,6144]{1,0:T(8,128)(2,1)S(1)}, bf16[8,6144]{1,0:T(8,128)(2,1)S(1)}, u32[]{:S(2)}, u32[]{:S(2)}) %collective-permute-start.16) | collective-permute-done | bytes 98336 | tf_op jit(solution)/shard_map/ppermute | solution.py:56
  64.7 1.6 %collective-permute-start.17 = (bf16[8,6144]{1,0:T(8,128)(2,1)S(1)}, bf16[8,6144]{1,0:T(8,128)(2,1)S(1)}, u32[]{:S(2)}, u32[]{:S(2)}) collective-permute-start(bf16[8,6144]{1,0:T(8,128)(2,1)S(1)} %fusion.23), channel_id=1, source_target_pairs={{0,4},{4,8},{8,12},{12,14},{14,10},{10,6},{6,2},{2,0},{1,5},{5,9},... | collective-permute-start | bytes 294920 | tf_op jit(solution)/shard_map/ppermute | solution.py:56
  66.3 3.1 %collective-permute-done.17 = bf16[8,6144]{1,0:T(8,128)(2,1)S(1)} collective-permute-done((bf16[8,6144]{1,0:T(8,128)(2,1)S(1)}, bf16[8,6144]{1,0:T(8,128)(2,1)S(1)}, u32[]{:S(2)}, u32[]{:S(2)}) %collective-permute-start.17) | collective-permute-done | bytes 98336 | tf_op jit(solution)/shard_map/ppermute | solution.py:56
  78.3 2.5 %collective-permute-done.21 = bf16[8,6144]{1,0:T(8,128)(2,1)S(1)} collective-permute-done((bf16[8,6144]{1,0:T(8,128)(2,1)S(1)}, bf16[8,6144]{1,0:T(8,128)(2,1)S(1)}, u32[]{:S(2)}, u32[]{:S(2)}) %collective-permute-start.21) | collective-permute-done | bytes 98336 | tf_op jit(solution)/shard_map/ppermute | solution.py:56
  84.0 2.6 %collective-permute-done.23 = bf16[8,6144]{1,0:T(8,128)(2,1)S(1)} collective-permute-done((bf16[8,6144]{1,0:T(8,128)(2,1)S(1)}, bf16[8,6144]{1,0:T(8,128)(2,1)S(1)}, u32[]{:S(2)}, u32[]{:S(2)}) %collective-permute-start.23) | collective-permute-done | bytes 98336 | tf_op jit(solution)/shard_map/ppermute | solution.py:56
  86.6 1.6 %collective-permute-done.26 = bf16[8,6144]{1,0:T(8,128)(2,1)S(1)} collective-permute-done((bf16[8,6144]{1,0:T(8,128)(2,1)S(1)}, bf16[8,6144]{1,0:T(8,128)(2,1)S(1)}, u32[]{:S(2)}, u32[]{:S(2)}) %collective-permute-start.26) | collective-permute-done | bytes 98336 | tf_op jit(solution)/shard_map/ppermute | solution.py:56
  89.8 1.6 %collective-permute-start.24 = (bf16[8,6144]{1,0:T(8,128)(2,1)S(1)}, bf16[8,6144]{1,0:T(8,128)(2,1)S(1)}, u32[]{:S(2)}, u32[]{:S(2)}) collective-permute-start(bf16[8,6144]{1,0:T(8,128)(2,1)S(1)} %get-tuple-element.10), channel_id=1, source_target_pairs={{0,4},{4,8},{8,12},{12,14},{14,10},{10,6},{6,2},{2,0},{1,5},{5,9},... | collective-permute-start | bytes 294920 | tf_op jit(solution)/shard_map/ppermute | solution.py:56
  91.4 2.6 %collective-permute-done.27 = bf16[8,6144]{1,0:T(8,128)(2,1)S(1)} collective-permute-done((bf16[8,6144]{1,0:T(8,128)(2,1)S(1)}, bf16[8,6144]{1,0:T(8,128)(2,1)S(1)}, u32[]{:S(2)}, u32[]{:S(2)}) %collective-permute-start.27) | collective-permute-done | bytes 98336 | tf_op jit(solution)/shard_map/ppermute | solution.py:56
  95.4 4.2 %collective-permute-done.28 = bf16[8,6144]{1,0:T(8,128)(2,1)S(1)} collective-permute-done((bf16[8,6144]{1,0:T(8,128)(2,1)S(1)}, bf16[8,6144]{1,0:T(8,128)(2,1)S(1)}, u32[]{:S(2)}, u32[]{:S(2)}) %collective-permute-start.28) | collective-permute-done | bytes 98336 | tf_op jit(solution)/shard_map/ppermute | solution.py:56
  (81 shorter events, 27.0 us)
Async XLA Ops:
  1.4 6.4 %collective-permute-start = (bf16[8,6144]{1,0:T(8,128)(2,1)S(1)}, bf16[8,6144]{1,0:T(8,128)(2,1)S(1)}, u32[]{:S(2)}, u32[]{:S(2)}) collective-permute-start(bf16[8,6144]{1,0:T(8,128)(2,1)S(1)} %get-tuple-element.17), channel_id=1, source_target_pairs={{0,4},{4,8},{8,12},{12,14},{14,10},{10,6},{6,2},{2,0},{1,5},{5,9},... | collective-permute-start | bytes 294920 | tf_op jit(solution)/shard_map/ppermute | solution.py:42
  4.5 5.4 %collective-permute-start.1 = (bf16[8,6144]{1,0:T(8,128)(2,1)S(1)}, bf16[8,6144]{1,0:T(8,128)(2,1)S(1)}, u32[]{:S(2)}, u32[]{:S(2)}) collective-permute-start(bf16[8,6144]{1,0:T(8,128)(2,1)S(1)} %get-tuple-element.17), channel_id=1, source_target_pairs={{4,0},{8,4},{12,8},{14,12},{10,14},{6,10},{2,6},{0,2},{5,1},{9,5},... | collective-permute-start | bytes 294920 | tf_op jit(solution)/shard_map/ppermute | solution.py:45
  5.8 9.3 %collective-permute-start.8 = (bf16[8,6144]{1,0:T(8,128)(2,1)S(1)}, bf16[8,6144]{1,0:T(8,128)(2,1)S(1)}, u32[]{:S(2)}, u32[]{:S(2)}) collective-permute-start(bf16[8,6144]{1,0:T(8,128)(2,1)S(1)} %collective-permute-done.7), channel_id=1, source_target_pairs={{0,4},{4,8},{8,12},{12,14},{14,10},{10,6},{6,2},{2,0},{1,5},{5,9},... | collective-permute-start | bytes 294920 | tf_op jit(solution)/shard_map/ppermute | solution.py:42
  7.8 9.1 %collective-permute-start.9 = (bf16[8,6144]{1,0:T(8,128)(2,1)S(1)}, bf16[8,6144]{1,0:T(8,128)(2,1)S(1)}, u32[]{:S(2)}, u32[]{:S(2)}) collective-permute-start(bf16[8,6144]{1,0:T(8,128)(2,1)S(1)} %collective-permute-done.7), channel_id=1, source_target_pairs={{4,0},{8,4},{12,8},{14,12},{10,14},{6,10},{2,6},{0,2},{5,1},{9,5},... | collective-permute-start | bytes 294920 | tf_op jit(solution)/shard_map/ppermute | solution.py:45
  7.8 5.1 %collective-permute-start.2 = (bf16[8,6144]{1,0:T(8,128)(2,1)S(1)}, bf16[8,6144]{1,0:T(8,128)(2,1)S(1)}, u32[]{:S(2)}, u32[]{:S(2)}) collective-permute-start(bf16[8,6144]{1,0:T(8,128)(2,1)S(1)} %collective-permute-done), channel_id=1, source_target_pairs={{0,4},{4,8},{8,12},{12,14},{14,10},{10,6},{6,2},{2,0},{1,5},{5,9},... | collective-permute-start | bytes 294920 | tf_op jit(solution)/shard_map/ppermute | solution.py:42
  9.9 4.9 %collective-permute-start.3 = (bf16[8,6144]{1,0:T(8,128)(2,1)S(1)}, bf16[8,6144]{1,0:T(8,128)(2,1)S(1)}, u32[]{:S(2)}, u32[]{:S(2)}) collective-permute-start(bf16[8,6144]{1,0:T(8,128)(2,1)S(1)} %collective-permute-done.1), channel_id=1, source_target_pairs={{4,0},{8,4},{12,8},{14,12},{10,14},{6,10},{2,6},{0,2},{5,1},{9,5},... | collective-permute-start | bytes 294920 | tf_op jit(solution)/shard_map/ppermute | solution.py:45
  13.0 5.5 %collective-permute-start.4 = (bf16[8,6144]{1,0:T(8,128)(2,1)S(1)}, bf16[8,6144]{1,0:T(8,128)(2,1)S(1)}, u32[]{:S(2)}, u32[]{:S(2)}) collective-permute-start(bf16[8,6144]{1,0:T(8,128)(2,1)S(1)} %collective-permute-done.2), channel_id=1, source_target_pairs={{0,4},{4,8},{8,12},{12,14},{14,10},{10,6},{6,2},{2,0},{1,5},{5,9},... | collective-permute-start | bytes 294920 | tf_op jit(solution)/shard_map/ppermute | solution.py:42
  14.8 8.0 %collective-permute-start.5 = (bf16[8,6144]{1,0:T(8,128)(2,1)S(1)}, bf16[8,6144]{1,0:T(8,128)(2,1)S(1)}, u32[]{:S(2)}, u32[]{:S(2)}) collective-permute-start(bf16[8,6144]{1,0:T(8,128)(2,1)S(1)} %collective-permute-done.3), channel_id=1, source_target_pairs={{4,0},{8,4},{12,8},{14,12},{10,14},{6,10},{2,6},{0,2},{5,1},{9,5},... | collective-permute-start | bytes 294920 | tf_op jit(solution)/shard_map/ppermute | solution.py:45
  15.1 5.7 %collective-permute-start.10 = (bf16[8,6144]{1,0:T(8,128)(2,1)S(1)}, bf16[8,6144]{1,0:T(8,128)(2,1)S(1)}, u32[]{:S(2)}, u32[]{:S(2)}) collective-permute-start(bf16[8,6144]{1,0:T(8,128)(2,1)S(1)} %collective-permute-done.8), channel_id=1, source_target_pairs={{0,4},{4,8},{8,12},{12,14},{14,10},{10,6},{6,2},{2,0},{1,5},{5,9},... | collective-permute-start | bytes 294920 | tf_op jit(solution)/shard_map/ppermute | solution.py:42
  16.9 5.6 %collective-permute-start.11 = (bf16[8,6144]{1,0:T(8,128)(2,1)S(1)}, bf16[8,6144]{1,0:T(8,128)(2,1)S(1)}, u32[]{:S(2)}, u32[]{:S(2)}) collective-permute-start(bf16[8,6144]{1,0:T(8,128)(2,1)S(1)} %collective-permute-done.9), channel_id=1, source_target_pairs={{4,0},{8,4},{12,8},{14,12},{10,14},{6,10},{2,6},{0,2},{5,1},{9,5},... | collective-permute-start | bytes 294920 | tf_op jit(solution)/shard_map/ppermute | solution.py:45
  18.4 5.0 %collective-permute-start.6 = (bf16[8,6144]{1,0:T(8,128)(2,1)S(1)}, bf16[8,6144]{1,0:T(8,128)(2,1)S(1)}, u32[]{:S(2)}, u32[]{:S(2)}) collective-permute-start(bf16[8,6144]{1,0:T(8,128)(2,1)S(1)} %collective-permute-done.4), channel_id=1, source_target_pairs={{0,4},{4,8},{8,12},{12,14},{14,10},{10,6},{6,2},{2,0},{1,5},{5,9},... | collective-permute-start | bytes 294920 | tf_op jit(solution)/shard_map/ppermute | solution.py:42
  20.7 7.3 %collective-permute-start.12 = (bf16[8,6144]{1,0:T(8,128)(2,1)S(1)}, bf16[8,6144]{1,0:T(8,128)(2,1)S(1)}, u32[]{:S(2)}, u32[]{:S(2)}) collective-permute-start(bf16[8,6144]{1,0:T(8,128)(2,1)S(1)} %collective-permute-done.10), channel_id=1, source_target_pairs={{0,4},{4,8},{8,12},{12,14},{14,10},{10,6},{6,2},{2,0},{1,5},{5,9},... | collective-permute-start | bytes 294920 | tf_op jit(solution)/shard_map/ppermute | solution.py:42
  22.5 5.5 %collective-permute-start.13 = (bf16[8,6144]{1,0:T(8,128)(2,1)S(1)}, bf16[8,6144]{1,0:T(8,128)(2,1)S(1)}, u32[]{:S(2)}, u32[]{:S(2)}) collective-permute-start(bf16[8,6144]{1,0:T(8,128)(2,1)S(1)} %collective-permute-done.11), channel_id=1, source_target_pairs={{4,0},{8,4},{12,8},{14,12},{10,14},{6,10},{2,6},{0,2},{5,1},{9,5},... | collective-permute-start | bytes 294920 | tf_op jit(solution)/shard_map/ppermute | solution.py:45
  53.4 4.7 %collective-permute-start.15 = (bf16[8,6144]{1,0:T(8,128)(2,1)S(1)}, bf16[8,6144]{1,0:T(8,128)(2,1)S(1)}, u32[]{:S(2)}, u32[]{:S(2)}) collective-permute-start(bf16[8,6144]{1,0:T(8,128)(2,1)S(1)} %get-tuple-element.12), channel_id=1, source_target_pairs={{0,4},{4,8},{8,12},{12,14},{14,10},{10,6},{6,2},{2,0},{1,5},{5,9},... | collective-permute-start | bytes 294920 | tf_op jit(solution)/shard_map/ppermute | solution.py:56
  59.1 4.7 %collective-permute-start.16 = (bf16[8,6144]{1,0:T(8,128)(2,1)S(1)}, bf16[8,6144]{1,0:T(8,128)(2,1)S(1)}, u32[]{:S(2)}, u32[]{:S(2)}) collective-permute-start(bf16[8,6144]{1,0:T(8,128)(2,1)S(1)} %fusion.22), channel_id=1, source_target_pairs={{0,4},{4,8},{8,12},{12,14},{14,10},{10,6},{6,2},{2,0},{1,5},{5,9},... | collective-permute-start | bytes 294920 | tf_op jit(solution)/shard_map/ppermute | solution.py:56
  60.7 5.6 %collective-permute-start.19 = (bf16[8,6144]{1,0:T(8,128)(2,1)S(1)}, bf16[8,6144]{1,0:T(8,128)(2,1)S(1)}, u32[]{:S(2)}, u32[]{:S(2)}) collective-permute-start(bf16[8,6144]{1,0:T(8,128)(2,1)S(1)} %get-tuple-element.15), channel_id=1, source_target_pairs={{4,0},{8,4},{12,8},{14,12},{10,14},{6,10},{2,6},{0,2},{5,1},{9,5},... | collective-permute-start | bytes 294920 | tf_op jit(solution)/shard_map/ppermute | solution.py:56
  64.7 4.7 %collective-permute-start.17 = (bf16[8,6144]{1,0:T(8,128)(2,1)S(1)}, bf16[8,6144]{1,0:T(8,128)(2,1)S(1)}, u32[]{:S(2)}, u32[]{:S(2)}) collective-permute-start(bf16[8,6144]{1,0:T(8,128)(2,1)S(1)} %fusion.23), channel_id=1, source_target_pairs={{0,4},{4,8},{8,12},{12,14},{14,10},{10,6},{6,2},{2,0},{1,5},{5,9},... | collective-permute-start | bytes 294920 | tf_op jit(solution)/shard_map/ppermute | solution.py:56
  70.4 4.7 %collective-permute-start.20 = (bf16[8,6144]{1,0:T(8,128)(2,1)S(1)}, bf16[8,6144]{1,0:T(8,128)(2,1)S(1)}, u32[]{:S(2)}, u32[]{:S(2)}) collective-permute-start(bf16[8,6144]{1,0:T(8,128)(2,1)S(1)} %get-tuple-element.9), channel_id=1, source_target_pairs={{4,0},{8,4},{12,8},{14,12},{10,14},{6,10},{2,6},{0,2},{5,1},{9,5},... | collective-permute-start | bytes 294920 | tf_op jit(solution)/shard_map/ppermute | solution.py:56
  71.6 5.8 %collective-permute-start.22 = (bf16[8,6144]{1,0:T(8,128)(2,1)S(1)}, bf16[8,6144]{1,0:T(8,128)(2,1)S(1)}, u32[]{:S(2)}, u32[]{:S(2)}) collective-permute-start(bf16[8,6144]{1,0:T(8,128)(2,1)S(1)} %get-tuple-element.14), channel_id=1, source_target_pairs={{0,4},{4,8},{8,12},{12,14},{14,10},{10,6},{6,2},{2,0},{1,5},{5,9},... | collective-permute-start | bytes 294920 | tf_op jit(solution)/shard_map/ppermute | solution.py:56
  72.5 5.5 %collective-permute-start.25 = (bf16[8,6144]{1,0:T(8,128)(2,1)S(1)}, bf16[8,6144]{1,0:T(8,128)(2,1)S(1)}, u32[]{:S(2)}, u32[]{:S(2)}) collective-permute-start(bf16[8,6144]{1,0:T(8,128)(2,1)S(1)} %get-tuple-element.13), channel_id=1, source_target_pairs={{4,0},{8,4},{12,8},{14,12},{10,14},{6,10},{2,6},{0,2},{5,1},{9,5},... | collective-permute-start | bytes 294920 | tf_op jit(solution)/shard_map/ppermute | solution.py:56
  76.1 4.7 %collective-permute-start.21 = (bf16[8,6144]{1,0:T(8,128)(2,1)S(1)}, bf16[8,6144]{1,0:T(8,128)(2,1)S(1)}, u32[]{:S(2)}, u32[]{:S(2)}) collective-permute-start(bf16[8,6144]{1,0:T(8,128)(2,1)S(1)} %fusion.21), channel_id=1, source_target_pairs={{4,0},{8,4},{12,8},{14,12},{10,14},{6,10},{2,6},{0,2},{5,1},{9,5},... | collective-permute-start | bytes 294920 | tf_op jit(solution)/shard_map/ppermute | solution.py:56
  83.5 4.7 %collective-permute-start.26 = (bf16[8,6144]{1,0:T(8,128)(2,1)S(1)}, bf16[8,6144]{1,0:T(8,128)(2,1)S(1)}, u32[]{:S(2)}, u32[]{:S(2)}) collective-permute-start(bf16[8,6144]{1,0:T(8,128)(2,1)S(1)} %get-tuple-element.6), channel_id=1, source_target_pairs={{4,0},{8,4},{12,8},{14,12},{10,14},{6,10},{2,6},{0,2},{5,1},{9,5},... | collective-permute-start | bytes 294920 | tf_op jit(solution)/shard_map/ppermute | solution.py:56
  89.3 4.7 %collective-permute-start.27 = (bf16[8,6144]{1,0:T(8,128)(2,1)S(1)}, bf16[8,6144]{1,0:T(8,128)(2,1)S(1)}, u32[]{:S(2)}, u32[]{:S(2)}) collective-permute-start(bf16[8,6144]{1,0:T(8,128)(2,1)S(1)} %get-tuple-element.11), channel_id=1, source_target_pairs={{4,0},{8,4},{12,8},{14,12},{10,14},{6,10},{2,6},{0,2},{5,1},{9,5},... | collective-permute-start | bytes 294920 | tf_op jit(solution)/shard_map/ppermute | solution.py:56
  89.8 5.6 %collective-permute-start.24 = (bf16[8,6144]{1,0:T(8,128)(2,1)S(1)}, bf16[8,6144]{1,0:T(8,128)(2,1)S(1)}, u32[]{:S(2)}, u32[]{:S(2)}) collective-permute-start(bf16[8,6144]{1,0:T(8,128)(2,1)S(1)} %get-tuple-element.10), channel_id=1, source_target_pairs={{0,4},{4,8},{8,12},{12,14},{14,10},{10,6},{6,2},{2,0},{1,5},{5,9},... | collective-permute-start | bytes 294920 | tf_op jit(solution)/shard_map/ppermute | solution.py:56
  (9 other events, 71.6 us)

commit v2 on v1

--- a/solution.py
+++ b/solution.py
@@ -1,7 +1,11 @@
+import functools
+
 import jax
 import jax.numpy as jnp
 import numpy as np
 from jax import lax
+from jax.experimental import pallas as pl
+from jax.experimental.pallas import tpu as pltpu
 from jax.sharding import PartitionSpec as P
 
 
@@ -27,6 +31,118 @@
     return up + down
 
 
+def route_kernel(own, ids, gates, tokens, mine, theirs, coefficient):
+    rows_here = tokens.shape[0]
+    capacity = mine.shape[0]
+    earlier = (
+        lax.broadcasted_iota(jnp.int32, (rows_here, rows_here), 0)
+        < lax.broadcasted_iota(jnp.int32, (rows_here, rows_here), 1)
+    ).astype(jnp.float32)
+    slots = lax.broadcasted_iota(jnp.int32, (capacity, rows_here), 0).astype(jnp.float32)
+    for side, rows in enumerate((mine, theirs)):
+        expert = own[0] if side == 0 else 1 - own[0]
+        matches = ids[...] == expert
+        picked = jnp.sum(matches.astype(jnp.float32), axis=0, keepdims=True)
+        weight = jnp.sum(jnp.where(matches, gates[...], 0.0), axis=0, keepdims=True)
+        slot = jnp.dot(
+            jnp.broadcast_to(picked, (capacity, rows_here)), earlier, preferred_element_type=jnp.float32
+        )
+        onehot = jnp.where((picked > 0.0) & (slot == slots), 1.0, 0.0)
+        rows[...] = jnp.dot(
+            onehot.astype(jnp.bfloat16), tokens[...], preferred_element_type=jnp.float32
+        ).astype(rows.dtype)
+        coefficient[side * capacity : (side + 1) * capacity, :] = onehot * weight
+
+
+def route(own, ids, gates, tokens):
+    rows_here, width = tokens.shape
+    capacity = rows_here // 4
+    in_vmem = pl.BlockSpec(memory_space=pltpu.VMEM)
+    return pl.pallas_call(
+        route_kernel,
+        out_shape=[
+            pltpu.VMEM((capacity, width), tokens.dtype),
+            pltpu.VMEM((capacity, width), tokens.dtype),
+            pltpu.VMEM((2 * capacity, rows_here), jnp.float32),
+        ],
+        in_specs=[pl.BlockSpec(memory_space=pltpu.SMEM), in_vmem, in_vmem, in_vmem],
+        out_specs=[in_vmem] * 3,
+        compiler_params=pltpu.CompilerParams(vmem_limit_bytes=4 * 1024 * 1024),
+        cost_estimate=pl.CostEstimate(flops=30_000_000_000, bytes_accessed=0, transcendentals=0),
+    )(own, ids, gates, tokens)
+
+
+def combine_kernel(coefficient, first, second, out):
+    left = coefficient[...]
+    high = left.astype(jnp.bfloat16)
+    rest = left - high.astype(jnp.float32)
+    middle = rest.astype(jnp.bfloat16)
+    low = (rest - middle.astype(jnp.float32)).astype(jnp.bfloat16)
+    split = jnp.concatenate([high, middle, low], axis=0)
+    pair = jnp.concatenate([first[...], second[...]], axis=0)
+    rows = jnp.concatenate([pair, pair, pair], axis=0)
+    out[...] = lax.dot_general(
+        split, rows, (((0,), (0,)), ((), ())), preferred_element_type=jnp.float32
+    ).astype(out.dtype)
+
+
+def combine(coefficient, first, second):
+    rows_here, width = coefficient.shape[1], first.shape[1]
+    in_vmem = pl.BlockSpec(memory_space=pltpu.VMEM)
+    return pl.pallas_call(
+        combine_kernel,
+        out_shape=jax.ShapeDtypeStruct((rows_here, width), first.dtype),
+        in_specs=[in_vmem] * 3,
+        out_specs=in_vmem,
+        compiler_params=pltpu.CompilerParams(vmem_limit_bytes=4 * 1024 * 1024),
+    )(coefficient, first, second)
+
+
+def feed_forward_kernel(count, capacity, *refs):
+    blocks, (w_gate, w_up, w_down) = refs[:count], refs[count : count + 3]
+    outs = refs[count + 3 : 2 * count + 3]
+    rows, hidden = refs[2 * count + 3 :]
+    for i, block in enumerate(blocks):
+        rows[i * capacity : (i + 1) * capacity, :] = block[...]
+    units, width = w_down.shape
+    step = min(256, units)
+
+    @pl.loop(0, units // step)
+    def _(j):
+        here = pl.ds(pl.multiple_of(j * step, step), step)
+        gate = jnp.dot(rows[...], w_gate[:, here], preferred_element_type=jnp.float32)
+        up = jnp.dot(rows[...], w_up[:, here], preferred_element_type=jnp.float32)
+        hidden[:, here] = (gate / (1.0 + jnp.exp(-gate)) * up).astype(hidden.dtype)
+
+    @pl.loop(0, width // 512)
+    def _(j):
+        here = pl.ds(pl.multiple_of(j * 512, 512), 512)
+        part = jnp.dot(hidden[...], w_down[:, here], preferred_element_type=jnp.float32)
+        for i, out in enumerate(outs):
+            out[:, here] = part[i * capacity : (i + 1) * capacity]
+
+
+def feed_forward(blocks, w_gate, w_up, w_down):
+    count, (capacity, width) = len(blocks), blocks[0].shape
+    units = w_down.shape[0]
+    weights = [pltpu.with_memory_space_constraint(w, pltpu.VMEM) for w in (w_gate, w_up, w_down)]
+    in_vmem = pl.BlockSpec(memory_space=pltpu.VMEM)
+    return pl.pallas_call(
+        functools.partial(feed_forward_kernel, count, capacity),
+        out_shape=[pltpu.VMEM((capacity, width), jnp.float32) for _ in blocks],
+        in_specs=[in_vmem] * (count + 3),
+        out_specs=[in_vmem] * count,
+        scratch_shapes=[
+            pltpu.VMEM((count * capacity, width), jnp.bfloat16),
+            pltpu.VMEM((count * capacity, units), jnp.bfloat16),
+        ],
+        compiler_params=pltpu.CompilerParams(vmem_limit_bytes=12 * 1024 * 1024),
+        cost_estimate=pl.CostEstimate(
+            flops=6 * count * capacity * width * units, bytes_accessed=0, transcendentals=0
+        ),
+    )(*[pltpu.with_memory_space_constraint(b, pltpu.VMEM) for b in blocks], *weights)
+
+
 def make_per_device(ring):
     count = len(ring)
     forward = [(ring[i], ring[(i + 1) % count]) for i in range(count)]
@@ -63,42 +179,21 @@
         return total
 
     def per_device(tokens, expert_ids, gates, w_gate, w_up, w_down):
-        expert_count = lax.axis_size("expert")
-        rows_here = tokens.shape[0]
-        capacity = rows_here // 4
-        own = lax.axis_index("expert")
-        experts = (own + jnp.arange(expert_count, dtype=jnp.int32)) % expert_count
-        matches = expert_ids[:, :, None] == experts
-        picked = jnp.any(matches, axis=1).astype(jnp.int32)
-        weight = jnp.sum(jnp.where(matches, gates[:, :, None], jnp.float32(0.0)), axis=1)
-        slot_of = jnp.cumsum(picked, axis=0) - picked
-        onehot = (
-            (picked[..., None] == 1) & (slot_of[..., None] == jnp.arange(capacity, dtype=jnp.int32))
-        ).astype(jnp.bfloat16)
-        routed = jnp.einsum("tec,td->ecd", onehot, tokens, preferred_element_type=jnp.float32).astype(
-            jnp.bfloat16
-        )
-        sibling = lax.ppermute(routed[1], "expert", swap)
-        held_a = gather(routed[0], longer, shorter)
+        own = lax.axis_index("expert").astype(jnp.int32).reshape(1)
+        mine, theirs, coefficient = route(own, expert_ids.T, gates.T, tokens)
+        sibling = lax.ppermute(theirs, "expert", swap)
+        held_a = gather(mine, longer, shorter)
         held_b = gather(sibling, shorter, longer)
         keys = [("a", k) for k in held_a] + [("b", k) for k in held_b]
-        rows = jnp.concatenate(list(held_a.values()) + list(held_b.values()), axis=0)
-        gate_proj = jnp.dot(rows, w_gate[0], preferred_element_type=jnp.float32)
-        up_proj = jnp.dot(rows, w_up[0], preferred_element_type=jnp.float32)
-        hidden = (jax.nn.silu(gate_proj) * up_proj).astype(jnp.bfloat16)
-        parts = jnp.dot(hidden, w_down[0], preferred_element_type=jnp.float32)
+        blocks = list(held_a.values()) + list(held_b.values())
+        parts = feed_forward(blocks, w_gate[0], w_up[0], w_down[0])
         terms = {"a": {}, "b": {}}
-        for i, (chain, distance) in enumerate(keys):
-            terms[chain][distance] = parts[i * capacity : (i + 1) * capacity]
+        for (chain, distance), part in zip(keys, parts):
+            terms[chain][distance] = part
         sum_b = scatter_sum(terms["b"], shorter, longer)
         other = lax.ppermute(sum_b.astype(jnp.bfloat16), "expert", swap)
         sum_a = scatter_sum(terms["a"], longer, shorter).astype(jnp.bfloat16)
-        returned = jnp.stack([sum_a, other]).astype(jnp.float32)
-        coefficient = onehot.astype(jnp.float32) * weight[:, :, None]
-        layer_out = jnp.einsum(
-            "tec,ecd->td", coefficient, returned, precision=lax.Precision.HIGHEST
-        )
-        return layer_out.astype(jnp.bfloat16)
+        return combine(coefficient, sum_a, other)
 
     return per_device
 

time: 104 us -> 59.8 us (0.57)
  waiting for transfers between devices: 40.5 us -> 14.1 us
  matrix products: 22.2 us -> 0 us
  Pallas kernels: 0 us -> 9.82 us
  other arithmetic: 9.07 us -> 0.34 us
  starting transfers between devices: 30.7 us -> 32.7 us
  local copies, waits for them, and re-layouts: 0.46 us -> 2.36 us
    dot_general x4 -> x0, matrix products: 22.2 us -> none  [the longest x1 13.6 us: per_device(): parts = jnp.dot(hidden, w_down[0], preferred_element_type=jnp.float32)]
    ppermute x14, waiting for transfers between devices: 23.7 us -> 8.73 us  [flow(): running = lax.ppermute(total.astype(jnp.bfloat16), 'tensor', perm)]
    pallas_call x0 -> x3, Pallas kernels: none -> 9.82 us  [the longest x1 8.3 us: feed_forward(): pl.pallas_call(functools.partial(feed_forward_kernel, count, capacity), o...]
    ppermute x7, starting transfers between devices: 0.86 us -> 9.08 us  [gather(): ahead = lax.ppermute(ahead, 'tensor', backward)]
    ppermute x7, waiting for transfers between devices: 9.04 us -> 3.07 us  [gather(): ahead = lax.ppermute(ahead, 'tensor', backward)]
    ppermute x7, starting transfers between devices: 14.5 us -> 8.74 us  [gather(): behind = lax.ppermute(behind, 'tensor', forward)]
    convert_element_type x6 -> x14, other arithmetic: 5.94 us -> 0.27 us  [flow(): running = lax.ppermute(total.astype(jnp.bfloat16), 'tensor', perm)]
    ppermute x7, waiting for transfers between devices: 5.28 us -> 2.34 us  [gather(): behind = lax.ppermute(behind, 'tensor', forward)]
  transfers between devices with their start and end apart: 30 -> 30, of which waited for: 19 -> 17; matrix products, arithmetic and copies ran while one was open for 3% -> 1% of each run, Pallas kernels for 0% -> 0%
where the time goes in v2:
time: 59.8 us; the launch traced here: 59.6 us
  starting transfers between devices  32.7 us (55%)
  waiting for transfers between devices  14.1 us (24%)
  Pallas kernels  9.82 us (16%)
  local copies, waits for them, and re-layouts  2.36 us (4%)
    ppermute x14, starting transfers between devices, flow(): running = lax.ppermute(total.astype(jnp.bfloat16), 'tensor', perm)  14.3 us
    ppermute x7, starting transfers between devices, gather(): ahead = lax.ppermute(ahead, 'tensor', backward)  9.08 us
    ppermute x7, starting transfers between devices, gather(): behind = lax.ppermute(behind, 'tensor', forward)  8.74 us
    ppermute x14, waiting for transfers between devices, flow(): running = lax.ppermute(total.astype(jnp.bfloat16), 'tensor', perm)  8.73 us
    pallas_call x1, Pallas kernels, feed_forward(): pl.pallas_call(functools.partial(feed_forward_kernel, count, capacity), o...  8.3 us
    ppermute x7, waiting for transfers between devices, gather(): ahead = lax.ppermute(ahead, 'tensor', backward)  3.07 us
    unnamed x12, local copies, waits for them, and re-layouts  2.36 us
    ppermute x7, waiting for transfers between devices, gather(): behind = lax.ppermute(behind, 'tensor', forward)  2.34 us
  transfers between devices with their start and end apart: 30, of which 17 were waited for; matrix products, arithmetic and copies ran while one was open for 1% of the time, Pallas kernels for 0%

profile of v2, /device:TPU:0, one launch (start us, length us, event | category | flops | bytes accessed | tf_op | source)
XLA Modules:
  0.0 59.6 jit_solution(15740318388764218602)
XLA Ops:
  0.0 1.0 %copy-done.3 = bf16[32,6144]{1,0:T(8,128)(2,1)S(1)} copy-done((bf16[32,6144]{1,0:T(8,128)(2,1)S(1)}, bf16[32,6144]{1,0:T(8,128)(2,1)}, u32[]{:S(2)}) %copy-start.3) | copy-done | bytes 393240
  3.4 2.6 %collective-permute-start = (bf16[8,6144]{1,0:T(8,128)(2,1)S(1)}, bf16[8,6144]{1,0:T(8,128)(2,1)S(1)}, u32[]{:S(2)}, u32[]{:S(2)}) collective-permute-start(bf16[8,6144]{1,0:T(8,128)(2,1)S(1)} %get-tuple-element.25.refs_0_), channel_id=1, source_target_pairs={{0,4},{4,8},{8,12},{12,14},{14,10},{10,6},{6,2},{2,0},{1,5},{5,9},... | collective-permute-start | bytes 294920 | tf_op jit(solution)/shard_map/ppermute | solution.py:158
  6.0 1.2 %collective-permute-start.9 = (bf16[8,6144]{1,0:T(8,128)(2,1)S(1)}, bf16[8,6144]{1,0:T(8,128)(2,1)S(1)}, u32[]{:S(2)}, u32[]{:S(2)}) collective-permute-start(bf16[8,6144]{1,0:T(8,128)(2,1)S(1)} %collective-permute-done.7.refs_8_), channel_id=1, source_target_pairs={{4,0},{8,4},{12,8},{14,12},{10,14},{6,10},{2,6},{0,2},{5,1},{9,5},... | collective-permute-start | bytes 294920 | tf_op jit(solution)/shard_map/ppermute | solution.py:161
  7.2 1.6 %collective-permute-start.1 = (bf16[8,6144]{1,0:T(8,128)(2,1)S(1)}, bf16[8,6144]{1,0:T(8,128)(2,1)S(1)}, u32[]{:S(2)}, u32[]{:S(2)}) collective-permute-start(bf16[8,6144]{1,0:T(8,128)(2,1)S(1)} %get-tuple-element.25.refs_0_), channel_id=1, source_target_pairs={{4,0},{8,4},{12,8},{14,12},{10,14},{6,10},{2,6},{0,2},{5,1},{9,5},... | collective-permute-start | bytes 294920 | tf_op jit(solution)/shard_map/ppermute | solution.py:161
  9.4 1.8 %collective-permute-start.2 = (bf16[8,6144]{1,0:T(8,128)(2,1)S(1)}, bf16[8,6144]{1,0:T(8,128)(2,1)S(1)}, u32[]{:S(2)}, u32[]{:S(2)}) collective-permute-start(bf16[8,6144]{1,0:T(8,128)(2,1)S(1)} %collective-permute-done.refs_1_), channel_id=1, source_target_pairs={{0,4},{4,8},{8,12},{12,14},{14,10},{10,6},{6,2},{2,0},{1,5},{5,9},... | collective-permute-start | bytes 294920 | tf_op jit(solution)/shard_map/ppermute | solution.py:158
  11.6 1.2 %collective-permute-start.11 = (bf16[8,6144]{1,0:T(8,128)(2,1)S(1)}, bf16[8,6144]{1,0:T(8,128)(2,1)S(1)}, u32[]{:S(2)}, u32[]{:S(2)}) collective-permute-start(bf16[8,6144]{1,0:T(8,128)(2,1)S(1)} %collective-permute-done.9.refs_10_), channel_id=1, source_target_pairs={{4,0},{8,4},{12,8},{14,12},{10,14},{6,10},{2,6},{0,2},{5,1},{9,5},... | collective-permute-start | bytes 294920 | tf_op jit(solution)/shard_map/ppermute | solution.py:161
  13.0 1.4 %collective-permute-start.3 = (bf16[8,6144]{1,0:T(8,128)(2,1)S(1)}, bf16[8,6144]{1,0:T(8,128)(2,1)S(1)}, u32[]{:S(2)}, u32[]{:S(2)}) collective-permute-start(bf16[8,6144]{1,0:T(8,128)(2,1)S(1)} %collective-permute-done.1.refs_2_), channel_id=1, source_target_pairs={{4,0},{8,4},{12,8},{14,12},{10,14},{6,10},{2,6},{0,2},{5,1},{9,5},... | collective-permute-start | bytes 294920 | tf_op jit(solution)/shard_map/ppermute | solution.py:161
  15.2 1.4 %collective-permute-start.4 = (bf16[8,6144]{1,0:T(8,128)(2,1)S(1)}, bf16[8,6144]{1,0:T(8,128)(2,1)S(1)}, u32[]{:S(2)}, u32[]{:S(2)}) collective-permute-start(bf16[8,6144]{1,0:T(8,128)(2,1)S(1)} %collective-permute-done.2.refs_3_), channel_id=1, source_target_pairs={{0,4},{4,8},{8,12},{12,14},{14,10},{10,6},{6,2},{2,0},{1,5},{5,9},... | collective-permute-start | bytes 294920 | tf_op jit(solution)/shard_map/ppermute | solution.py:158
  17.0 1.2 %collective-permute-start.13 = (bf16[8,6144]{1,0:T(8,128)(2,1)S(1)}, bf16[8,6144]{1,0:T(8,128)(2,1)S(1)}, u32[]{:S(2)}, u32[]{:S(2)}) collective-permute-start(bf16[8,6144]{1,0:T(8,128)(2,1)S(1)} %collective-permute-done.11.refs_12_), channel_id=1, source_target_pairs={{4,0},{8,4},{12,8},{14,12},{10,14},{6,10},{2,6},{0,2},{5,1},{9,5},... | collective-permute-start | bytes 294920 | tf_op jit(solution)/shard_map/ppermute | solution.py:161
  18.4 1.8 %collective-permute-start.5 = (bf16[8,6144]{1,0:T(8,128)(2,1)S(1)}, bf16[8,6144]{1,0:T(8,128)(2,1)S(1)}, u32[]{:S(2)}, u32[]{:S(2)}) collective-permute-start(bf16[8,6144]{1,0:T(8,128)(2,1)S(1)} %collective-permute-done.3.refs_4_), channel_id=1, source_target_pairs={{4,0},{8,4},{12,8},{14,12},{10,14},{6,10},{2,6},{0,2},{5,1},{9,5},... | collective-permute-start | bytes 294920 | tf_op jit(solution)/shard_map/ppermute | solution.py:161
  20.4 1.6 %collective-permute-start.6 = (bf16[8,6144]{1,0:T(8,128)(2,1)S(1)}, bf16[8,6144]{1,0:T(8,128)(2,1)S(1)}, u32[]{:S(2)}, u32[]{:S(2)}) collective-permute-start(bf16[8,6144]{1,0:T(8,128)(2,1)S(1)} %collective-permute-done.4.refs_5_), channel_id=1, source_target_pairs={{0,4},{4,8},{8,12},{12,14},{14,10},{10,6},{6,2},{2,0},{1,5},{5,9},... | collective-permute-start | bytes 294920 | tf_op jit(solution)/shard_map/ppermute | solution.py:158
  22.8 1.0 %collective-permute-done.5.refs_6_ = bf16[8,6144]{1,0:T(8,128)(2,1)S(1)} collective-permute-done((bf16[8,6144]{1,0:T(8,128)(2,1)S(1)}, bf16[8,6144]{1,0:T(8,128)(2,1)S(1)}, u32[]{:S(2)}, u32[]{:S(2)}) %collective-permute-start.5) | collective-permute-done | bytes 98336 | tf_op jit(solution)/shard_map/ppermute | solution.py:161
  23.8 1.0 %collective-permute-done.12.refs_13_ = bf16[8,6144]{1,0:T(8,128)(2,1)S(1)} collective-permute-done((bf16[8,6144]{1,0:T(8,128)(2,1)S(1)}, bf16[8,6144]{1,0:T(8,128)(2,1)S(1)}, u32[]{:S(2)}, u32[]{:S(2)}) %collective-permute-start.12) | collective-permute-done | bytes 98336 | tf_op jit(solution)/shard_map/ppermute | solution.py:158
  24.8 1.1 %collective-permute-done.6.refs_7_ = bf16[8,6144]{1,0:T(8,128)(2,1)S(1)} collective-permute-done((bf16[8,6144]{1,0:T(8,128)(2,1)S(1)}, bf16[8,6144]{1,0:T(8,128)(2,1)S(1)}, u32[]{:S(2)}, u32[]{:S(2)}) %collective-permute-start.6) | collective-permute-done | bytes 98336 | tf_op jit(solution)/shard_map/ppermute | solution.py:158
  26.6 8.3 %shard_map.65 = (f32[8,6144]{1,0:T(8,128)S(1)}, f32[8,6144]{1,0:T(8,128)S(1)}, f32[8,6144]{1,0:T(8,128)S(1)}, f32[8,6144]{1,0:T(8,128)S(1)}, f32[8,6144]{1,0:T(8...) custom-call(bf16[8,6144]{1,0:T(8,128)(2,1)S(1)} %get-tuple-element.2, ...), custom_call_target="tpu_custom_call" | custom-call | flops 4831838208 | tf_op jit(solution)/shard_map/pallas_call | solution.py:130
  35.9 1.2 %collective-permute-start.22 = (bf16[8,6144]{1,0:T(8,128)(2,1)S(1)}, bf16[8,6144]{1,0:T(8,128)(2,1)S(1)}, u32[]{:S(2)}, u32[]{:S(2)}) collective-permute-start(bf16[8,6144]{1,0:T(8,128)(2,1)S(1)} %convert_element_type.105), channel_id=1, source_target_pairs={{0,4},{4,8},{8,12},{12,14},{14,10},{10,6},{6,2},{2,0},{1,5},{5,9},... | collective-permute-start | bytes 294920 | tf_op jit(solution)/shard_map/ppermute | solution.py:172
  38.0 1.2 %collective-permute-start.15 = (bf16[8,6144]{1,0:T(8,128)(2,1)S(1)}, bf16[8,6144]{1,0:T(8,128)(2,1)S(1)}, u32[]{:S(2)}, u32[]{:S(2)}) collective-permute-start(bf16[8,6144]{1,0:T(8,128)(2,1)S(1)} %convert_element_type.90), channel_id=1, source_target_pairs={{0,4},{4,8},{8,12},{12,14},{14,10},{10,6},{6,2},{2,0},{1,5},{5,9},... | collective-permute-start | bytes 294920 | tf_op jit(solution)/shard_map/ppermute | solution.py:172
  39.2 1.4 %collective-permute-done.25 = bf16[8,6144]{1,0:T(8,128)(2,1)S(1)} collective-permute-done((bf16[8,6144]{1,0:T(8,128)(2,1)S(1)}, bf16[8,6144]{1,0:T(8,128)(2,1)S(1)}, u32[]{:S(2)}, u32[]{:S(2)}) %collective-permute-start.25) | collective-permute-done | bytes 98336 | tf_op jit(solution)/shard_map/ppermute | solution.py:172
  41.5 1.4 %collective-permute-start.23 = (bf16[8,6144]{1,0:T(8,128)(2,1)S(1)}, bf16[8,6144]{1,0:T(8,128)(2,1)S(1)}, u32[]{:S(2)}, u32[]{:S(2)}) collective-permute-start(bf16[8,6144]{1,0:T(8,128)(2,1)S(1)} %add_convert_fusion.5), channel_id=1, source_target_pairs={{0,4},{4,8},{8,12},{12,14},{14,10},{10,6},{6,2},{2,0},{1,5},{5,9},... | collective-permute-start | bytes 294920 | tf_op jit(solution)/shard_map/ppermute | solution.py:172
  43.7 1.4 %collective-permute-start.16 = (bf16[8,6144]{1,0:T(8,128)(2,1)S(1)}, bf16[8,6144]{1,0:T(8,128)(2,1)S(1)}, u32[]{:S(2)}, u32[]{:S(2)}) collective-permute-start(bf16[8,6144]{1,0:T(8,128)(2,1)S(1)} %add_convert_fusion.11), channel_id=1, source_target_pairs={{0,4},{4,8},{8,12},{12,14},{14,10},{10,6},{6,2},{2,0},{1,5},{5,9},... | collective-permute-start | bytes 294920 | tf_op jit(solution)/shard_map/ppermute | solution.py:172
  47.8 1.2 %collective-permute-start.21 = (bf16[8,6144]{1,0:T(8,128)(2,1)S(1)}, bf16[8,6144]{1,0:T(8,128)(2,1)S(1)}, u32[]{:S(2)}, u32[]{:S(2)}) collective-permute-start(bf16[8,6144]{1,0:T(8,128)(2,1)S(1)} %add_convert_fusion.7), channel_id=1, source_target_pairs={{4,0},{8,4},{12,8},{14,12},{10,14},{6,10},{2,6},{0,2},{5,1},{9,5},... | collective-permute-start | bytes 294920 | tf_op jit(solution)/shard_map/ppermute | solution.py:172
  51.3 2.5 %collective-permute-done.17 = bf16[8,6144]{1,0:T(8,128)(2,1)S(1)} collective-permute-done((bf16[8,6144]{1,0:T(8,128)(2,1)S(1)}, bf16[8,6144]{1,0:T(8,128)(2,1)S(1)}, u32[]{:S(2)}, u32[]{:S(2)}) %collective-permute-start.17) | collective-permute-done | bytes 98336 | tf_op jit(solution)/shard_map/ppermute | solution.py:172
  55.1 3.3 %collective-permute-done.18 = bf16[8,6144]{1,0:T(8,128)(2,1)S(1)} collective-permute-done((bf16[8,6144]{1,0:T(8,128)(2,1)S(1)}, bf16[8,6144]{1,0:T(8,128)(2,1)S(1)}, u32[]{:S(2)}, u32[]{:S(2)}) %collective-permute-start.18) | collective-permute-done | bytes 98336 | tf_op jit(solution)/shard_map/ppermute | solution.py:172
  58.5 1.0 %shard_map.66 = bf16[32,6144]{1,0:T(8,128)(2,1)} custom-call(f32[16,32]{1,0:T(8,128)S(1)} %get-tuple-element.24.coefficient, bf16[8,6144]{1,0:T(8,128)(2,1)S(1)} %add_convert_fusion.6.first, bf16[8,6144]{1,0:T(8,128)(2,1)S(1)} %collective-permute-done.29.second), custom_call_target="tpu_custom_call" | custom-call | tf_op jit(solution)/shard_map/pallas_call | solution.py:92
  (67 shorter events, 16.6 us)
Async XLA Ops:
  3.4 6.0 %collective-permute-start = (bf16[8,6144]{1,0:T(8,128)(2,1)S(1)}, bf16[8,6144]{1,0:T(8,128)(2,1)S(1)}, u32[]{:S(2)}, u32[]{:S(2)}) collective-permute-start(bf16[8,6144]{1,0:T(8,128)(2,1)S(1)} %get-tuple-element.25.refs_0_), channel_id=1, source_target_pairs={{0,4},{4,8},{8,12},{12,14},{14,10},{10,6},{6,2},{2,0},{1,5},{5,9},... | collective-permute-start | bytes 294920 | tf_op jit(solution)/shard_map/ppermute | solution.py:158
  6.0 5.6 %collective-permute-start.9 = (bf16[8,6144]{1,0:T(8,128)(2,1)S(1)}, bf16[8,6144]{1,0:T(8,128)(2,1)S(1)}, u32[]{:S(2)}, u32[]{:S(2)}) collective-permute-start(bf16[8,6144]{1,0:T(8,128)(2,1)S(1)} %collective-permute-done.7.refs_8_), channel_id=1, source_target_pairs={{4,0},{8,4},{12,8},{14,12},{10,14},{6,10},{2,6},{0,2},{5,1},{9,5},... | collective-permute-start | bytes 294920 | tf_op jit(solution)/shard_map/ppermute | solution.py:161
  7.2 5.8 %collective-permute-start.1 = (bf16[8,6144]{1,0:T(8,128)(2,1)S(1)}, bf16[8,6144]{1,0:T(8,128)(2,1)S(1)}, u32[]{:S(2)}, u32[]{:S(2)}) collective-permute-start(bf16[8,6144]{1,0:T(8,128)(2,1)S(1)} %get-tuple-element.25.refs_0_), channel_id=1, source_target_pairs={{4,0},{8,4},{12,8},{14,12},{10,14},{6,10},{2,6},{0,2},{5,1},{9,5},... | collective-permute-start | bytes 294920 | tf_op jit(solution)/shard_map/ppermute | solution.py:161
  8.8 5.6 %collective-permute-start.8 = (bf16[8,6144]{1,0:T(8,128)(2,1)S(1)}, bf16[8,6144]{1,0:T(8,128)(2,1)S(1)}, u32[]{:S(2)}, u32[]{:S(2)}) collective-permute-start(bf16[8,6144]{1,0:T(8,128)(2,1)S(1)} %collective-permute-done.7.refs_8_), channel_id=1, source_target_pairs={{0,4},{4,8},{8,12},{12,14},{14,10},{10,6},{6,2},{2,0},{1,5},{5,9},... | collective-permute-start | bytes 294920 | tf_op jit(solution)/shard_map/ppermute | solution.py:158
  9.4 5.8 %collective-permute-start.2 = (bf16[8,6144]{1,0:T(8,128)(2,1)S(1)}, bf16[8,6144]{1,0:T(8,128)(2,1)S(1)}, u32[]{:S(2)}, u32[]{:S(2)}) collective-permute-start(bf16[8,6144]{1,0:T(8,128)(2,1)S(1)} %collective-permute-done.refs_1_), channel_id=1, source_target_pairs={{0,4},{4,8},{8,12},{12,14},{14,10},{10,6},{6,2},{2,0},{1,5},{5,9},... | collective-permute-start | bytes 294920 | tf_op jit(solution)/shard_map/ppermute | solution.py:158
  11.6 5.4 %collective-permute-start.11 = (bf16[8,6144]{1,0:T(8,128)(2,1)S(1)}, bf16[8,6144]{1,0:T(8,128)(2,1)S(1)}, u32[]{:S(2)}, u32[]{:S(2)}) collective-permute-start(bf16[8,6144]{1,0:T(8,128)(2,1)S(1)} %collective-permute-done.9.refs_10_), channel_id=1, source_target_pairs={{4,0},{8,4},{12,8},{14,12},{10,14},{6,10},{2,6},{0,2},{5,1},{9,5},... | collective-permute-start | bytes 294920 | tf_op jit(solution)/shard_map/ppermute | solution.py:161
  13.0 5.4 %collective-permute-start.3 = (bf16[8,6144]{1,0:T(8,128)(2,1)S(1)}, bf16[8,6144]{1,0:T(8,128)(2,1)S(1)}, u32[]{:S(2)}, u32[]{:S(2)}) collective-permute-start(bf16[8,6144]{1,0:T(8,128)(2,1)S(1)} %collective-permute-done.1.refs_2_), channel_id=1, source_target_pairs={{4,0},{8,4},{12,8},{14,12},{10,14},{6,10},{2,6},{0,2},{5,1},{9,5},... | collective-permute-start | bytes 294920 | tf_op jit(solution)/shard_map/ppermute | solution.py:161
  14.4 5.8 %collective-permute-start.10 = (bf16[8,6144]{1,0:T(8,128)(2,1)S(1)}, bf16[8,6144]{1,0:T(8,128)(2,1)S(1)}, u32[]{:S(2)}, u32[]{:S(2)}) collective-permute-start(bf16[8,6144]{1,0:T(8,128)(2,1)S(1)} %collective-permute-done.8.refs_9_), channel_id=1, source_target_pairs={{0,4},{4,8},{8,12},{12,14},{14,10},{10,6},{6,2},{2,0},{1,5},{5,9},... | collective-permute-start | bytes 294920 | tf_op jit(solution)/shard_map/ppermute | solution.py:158
  15.2 5.3 %collective-permute-start.4 = (bf16[8,6144]{1,0:T(8,128)(2,1)S(1)}, bf16[8,6144]{1,0:T(8,128)(2,1)S(1)}, u32[]{:S(2)}, u32[]{:S(2)}) collective-permute-start(bf16[8,6144]{1,0:T(8,128)(2,1)S(1)} %collective-permute-done.2.refs_3_), channel_id=1, source_target_pairs={{0,4},{4,8},{8,12},{12,14},{14,10},{10,6},{6,2},{2,0},{1,5},{5,9},... | collective-permute-start | bytes 294920 | tf_op jit(solution)/shard_map/ppermute | solution.py:158
  17.0 5.0 %collective-permute-start.13 = (bf16[8,6144]{1,0:T(8,128)(2,1)S(1)}, bf16[8,6144]{1,0:T(8,128)(2,1)S(1)}, u32[]{:S(2)}, u32[]{:S(2)}) collective-permute-start(bf16[8,6144]{1,0:T(8,128)(2,1)S(1)} %collective-permute-done.11.refs_12_), channel_id=1, source_target_pairs={{4,0},{8,4},{12,8},{14,12},{10,14},{6,10},{2,6},{0,2},{5,1},{9,5},... | collective-permute-start | bytes 294920 | tf_op jit(solution)/shard_map/ppermute | solution.py:161
  18.4 5.4 %collective-permute-start.5 = (bf16[8,6144]{1,0:T(8,128)(2,1)S(1)}, bf16[8,6144]{1,0:T(8,128)(2,1)S(1)}, u32[]{:S(2)}, u32[]{:S(2)}) collective-permute-start(bf16[8,6144]{1,0:T(8,128)(2,1)S(1)} %collective-permute-done.3.refs_4_), channel_id=1, source_target_pairs={{4,0},{8,4},{12,8},{14,12},{10,14},{6,10},{2,6},{0,2},{5,1},{9,5},... | collective-permute-start | bytes 294920 | tf_op jit(solution)/shard_map/ppermute | solution.py:161
  20.4 5.4 %collective-permute-start.6 = (bf16[8,6144]{1,0:T(8,128)(2,1)S(1)}, bf16[8,6144]{1,0:T(8,128)(2,1)S(1)}, u32[]{:S(2)}, u32[]{:S(2)}) collective-permute-start(bf16[8,6144]{1,0:T(8,128)(2,1)S(1)} %collective-permute-done.4.refs_5_), channel_id=1, source_target_pairs={{0,4},{4,8},{8,12},{12,14},{14,10},{10,6},{6,2},{2,0},{1,5},{5,9},... | collective-permute-start | bytes 294920 | tf_op jit(solution)/shard_map/ppermute | solution.py:158
  35.0 5.6 %collective-permute-start.25 = (bf16[8,6144]{1,0:T(8,128)(2,1)S(1)}, bf16[8,6144]{1,0:T(8,128)(2,1)S(1)}, u32[]{:S(2)}, u32[]{:S(2)}) collective-permute-start(bf16[8,6144]{1,0:T(8,128)(2,1)S(1)} %convert_element_type.111), channel_id=1, source_target_pairs={{4,0},{8,4},{12,8},{14,12},{10,14},{6,10},{2,6},{0,2},{5,1},{9,5},... | collective-permute-start | bytes 294920 | tf_op jit(solution)/shard_map/ppermute | solution.py:172
  35.9 5.6 %collective-permute-start.22 = (bf16[8,6144]{1,0:T(8,128)(2,1)S(1)}, bf16[8,6144]{1,0:T(8,128)(2,1)S(1)}, u32[]{:S(2)}, u32[]{:S(2)}) collective-permute-start(bf16[8,6144]{1,0:T(8,128)(2,1)S(1)} %convert_element_type.105), channel_id=1, source_target_pairs={{0,4},{4,8},{8,12},{12,14},{14,10},{10,6},{6,2},{2,0},{1,5},{5,9},... | collective-permute-start | bytes 294920 | tf_op jit(solution)/shard_map/ppermute | solution.py:172
  37.1 5.7 %collective-permute-start.19 = (bf16[8,6144]{1,0:T(8,128)(2,1)S(1)}, bf16[8,6144]{1,0:T(8,128)(2,1)S(1)}, u32[]{:S(2)}, u32[]{:S(2)}) collective-permute-start(bf16[8,6144]{1,0:T(8,128)(2,1)S(1)} %convert_element_type.98), channel_id=1, source_target_pairs={{4,0},{8,4},{12,8},{14,12},{10,14},{6,10},{2,6},{0,2},{5,1},{9,5},... | collective-permute-start | bytes 294920 | tf_op jit(solution)/shard_map/ppermute | solution.py:172
  38.0 5.7 %collective-permute-start.15 = (bf16[8,6144]{1,0:T(8,128)(2,1)S(1)}, bf16[8,6144]{1,0:T(8,128)(2,1)S(1)}, u32[]{:S(2)}, u32[]{:S(2)}) collective-permute-start(bf16[8,6144]{1,0:T(8,128)(2,1)S(1)} %convert_element_type.90), channel_id=1, source_target_pairs={{0,4},{4,8},{8,12},{12,14},{14,10},{10,6},{6,2},{2,0},{1,5},{5,9},... | collective-permute-start | bytes 294920 | tf_op jit(solution)/shard_map/ppermute | solution.py:172
  40.6 5.1 %collective-permute-start.26 = (bf16[8,6144]{1,0:T(8,128)(2,1)S(1)}, bf16[8,6144]{1,0:T(8,128)(2,1)S(1)}, u32[]{:S(2)}, u32[]{:S(2)}) collective-permute-start(bf16[8,6144]{1,0:T(8,128)(2,1)S(1)} %add_convert_fusion.3), channel_id=1, source_target_pairs={{4,0},{8,4},{12,8},{14,12},{10,14},{6,10},{2,6},{0,2},{5,1},{9,5},... | collective-permute-start | bytes 294920 | tf_op jit(solution)/shard_map/ppermute | solution.py:172
  41.5 5.4 %collective-permute-start.23 = (bf16[8,6144]{1,0:T(8,128)(2,1)S(1)}, bf16[8,6144]{1,0:T(8,128)(2,1)S(1)}, u32[]{:S(2)}, u32[]{:S(2)}) collective-permute-start(bf16[8,6144]{1,0:T(8,128)(2,1)S(1)} %add_convert_fusion.5), channel_id=1, source_target_pairs={{0,4},{4,8},{8,12},{12,14},{14,10},{10,6},{6,2},{2,0},{1,5},{5,9},... | collective-permute-start | bytes 294920 | tf_op jit(solution)/shard_map/ppermute | solution.py:172
  42.9 4.9 %collective-permute-start.20 = (bf16[8,6144]{1,0:T(8,128)(2,1)S(1)}, bf16[8,6144]{1,0:T(8,128)(2,1)S(1)}, u32[]{:S(2)}, u32[]{:S(2)}) collective-permute-start(bf16[8,6144]{1,0:T(8,128)(2,1)S(1)} %add_convert_fusion.8), channel_id=1, source_target_pairs={{4,0},{8,4},{12,8},{14,12},{10,14},{6,10},{2,6},{0,2},{5,1},{9,5},... | collective-permute-start | bytes 294920 | tf_op jit(solution)/shard_map/ppermute | solution.py:172
  43.7 5.4 %collective-permute-start.16 = (bf16[8,6144]{1,0:T(8,128)(2,1)S(1)}, bf16[8,6144]{1,0:T(8,128)(2,1)S(1)}, u32[]{:S(2)}, u32[]{:S(2)}) collective-permute-start(bf16[8,6144]{1,0:T(8,128)(2,1)S(1)} %add_convert_fusion.11), channel_id=1, source_target_pairs={{0,4},{4,8},{8,12},{12,14},{14,10},{10,6},{6,2},{2,0},{1,5},{5,9},... | collective-permute-start | bytes 294920 | tf_op jit(solution)/shard_map/ppermute | solution.py:172
  45.7 4.7 %collective-permute-start.27 = (bf16[8,6144]{1,0:T(8,128)(2,1)S(1)}, bf16[8,6144]{1,0:T(8,128)(2,1)S(1)}, u32[]{:S(2)}, u32[]{:S(2)}) collective-permute-start(bf16[8,6144]{1,0:T(8,128)(2,1)S(1)} %add_convert_fusion.2), channel_id=1, source_target_pairs={{4,0},{8,4},{12,8},{14,12},{10,14},{6,10},{2,6},{0,2},{5,1},{9,5},... | collective-permute-start | bytes 294920 | tf_op jit(solution)/shard_map/ppermute | solution.py:172
  46.9 7.8 %collective-permute-start.24 = (bf16[8,6144]{1,0:T(8,128)(2,1)S(1)}, bf16[8,6144]{1,0:T(8,128)(2,1)S(1)}, u32[]{:S(2)}, u32[]{:S(2)}) collective-permute-start(bf16[8,6144]{1,0:T(8,128)(2,1)S(1)} %add_convert_fusion.4), channel_id=1, source_target_pairs={{0,4},{4,8},{8,12},{12,14},{14,10},{10,6},{6,2},{2,0},{1,5},{5,9},... | collective-permute-start | bytes 294920 | tf_op jit(solution)/shard_map/ppermute | solution.py:172
  47.8 7.3 %collective-permute-start.21 = (bf16[8,6144]{1,0:T(8,128)(2,1)S(1)}, bf16[8,6144]{1,0:T(8,128)(2,1)S(1)}, u32[]{:S(2)}, u32[]{:S(2)}) collective-permute-start(bf16[8,6144]{1,0:T(8,128)(2,1)S(1)} %add_convert_fusion.7), channel_id=1, source_target_pairs={{4,0},{8,4},{12,8},{14,12},{10,14},{6,10},{2,6},{0,2},{5,1},{9,5},... | collective-permute-start | bytes 294920 | tf_op jit(solution)/shard_map/ppermute | solution.py:172
  49.1 4.7 %collective-permute-start.17 = (bf16[8,6144]{1,0:T(8,128)(2,1)S(1)}, bf16[8,6144]{1,0:T(8,128)(2,1)S(1)}, u32[]{:S(2)}, u32[]{:S(2)}) collective-permute-start(bf16[8,6144]{1,0:T(8,128)(2,1)S(1)} %add_convert_fusion.10), channel_id=1, source_target_pairs={{0,4},{4,8},{8,12},{12,14},{14,10},{10,6},{6,2},{2,0},{1,5},{5,9},... | collective-permute-start | bytes 294920 | tf_op jit(solution)/shard_map/ppermute | solution.py:172
  (12 other events, 100.4 us)

commit v3 on v2

--- a/solution.py
+++ b/solution.py
@@ -31,7 +31,17 @@
     return up + down
 
 
-def route_kernel(own, ids, gates, tokens, mine, theirs, coefficient):
+def route_kernel(own, *refs):
+    sources, (mine, theirs, coefficient) = refs[:3], refs[3:6]
+    (ids, gates, tokens), arrived = refs[6:9], refs[9]
+    copies = [
+        pltpu.make_async_copy(source, target, arrived.at[i])
+        for i, (source, target) in enumerate(zip(sources, (ids, gates, tokens)))
+    ]
+    for copy in copies:
+        copy.start()
+    for copy in copies:
+        copy.wait()
     rows_here = tokens.shape[0]
     capacity = mine.shape[0]
     earlier = (
@@ -65,11 +75,13 @@
             pltpu.VMEM((capacity, width), tokens.dtype),
             pltpu.VMEM((2 * capacity, rows_here), jnp.float32),
         ],
-        in_specs=[pl.BlockSpec(memory_space=pltpu.SMEM), in_vmem, in_vmem, in_vmem],
+        in_specs=[pl.BlockSpec(memory_space=pltpu.SMEM)] + [pl.BlockSpec(memory_space=pl.ANY)] * 3,
         out_specs=[in_vmem] * 3,
+        scratch_shapes=[pltpu.VMEM(a.shape, a.dtype) for a in (ids, gates, tokens)]
+        + [pltpu.SemaphoreType.DMA((3,))],
         compiler_params=pltpu.CompilerParams(vmem_limit_bytes=4 * 1024 * 1024),
         cost_estimate=pl.CostEstimate(flops=30_000_000_000, bytes_accessed=0, transcendentals=0),
-    )(own, ids, gates, tokens)
+    )(own, *[pltpu.with_memory_space_constraint(a, pltpu.HBM) for a in (ids, gates, tokens)])
 
 
 def combine_kernel(coefficient, first, second, out):
@@ -101,25 +113,15 @@
 def feed_forward_kernel(count, capacity, *refs):
     blocks, (w_gate, w_up, w_down) = refs[:count], refs[count : count + 3]
     outs = refs[count + 3 : 2 * count + 3]
-    rows, hidden = refs[2 * count + 3 :]
+    rows, gate, hidden, parts = refs[2 * count + 3 :]
     for i, block in enumerate(blocks):
         rows[i * capacity : (i + 1) * capacity, :] = block[...]
-    units, width = w_down.shape
-    step = min(256, units)
-
-    @pl.loop(0, units // step)
-    def _(j):
-        here = pl.ds(pl.multiple_of(j * step, step), step)
-        gate = jnp.dot(rows[...], w_gate[:, here], preferred_element_type=jnp.float32)
-        up = jnp.dot(rows[...], w_up[:, here], preferred_element_type=jnp.float32)
-        hidden[:, here] = (gate / (1.0 + jnp.exp(-gate)) * up).astype(hidden.dtype)
-
-    @pl.loop(0, width // 512)
-    def _(j):
-        here = pl.ds(pl.multiple_of(j * 512, 512), 512)
-        part = jnp.dot(hidden[...], w_down[:, here], preferred_element_type=jnp.float32)
-        for i, out in enumerate(outs):
-            out[:, here] = part[i * capacity : (i + 1) * capacity]
+    gate[...] = jnp.dot(rows[...], w_gate[...], preferred_element_type=jnp.float32)
+    up = jnp.dot(rows[...], w_up[...], preferred_element_type=jnp.float32)
+    hidden[...] = (gate[...] / (1.0 + jnp.exp(-gate[...])) * up).astype(hidden.dtype)
+    parts[...] = jnp.dot(hidden[...], w_down[...], preferred_element_type=jnp.float32).astype(parts.dtype)
+    for i, out in enumerate(outs):
+        out[...] = parts[i * capacity : (i + 1) * capacity, :].astype(out.dtype)
 
 
 def feed_forward(blocks, w_gate, w_up, w_down):
@@ -127,20 +129,23 @@
     units = w_down.shape[0]
     weights = [pltpu.with_memory_space_constraint(w, pltpu.VMEM) for w in (w_gate, w_up, w_down)]
     in_vmem = pl.BlockSpec(memory_space=pltpu.VMEM)
-    return pl.pallas_call(
+    parts = pl.pallas_call(
         functools.partial(feed_forward_kernel, count, capacity),
         out_shape=[pltpu.VMEM((capacity, width), jnp.float32) for _ in blocks],
         in_specs=[in_vmem] * (count + 3),
         out_specs=[in_vmem] * count,
         scratch_shapes=[
             pltpu.VMEM((count * capacity, width), jnp.bfloat16),
+            pltpu.VMEM((count * capacity, units), jnp.float32),
             pltpu.VMEM((count * capacity, units), jnp.bfloat16),
+            pltpu.VMEM((count * capacity, width), jnp.float32),
         ],
         compiler_params=pltpu.CompilerParams(vmem_limit_bytes=12 * 1024 * 1024),
         cost_estimate=pl.CostEstimate(
             flops=6 * count * capacity * width * units, bytes_accessed=0, transcendentals=0
         ),
     )(*[pltpu.with_memory_space_constraint(b, pltpu.VMEM) for b in blocks], *weights)
+    return parts
 
 
 def make_per_device(ring):
@@ -168,11 +173,11 @@
             for step in range(steps, 0, -1):
                 distance = sign * step
                 term = terms[distance] if distance in terms else terms[distance - sign * count]
-                total = term if running is None else term + running.astype(jnp.float32)
+                total = term.astype(jnp.float32) + (0 if running is None else running.astype(jnp.float32))
                 running = lax.ppermute(total.astype(jnp.bfloat16), "tensor", perm)
             return running
 
-        total = terms[0]
+        total = terms[0].astype(jnp.float32)
         for part in (flow(forward_steps, 1, forward), flow(backward_steps, -1, backward)):
             if part is not None:
                 total = total + part.astype(jnp.float32)

time: 59.8 us -> 55.4 us (0.926)
  local copies, waits for them, and re-layouts: 2.36 us -> 0.01 us
  Pallas kernels: 9.82 us -> 7.88 us
    pallas_call x1, Pallas kernels: 8.3 us -> 5.14 us  [feed_forward(): pl.pallas_call(functools.partial(feed_forward_kernel, count, capacity), o...]
    unnamed x12 -> x6, local copies, waits for them, and re-layouts: 2.36 us -> 0.01 us
    pallas_call x1, Pallas kernels: 0.48 us -> 1.69 us  [route(): pl.pallas_call(route_kernel, out_shape=[pltpu.VMEM((capacity, width), tok...]
where the time goes in v3:
time: 55.4 us; the launch traced here: 55.3 us
  starting transfers between devices  32.8 us (59%)
  waiting for transfers between devices  14.1 us (25%)
  Pallas kernels  7.88 us (14%)
    ppermute x14, starting transfers between devices, flow(): running = lax.ppermute(total.astype(jnp.bfloat16), 'tensor', perm)  14.3 us
    ppermute x7, starting transfers between devices, gather(): ahead = lax.ppermute(ahead, 'tensor', backward)  9.08 us
    ppermute x7, starting transfers between devices, gather(): behind = lax.ppermute(behind, 'tensor', forward)  8.76 us
    ppermute x14, waiting for transfers between devices, flow(): running = lax.ppermute(total.astype(jnp.bfloat16), 'tensor', perm)  8.71 us
    pallas_call x1, Pallas kernels, feed_forward(): pl.pallas_call(functools.partial(feed_forward_kernel, count, capacity), o...  5.14 us
    ppermute x7, waiting for transfers between devices, gather(): ahead = lax.ppermute(ahead, 'tensor', backward)  3.07 us
    ppermute x7, waiting for transfers between devices, gather(): behind = lax.ppermute(behind, 'tensor', forward)  2.33 us
    pallas_call x1, Pallas kernels, route(): pl.pallas_call(route_kernel, out_shape=[pltpu.VMEM((capacity, width), tok...  1.69 us
  transfers between devices with their start and end apart: 30, of which 17 were waited for; matrix products, arithmetic and copies ran while one was open for 1% of the time, Pallas kernels for 0%

profile of v3, /device:TPU:0, one launch (start us, length us, event | category | flops | bytes accessed | tf_op | source)
XLA Modules:
  0.0 55.3 jit_solution(5459026743740855702)
XLA Ops:
  0.0 1.7 %shard_map.64 = (bf16[8,6144]{1,0:T(8,128)(2,1)S(1)}, bf16[8,6144]{1,0:T(8,128)(2,1)S(1)}, f32[16,32]{1,0:T(8,128)S(1)}) custom-call(s32[1]{0:T(128)} %bitcast.own, s32[2,32]{1,0:T(2,128)} %bitcast.9, f32[2,32]{1,0:T(2,128)} %bitcast.10, bf16[32,6144]{1,0:T(8,128)(2,1)} %refs_2_.1), custom_call_target="tpu_custom_call" | custom-call | flops 30000001024 | tf_op jit(solution)/shard_map/pallas_call | solution.py:71
  2.2 2.6 %collective-permute-start = (bf16[8,6144]{1,0:T(8,128)(2,1)S(1)}, bf16[8,6144]{1,0:T(8,128)(2,1)S(1)}, u32[]{:S(2)}, u32[]{:S(2)}) collective-permute-start(bf16[8,6144]{1,0:T(8,128)(2,1)S(1)} %get-tuple-element.25.refs_0_), channel_id=1, source_target_pairs={{0,4},{4,8},{8,12},{12,14},{14,10},{10,6},{6,2},{2,0},{1,5},{5,9},... | collective-permute-start | bytes 294920 | tf_op jit(solution)/shard_map/ppermute | solution.py:163
  4.9 1.2 %collective-permute-start.9 = (bf16[8,6144]{1,0:T(8,128)(2,1)S(1)}, bf16[8,6144]{1,0:T(8,128)(2,1)S(1)}, u32[]{:S(2)}, u32[]{:S(2)}) collective-permute-start(bf16[8,6144]{1,0:T(8,128)(2,1)S(1)} %collective-permute-done.7.refs_8_), channel_id=1, source_target_pairs={{4,0},{8,4},{12,8},{14,12},{10,14},{6,10},{2,6},{0,2},{5,1},{9,5},... | collective-permute-start | bytes 294920 | tf_op jit(solution)/shard_map/ppermute | solution.py:166
  6.0 1.6 %collective-permute-start.1 = (bf16[8,6144]{1,0:T(8,128)(2,1)S(1)}, bf16[8,6144]{1,0:T(8,128)(2,1)S(1)}, u32[]{:S(2)}, u32[]{:S(2)}) collective-permute-start(bf16[8,6144]{1,0:T(8,128)(2,1)S(1)} %get-tuple-element.25.refs_0_), channel_id=1, source_target_pairs={{4,0},{8,4},{12,8},{14,12},{10,14},{6,10},{2,6},{0,2},{5,1},{9,5},... | collective-permute-start | bytes 294920 | tf_op jit(solution)/shard_map/ppermute | solution.py:166
  8.2 1.8 %collective-permute-start.2 = (bf16[8,6144]{1,0:T(8,128)(2,1)S(1)}, bf16[8,6144]{1,0:T(8,128)(2,1)S(1)}, u32[]{:S(2)}, u32[]{:S(2)}) collective-permute-start(bf16[8,6144]{1,0:T(8,128)(2,1)S(1)} %collective-permute-done.refs_1_), channel_id=1, source_target_pairs={{0,4},{4,8},{8,12},{12,14},{14,10},{10,6},{6,2},{2,0},{1,5},{5,9},... | collective-permute-start | bytes 294920 | tf_op jit(solution)/shard_map/ppermute | solution.py:163
  10.5 1.2 %collective-permute-start.11 = (bf16[8,6144]{1,0:T(8,128)(2,1)S(1)}, bf16[8,6144]{1,0:T(8,128)(2,1)S(1)}, u32[]{:S(2)}, u32[]{:S(2)}) collective-permute-start(bf16[8,6144]{1,0:T(8,128)(2,1)S(1)} %collective-permute-done.9.refs_10_), channel_id=1, source_target_pairs={{4,0},{8,4},{12,8},{14,12},{10,14},{6,10},{2,6},{0,2},{5,1},{9,5},... | collective-permute-start | bytes 294920 | tf_op jit(solution)/shard_map/ppermute | solution.py:166
  11.8 1.4 %collective-permute-start.3 = (bf16[8,6144]{1,0:T(8,128)(2,1)S(1)}, bf16[8,6144]{1,0:T(8,128)(2,1)S(1)}, u32[]{:S(2)}, u32[]{:S(2)}) collective-permute-start(bf16[8,6144]{1,0:T(8,128)(2,1)S(1)} %collective-permute-done.1.refs_2_), channel_id=1, source_target_pairs={{4,0},{8,4},{12,8},{14,12},{10,14},{6,10},{2,6},{0,2},{5,1},{9,5},... | collective-permute-start | bytes 294920 | tf_op jit(solution)/shard_map/ppermute | solution.py:166
  14.0 1.4 %collective-permute-start.4 = (bf16[8,6144]{1,0:T(8,128)(2,1)S(1)}, bf16[8,6144]{1,0:T(8,128)(2,1)S(1)}, u32[]{:S(2)}, u32[]{:S(2)}) collective-permute-start(bf16[8,6144]{1,0:T(8,128)(2,1)S(1)} %collective-permute-done.2.refs_3_), channel_id=1, source_target_pairs={{0,4},{4,8},{8,12},{12,14},{14,10},{10,6},{6,2},{2,0},{1,5},{5,9},... | collective-permute-start | bytes 294920 | tf_op jit(solution)/shard_map/ppermute | solution.py:163
  15.9 1.2 %collective-permute-start.13 = (bf16[8,6144]{1,0:T(8,128)(2,1)S(1)}, bf16[8,6144]{1,0:T(8,128)(2,1)S(1)}, u32[]{:S(2)}, u32[]{:S(2)}) collective-permute-start(bf16[8,6144]{1,0:T(8,128)(2,1)S(1)} %collective-permute-done.11.refs_12_), channel_id=1, source_target_pairs={{4,0},{8,4},{12,8},{14,12},{10,14},{6,10},{2,6},{0,2},{5,1},{9,5},... | collective-permute-start | bytes 294920 | tf_op jit(solution)/shard_map/ppermute | solution.py:166
  17.3 1.8 %collective-permute-start.5 = (bf16[8,6144]{1,0:T(8,128)(2,1)S(1)}, bf16[8,6144]{1,0:T(8,128)(2,1)S(1)}, u32[]{:S(2)}, u32[]{:S(2)}) collective-permute-start(bf16[8,6144]{1,0:T(8,128)(2,1)S(1)} %collective-permute-done.3.refs_4_), channel_id=1, source_target_pairs={{4,0},{8,4},{12,8},{14,12},{10,14},{6,10},{2,6},{0,2},{5,1},{9,5},... | collective-permute-start | bytes 294920 | tf_op jit(solution)/shard_map/ppermute | solution.py:166
  19.3 1.6 %collective-permute-start.6 = (bf16[8,6144]{1,0:T(8,128)(2,1)S(1)}, bf16[8,6144]{1,0:T(8,128)(2,1)S(1)}, u32[]{:S(2)}, u32[]{:S(2)}) collective-permute-start(bf16[8,6144]{1,0:T(8,128)(2,1)S(1)} %collective-permute-done.4.refs_5_), channel_id=1, source_target_pairs={{0,4},{4,8},{8,12},{12,14},{14,10},{10,6},{6,2},{2,0},{1,5},{5,9},... | collective-permute-start | bytes 294920 | tf_op jit(solution)/shard_map/ppermute | solution.py:163
  21.6 1.0 %collective-permute-done.5.refs_6_ = bf16[8,6144]{1,0:T(8,128)(2,1)S(1)} collective-permute-done((bf16[8,6144]{1,0:T(8,128)(2,1)S(1)}, bf16[8,6144]{1,0:T(8,128)(2,1)S(1)}, u32[]{:S(2)}, u32[]{:S(2)}) %collective-permute-start.5) | collective-permute-done | bytes 98336 | tf_op jit(solution)/shard_map/ppermute | solution.py:166
  22.7 1.0 %collective-permute-done.12.refs_13_ = bf16[8,6144]{1,0:T(8,128)(2,1)S(1)} collective-permute-done((bf16[8,6144]{1,0:T(8,128)(2,1)S(1)}, bf16[8,6144]{1,0:T(8,128)(2,1)S(1)}, u32[]{:S(2)}, u32[]{:S(2)}) %collective-permute-start.12) | collective-permute-done | bytes 98336 | tf_op jit(solution)/shard_map/ppermute | solution.py:163
  23.7 1.1 %collective-permute-done.6.refs_7_ = bf16[8,6144]{1,0:T(8,128)(2,1)S(1)} collective-permute-done((bf16[8,6144]{1,0:T(8,128)(2,1)S(1)}, bf16[8,6144]{1,0:T(8,128)(2,1)S(1)}, u32[]{:S(2)}, u32[]{:S(2)}) %collective-permute-start.6) | collective-permute-done | bytes 98336 | tf_op jit(solution)/shard_map/ppermute | solution.py:163
  25.5 5.1 %shard_map.65 = (f32[8,6144]{1,0:T(8,128)S(1)}, f32[8,6144]{1,0:T(8,128)S(1)}, f32[8,6144]{1,0:T(8,128)S(1)}, f32[8,6144]{1,0:T(8,128)S(1)}, f32[8,6144]{1,0:T(8...) custom-call(bf16[8,6144]{1,0:T(8,128)(2,1)S(1)} %get-tuple-element.2, ...), custom_call_target="tpu_custom_call" | custom-call | flops 4831838208 | tf_op jit(solution)/shard_map/pallas_call | solution.py:132
  31.6 1.3 %collective-permute-start.22 = (bf16[8,6144]{1,0:T(8,128)(2,1)S(1)}, bf16[8,6144]{1,0:T(8,128)(2,1)S(1)}, u32[]{:S(2)}, u32[]{:S(2)}) collective-permute-start(bf16[8,6144]{1,0:T(8,128)(2,1)S(1)} %convert_element_type.105), channel_id=1, source_target_pairs={{0,4},{4,8},{8,12},{12,14},{14,10},{10,6},{6,2},{2,0},{1,5},{5,9},... | collective-permute-start | bytes 294920 | tf_op jit(solution)/shard_map/ppermute | solution.py:177
  33.7 1.2 %collective-permute-start.15 = (bf16[8,6144]{1,0:T(8,128)(2,1)S(1)}, bf16[8,6144]{1,0:T(8,128)(2,1)S(1)}, u32[]{:S(2)}, u32[]{:S(2)}) collective-permute-start(bf16[8,6144]{1,0:T(8,128)(2,1)S(1)} %convert_element_type.90), channel_id=1, source_target_pairs={{0,4},{4,8},{8,12},{12,14},{14,10},{10,6},{6,2},{2,0},{1,5},{5,9},... | collective-permute-start | bytes 294920 | tf_op jit(solution)/shard_map/ppermute | solution.py:177
  34.9 1.4 %collective-permute-done.25 = bf16[8,6144]{1,0:T(8,128)(2,1)S(1)} collective-permute-done((bf16[8,6144]{1,0:T(8,128)(2,1)S(1)}, bf16[8,6144]{1,0:T(8,128)(2,1)S(1)}, u32[]{:S(2)}, u32[]{:S(2)}) %collective-permute-start.25) | collective-permute-done | bytes 98336 | tf_op jit(solution)/shard_map/ppermute | solution.py:177
  37.2 1.4 %collective-permute-start.23 = (bf16[8,6144]{1,0:T(8,128)(2,1)S(1)}, bf16[8,6144]{1,0:T(8,128)(2,1)S(1)}, u32[]{:S(2)}, u32[]{:S(2)}) collective-permute-start(bf16[8,6144]{1,0:T(8,128)(2,1)S(1)} %add_convert_fusion.5), channel_id=1, source_target_pairs={{0,4},{4,8},{8,12},{12,14},{14,10},{10,6},{6,2},{2,0},{1,5},{5,9},... | collective-permute-start | bytes 294920 | tf_op jit(solution)/shard_map/ppermute | solution.py:177
  39.4 1.4 %collective-permute-start.16 = (bf16[8,6144]{1,0:T(8,128)(2,1)S(1)}, bf16[8,6144]{1,0:T(8,128)(2,1)S(1)}, u32[]{:S(2)}, u32[]{:S(2)}) collective-permute-start(bf16[8,6144]{1,0:T(8,128)(2,1)S(1)} %add_convert_fusion.11), channel_id=1, source_target_pairs={{0,4},{4,8},{8,12},{12,14},{14,10},{10,6},{6,2},{2,0},{1,5},{5,9},... | collective-permute-start | bytes 294920 | tf_op jit(solution)/shard_map/ppermute | solution.py:177
  43.5 1.2 %collective-permute-start.21 = (bf16[8,6144]{1,0:T(8,128)(2,1)S(1)}, bf16[8,6144]{1,0:T(8,128)(2,1)S(1)}, u32[]{:S(2)}, u32[]{:S(2)}) collective-permute-start(bf16[8,6144]{1,0:T(8,128)(2,1)S(1)} %add_convert_fusion.7), channel_id=1, source_target_pairs={{4,0},{8,4},{12,8},{14,12},{10,14},{6,10},{2,6},{0,2},{5,1},{9,5},... | collective-permute-start | bytes 294920 | tf_op jit(solution)/shard_map/ppermute | solution.py:177
  47.0 2.5 %collective-permute-done.17 = bf16[8,6144]{1,0:T(8,128)(2,1)S(1)} collective-permute-done((bf16[8,6144]{1,0:T(8,128)(2,1)S(1)}, bf16[8,6144]{1,0:T(8,128)(2,1)S(1)}, u32[]{:S(2)}, u32[]{:S(2)}) %collective-permute-start.17) | collective-permute-done | bytes 98336 | tf_op jit(solution)/shard_map/ppermute | solution.py:177
  50.8 3.3 %collective-permute-done.18 = bf16[8,6144]{1,0:T(8,128)(2,1)S(1)} collective-permute-done((bf16[8,6144]{1,0:T(8,128)(2,1)S(1)}, bf16[8,6144]{1,0:T(8,128)(2,1)S(1)}, u32[]{:S(2)}, u32[]{:S(2)}) %collective-permute-start.18) | collective-permute-done | bytes 98336 | tf_op jit(solution)/shard_map/ppermute | solution.py:177
  54.2 1.1 %shard_map.66 = bf16[32,6144]{1,0:T(8,128)(2,1)} custom-call(f32[16,32]{1,0:T(8,128)S(1)} %get-tuple-element.24.coefficient, bf16[8,6144]{1,0:T(8,128)(2,1)S(1)} %add_convert_fusion.6.first, bf16[8,6144]{1,0:T(8,128)(2,1)S(1)} %collective-permute-done.29.second), custom_call_target="tpu_custom_call" | custom-call | tf_op jit(solution)/shard_map/pallas_call | solution.py:104
  (61 shorter events, 14.8 us)
Async XLA Ops:
  2.2 6.0 %collective-permute-start = (bf16[8,6144]{1,0:T(8,128)(2,1)S(1)}, bf16[8,6144]{1,0:T(8,128)(2,1)S(1)}, u32[]{:S(2)}, u32[]{:S(2)}) collective-permute-start(bf16[8,6144]{1,0:T(8,128)(2,1)S(1)} %get-tuple-element.25.refs_0_), channel_id=1, source_target_pairs={{0,4},{4,8},{8,12},{12,14},{14,10},{10,6},{6,2},{2,0},{1,5},{5,9},... | collective-permute-start | bytes 294920 | tf_op jit(solution)/shard_map/ppermute | solution.py:163
  4.9 5.6 %collective-permute-start.9 = (bf16[8,6144]{1,0:T(8,128)(2,1)S(1)}, bf16[8,6144]{1,0:T(8,128)(2,1)S(1)}, u32[]{:S(2)}, u32[]{:S(2)}) collective-permute-start(bf16[8,6144]{1,0:T(8,128)(2,1)S(1)} %collective-permute-done.7.refs_8_), channel_id=1, source_target_pairs={{4,0},{8,4},{12,8},{14,12},{10,14},{6,10},{2,6},{0,2},{5,1},{9,5},... | collective-permute-start | bytes 294920 | tf_op jit(solution)/shard_map/ppermute | solution.py:166
  6.0 5.8 %collective-permute-start.1 = (bf16[8,6144]{1,0:T(8,128)(2,1)S(1)}, bf16[8,6144]{1,0:T(8,128)(2,1)S(1)}, u32[]{:S(2)}, u32[]{:S(2)}) collective-permute-start(bf16[8,6144]{1,0:T(8,128)(2,1)S(1)} %get-tuple-element.25.refs_0_), channel_id=1, source_target_pairs={{4,0},{8,4},{12,8},{14,12},{10,14},{6,10},{2,6},{0,2},{5,1},{9,5},... | collective-permute-start | bytes 294920 | tf_op jit(solution)/shard_map/ppermute | solution.py:166
  7.6 5.6 %collective-permute-start.8 = (bf16[8,6144]{1,0:T(8,128)(2,1)S(1)}, bf16[8,6144]{1,0:T(8,128)(2,1)S(1)}, u32[]{:S(2)}, u32[]{:S(2)}) collective-permute-start(bf16[8,6144]{1,0:T(8,128)(2,1)S(1)} %collective-permute-done.7.refs_8_), channel_id=1, source_target_pairs={{0,4},{4,8},{8,12},{12,14},{14,10},{10,6},{6,2},{2,0},{1,5},{5,9},... | collective-permute-start | bytes 294920 | tf_op jit(solution)/shard_map/ppermute | solution.py:163
  8.2 5.8 %collective-permute-start.2 = (bf16[8,6144]{1,0:T(8,128)(2,1)S(1)}, bf16[8,6144]{1,0:T(8,128)(2,1)S(1)}, u32[]{:S(2)}, u32[]{:S(2)}) collective-permute-start(bf16[8,6144]{1,0:T(8,128)(2,1)S(1)} %collective-permute-done.refs_1_), channel_id=1, source_target_pairs={{0,4},{4,8},{8,12},{12,14},{14,10},{10,6},{6,2},{2,0},{1,5},{5,9},... | collective-permute-start | bytes 294920 | tf_op jit(solution)/shard_map/ppermute | solution.py:163
  10.5 5.4 %collective-permute-start.11 = (bf16[8,6144]{1,0:T(8,128)(2,1)S(1)}, bf16[8,6144]{1,0:T(8,128)(2,1)S(1)}, u32[]{:S(2)}, u32[]{:S(2)}) collective-permute-start(bf16[8,6144]{1,0:T(8,128)(2,1)S(1)} %collective-permute-done.9.refs_10_), channel_id=1, source_target_pairs={{4,0},{8,4},{12,8},{14,12},{10,14},{6,10},{2,6},{0,2},{5,1},{9,5},... | collective-permute-start | bytes 294920 | tf_op jit(solution)/shard_map/ppermute | solution.py:166
  11.8 5.4 %collective-permute-start.3 = (bf16[8,6144]{1,0:T(8,128)(2,1)S(1)}, bf16[8,6144]{1,0:T(8,128)(2,1)S(1)}, u32[]{:S(2)}, u32[]{:S(2)}) collective-permute-start(bf16[8,6144]{1,0:T(8,128)(2,1)S(1)} %collective-permute-done.1.refs_2_), channel_id=1, source_target_pairs={{4,0},{8,4},{12,8},{14,12},{10,14},{6,10},{2,6},{0,2},{5,1},{9,5},... | collective-permute-start | bytes 294920 | tf_op jit(solution)/shard_map/ppermute | solution.py:166
  13.3 5.8 %collective-permute-start.10 = (bf16[8,6144]{1,0:T(8,128)(2,1)S(1)}, bf16[8,6144]{1,0:T(8,128)(2,1)S(1)}, u32[]{:S(2)}, u32[]{:S(2)}) collective-permute-start(bf16[8,6144]{1,0:T(8,128)(2,1)S(1)} %collective-permute-done.8.refs_9_), channel_id=1, source_target_pairs={{0,4},{4,8},{8,12},{12,14},{14,10},{10,6},{6,2},{2,0},{1,5},{5,9},... | collective-permute-start | bytes 294920 | tf_op jit(solution)/shard_map/ppermute | solution.py:163
  14.0 5.3 %collective-permute-start.4 = (bf16[8,6144]{1,0:T(8,128)(2,1)S(1)}, bf16[8,6144]{1,0:T(8,128)(2,1)S(1)}, u32[]{:S(2)}, u32[]{:S(2)}) collective-permute-start(bf16[8,6144]{1,0:T(8,128)(2,1)S(1)} %collective-permute-done.2.refs_3_), channel_id=1, source_target_pairs={{0,4},{4,8},{8,12},{12,14},{14,10},{10,6},{6,2},{2,0},{1,5},{5,9},... | collective-permute-start | bytes 294920 | tf_op jit(solution)/shard_map/ppermute | solution.py:163
  15.9 5.0 %collective-permute-start.13 = (bf16[8,6144]{1,0:T(8,128)(2,1)S(1)}, bf16[8,6144]{1,0:T(8,128)(2,1)S(1)}, u32[]{:S(2)}, u32[]{:S(2)}) collective-permute-start(bf16[8,6144]{1,0:T(8,128)(2,1)S(1)} %collective-permute-done.11.refs_12_), channel_id=1, source_target_pairs={{4,0},{8,4},{12,8},{14,12},{10,14},{6,10},{2,6},{0,2},{5,1},{9,5},... | collective-permute-start | bytes 294920 | tf_op jit(solution)/shard_map/ppermute | solution.py:166
  17.3 5.4 %collective-permute-start.5 = (bf16[8,6144]{1,0:T(8,128)(2,1)S(1)}, bf16[8,6144]{1,0:T(8,128)(2,1)S(1)}, u32[]{:S(2)}, u32[]{:S(2)}) collective-permute-start(bf16[8,6144]{1,0:T(8,128)(2,1)S(1)} %collective-permute-done.3.refs_4_), channel_id=1, source_target_pairs={{4,0},{8,4},{12,8},{14,12},{10,14},{6,10},{2,6},{0,2},{5,1},{9,5},... | collective-permute-start | bytes 294920 | tf_op jit(solution)/shard_map/ppermute | solution.py:166
  19.3 5.4 %collective-permute-start.6 = (bf16[8,6144]{1,0:T(8,128)(2,1)S(1)}, bf16[8,6144]{1,0:T(8,128)(2,1)S(1)}, u32[]{:S(2)}, u32[]{:S(2)}) collective-permute-start(bf16[8,6144]{1,0:T(8,128)(2,1)S(1)} %collective-permute-done.4.refs_5_), channel_id=1, source_target_pairs={{0,4},{4,8},{8,12},{12,14},{14,10},{10,6},{6,2},{2,0},{1,5},{5,9},... | collective-permute-start | bytes 294920 | tf_op jit(solution)/shard_map/ppermute | solution.py:163
  30.7 5.6 %collective-permute-start.25 = (bf16[8,6144]{1,0:T(8,128)(2,1)S(1)}, bf16[8,6144]{1,0:T(8,128)(2,1)S(1)}, u32[]{:S(2)}, u32[]{:S(2)}) collective-permute-start(bf16[8,6144]{1,0:T(8,128)(2,1)S(1)} %convert_element_type.111), channel_id=1, source_target_pairs={{4,0},{8,4},{12,8},{14,12},{10,14},{6,10},{2,6},{0,2},{5,1},{9,5},... | collective-permute-start | bytes 294920 | tf_op jit(solution)/shard_map/ppermute | solution.py:177
  31.6 5.6 %collective-permute-start.22 = (bf16[8,6144]{1,0:T(8,128)(2,1)S(1)}, bf16[8,6144]{1,0:T(8,128)(2,1)S(1)}, u32[]{:S(2)}, u32[]{:S(2)}) collective-permute-start(bf16[8,6144]{1,0:T(8,128)(2,1)S(1)} %convert_element_type.105), channel_id=1, source_target_pairs={{0,4},{4,8},{8,12},{12,14},{14,10},{10,6},{6,2},{2,0},{1,5},{5,9},... | collective-permute-start | bytes 294920 | tf_op jit(solution)/shard_map/ppermute | solution.py:177
  32.8 5.7 %collective-permute-start.19 = (bf16[8,6144]{1,0:T(8,128)(2,1)S(1)}, bf16[8,6144]{1,0:T(8,128)(2,1)S(1)}, u32[]{:S(2)}, u32[]{:S(2)}) collective-permute-start(bf16[8,6144]{1,0:T(8,128)(2,1)S(1)} %convert_element_type.98), channel_id=1, source_target_pairs={{4,0},{8,4},{12,8},{14,12},{10,14},{6,10},{2,6},{0,2},{5,1},{9,5},... | collective-permute-start | bytes 294920 | tf_op jit(solution)/shard_map/ppermute | solution.py:177
  33.7 5.7 %collective-permute-start.15 = (bf16[8,6144]{1,0:T(8,128)(2,1)S(1)}, bf16[8,6144]{1,0:T(8,128)(2,1)S(1)}, u32[]{:S(2)}, u32[]{:S(2)}) collective-permute-start(bf16[8,6144]{1,0:T(8,128)(2,1)S(1)} %convert_element_type.90), channel_id=1, source_target_pairs={{0,4},{4,8},{8,12},{12,14},{14,10},{10,6},{6,2},{2,0},{1,5},{5,9},... | collective-permute-start | bytes 294920 | tf_op jit(solution)/shard_map/ppermute | solution.py:177
  36.3 5.1 %collective-permute-start.26 = (bf16[8,6144]{1,0:T(8,128)(2,1)S(1)}, bf16[8,6144]{1,0:T(8,128)(2,1)S(1)}, u32[]{:S(2)}, u32[]{:S(2)}) collective-permute-start(bf16[8,6144]{1,0:T(8,128)(2,1)S(1)} %add_convert_fusion.3), channel_id=1, source_target_pairs={{4,0},{8,4},{12,8},{14,12},{10,14},{6,10},{2,6},{0,2},{5,1},{9,5},... | collective-permute-start | bytes 294920 | tf_op jit(solution)/shard_map/ppermute | solution.py:177
  37.2 5.4 %collective-permute-start.23 = (bf16[8,6144]{1,0:T(8,128)(2,1)S(1)}, bf16[8,6144]{1,0:T(8,128)(2,1)S(1)}, u32[]{:S(2)}, u32[]{:S(2)}) collective-permute-start(bf16[8,6144]{1,0:T(8,128)(2,1)S(1)} %add_convert_fusion.5), channel_id=1, source_target_pairs={{0,4},{4,8},{8,12},{12,14},{14,10},{10,6},{6,2},{2,0},{1,5},{5,9},... | collective-permute-start | bytes 294920 | tf_op jit(solution)/shard_map/ppermute | solution.py:177
  38.6 4.9 %collective-permute-start.20 = (bf16[8,6144]{1,0:T(8,128)(2,1)S(1)}, bf16[8,6144]{1,0:T(8,128)(2,1)S(1)}, u32[]{:S(2)}, u32[]{:S(2)}) collective-permute-start(bf16[8,6144]{1,0:T(8,128)(2,1)S(1)} %add_convert_fusion.8), channel_id=1, source_target_pairs={{4,0},{8,4},{12,8},{14,12},{10,14},{6,10},{2,6},{0,2},{5,1},{9,5},... | collective-permute-start | bytes 294920 | tf_op jit(solution)/shard_map/ppermute | solution.py:177
  39.4 5.4 %collective-permute-start.16 = (bf16[8,6144]{1,0:T(8,128)(2,1)S(1)}, bf16[8,6144]{1,0:T(8,128)(2,1)S(1)}, u32[]{:S(2)}, u32[]{:S(2)}) collective-permute-start(bf16[8,6144]{1,0:T(8,128)(2,1)S(1)} %add_convert_fusion.11), channel_id=1, source_target_pairs={{0,4},{4,8},{8,12},{12,14},{14,10},{10,6},{6,2},{2,0},{1,5},{5,9},... | collective-permute-start | bytes 294920 | tf_op jit(solution)/shard_map/ppermute | solution.py:177
  42.6 7.8 %collective-permute-start.24 = (bf16[8,6144]{1,0:T(8,128)(2,1)S(1)}, bf16[8,6144]{1,0:T(8,128)(2,1)S(1)}, u32[]{:S(2)}, u32[]{:S(2)}) collective-permute-start(bf16[8,6144]{1,0:T(8,128)(2,1)S(1)} %add_convert_fusion.4), channel_id=1, source_target_pairs={{0,4},{4,8},{8,12},{12,14},{14,10},{10,6},{6,2},{2,0},{1,5},{5,9},... | collective-permute-start | bytes 294920 | tf_op jit(solution)/shard_map/ppermute | solution.py:177
  43.5 7.3 %collective-permute-start.21 = (bf16[8,6144]{1,0:T(8,128)(2,1)S(1)}, bf16[8,6144]{1,0:T(8,128)(2,1)S(1)}, u32[]{:S(2)}, u32[]{:S(2)}) collective-permute-start(bf16[8,6144]{1,0:T(8,128)(2,1)S(1)} %add_convert_fusion.7), channel_id=1, source_target_pairs={{4,0},{8,4},{12,8},{14,12},{10,14},{6,10},{2,6},{0,2},{5,1},{9,5},... | collective-permute-start | bytes 294920 | tf_op jit(solution)/shard_map/ppermute | solution.py:177
  44.8 4.7 %collective-permute-start.17 = (bf16[8,6144]{1,0:T(8,128)(2,1)S(1)}, bf16[8,6144]{1,0:T(8,128)(2,1)S(1)}, u32[]{:S(2)}, u32[]{:S(2)}) collective-permute-start(bf16[8,6144]{1,0:T(8,128)(2,1)S(1)} %add_convert_fusion.10), channel_id=1, source_target_pairs={{0,4},{4,8},{8,12},{12,14},{14,10},{10,6},{6,2},{2,0},{1,5},{5,9},... | collective-permute-start | bytes 294920 | tf_op jit(solution)/shard_map/ppermute | solution.py:177
  46.0 4.7 %collective-permute-start.28 = (bf16[8,6144]{1,0:T(8,128)(2,1)S(1)}, bf16[8,6144]{1,0:T(8,128)(2,1)S(1)}, u32[]{:S(2)}, u32[]{:S(2)}) collective-permute-start(bf16[8,6144]{1,0:T(8,128)(2,1)S(1)} %add_convert_fusion.1), channel_id=1, source_target_pairs={{4,0},{8,4},{12,8},{14,12},{10,14},{6,10},{2,6},{0,2},{5,1},{9,5},... | collective-permute-start | bytes 294920 | tf_op jit(solution)/shard_map/ppermute | solution.py:177
  (9 other events, 101.6 us)

commit v4 on v3

--- a/solution.py
+++ b/solution.py
@@ -42,26 +42,26 @@
         copy.start()
     for copy in copies:
         copy.wait()
-    rows_here = tokens.shape[0]
-    capacity = mine.shape[0]
-    earlier = (
-        lax.broadcasted_iota(jnp.int32, (rows_here, rows_here), 0)
-        < lax.broadcasted_iota(jnp.int32, (rows_here, rows_here), 1)
-    ).astype(jnp.float32)
-    slots = lax.broadcasted_iota(jnp.int32, (capacity, rows_here), 0).astype(jnp.float32)
-    for side, rows in enumerate((mine, theirs)):
-        expert = own[0] if side == 0 else 1 - own[0]
-        matches = ids[...] == expert
-        picked = jnp.sum(matches.astype(jnp.float32), axis=0, keepdims=True)
-        weight = jnp.sum(jnp.where(matches, gates[...], 0.0), axis=0, keepdims=True)
-        slot = jnp.dot(
-            jnp.broadcast_to(picked, (capacity, rows_here)), earlier, preferred_element_type=jnp.float32
-        )
-        onehot = jnp.where((picked > 0.0) & (slot == slots), 1.0, 0.0)
-        rows[...] = jnp.dot(
-            onehot.astype(jnp.bfloat16), tokens[...], preferred_element_type=jnp.float32
-        ).astype(rows.dtype)
-        coefficient[side * capacity : (side + 1) * capacity, :] = onehot * weight
+    rows_here, capacity = tokens.shape[0], mine.shape[0]
+    place = lax.broadcasted_iota(jnp.int32, (2 * capacity, rows_here), 0)
+    expert = jnp.where(place < capacity, own[0], 1 - own[0])
+    slots = jnp.where(place < capacity, place, place - capacity).astype(jnp.float32)
+    earlier = lax.broadcasted_iota(jnp.int32, (rows_here, rows_here), 0) < lax.broadcasted_iota(
+        jnp.int32, (rows_here, rows_here), 1
+    )
+    matches = [ids[k : k + 1, :] == expert for k in range(ids.shape[0])]
+    picked = functools.reduce(jnp.logical_or, matches)
+    weight = sum(jnp.where(match, gates[k : k + 1, :], 0.0) for k, match in enumerate(matches))
+    slot = jnp.dot(
+        picked.astype(jnp.float32).astype(jnp.bfloat16),
+        earlier.astype(jnp.float32).astype(jnp.bfloat16),
+        preferred_element_type=jnp.float32,
+    )
+    onehot = jnp.where(picked & (slot == slots), 1.0, 0.0)
+    rows = jnp.dot(onehot.astype(jnp.bfloat16), tokens[...], preferred_element_type=jnp.float32)
+    mine[...] = rows[:capacity].astype(mine.dtype)
+    theirs[...] = rows[capacity:].astype(theirs.dtype)
+    coefficient[...] = onehot * weight
 
 
 def route(own, ids, gates, tokens):
@@ -84,30 +84,60 @@
     )(own, *[pltpu.with_memory_space_constraint(a, pltpu.HBM) for a in (ids, gates, tokens)])
 
 
-def combine_kernel(coefficient, first, second, out):
+def presum_kernel(counts, *refs):
+    parts, outs = refs[:-2], refs[-2:]
+    for group, out in zip((parts[: counts[0]], parts[counts[0] :]), outs):
+        total = group[0][...].astype(jnp.float32)
+        for part in group[1:]:
+            total = total + part[...].astype(jnp.float32)
+        out[...] = total
+
+
+def presum(own, other):
+    in_vmem = pl.BlockSpec(memory_space=pltpu.VMEM)
+    parts = [pltpu.with_memory_space_constraint(part, pltpu.VMEM) for part in (*own, *other)]
+    return pl.pallas_call(
+        functools.partial(presum_kernel, (len(own), len(other))),
+        out_shape=[pltpu.VMEM(own[0].shape, jnp.float32)] * 2,
+        in_specs=[in_vmem] * len(parts),
+        out_specs=[in_vmem] * 2,
+        compiler_params=pltpu.CompilerParams(vmem_limit_bytes=4 * 1024 * 1024),
+        cost_estimate=pl.CostEstimate(flops=4_000_000_000, bytes_accessed=0, transcendentals=0),
+    )(*parts)
+
+
+def combine_kernel(counts, coefficient, *refs):
+    (*parts, out) = refs
     left = coefficient[...]
     high = left.astype(jnp.bfloat16)
     rest = left - high.astype(jnp.float32)
     middle = rest.astype(jnp.bfloat16)
     low = (rest - middle.astype(jnp.float32)).astype(jnp.bfloat16)
     split = jnp.concatenate([high, middle, low], axis=0)
-    pair = jnp.concatenate([first[...], second[...]], axis=0)
+    sums = []
+    for group in (parts[: counts[0]], parts[counts[0] :]):
+        total = group[0][...].astype(jnp.float32)
+        for part in group[1:]:
+            total = total + part[...].astype(jnp.float32)
+        sums.append(total.astype(jnp.bfloat16))
+    pair = jnp.concatenate(sums, axis=0)
     rows = jnp.concatenate([pair, pair, pair], axis=0)
     out[...] = lax.dot_general(
         split, rows, (((0,), (0,)), ((), ())), preferred_element_type=jnp.float32
     ).astype(out.dtype)
 
 
-def combine(coefficient, first, second):
-    rows_here, width = coefficient.shape[1], first.shape[1]
-    in_vmem = pl.BlockSpec(memory_space=pltpu.VMEM)
+def combine(coefficient, own, other):
+    rows_here, width = coefficient.shape[1], own[0].shape[1]
+    in_vmem = pl.BlockSpec(memory_space=pltpu.VMEM)
+    parts = [pltpu.with_memory_space_constraint(part, pltpu.VMEM) for part in (*own, *other)]
     return pl.pallas_call(
-        combine_kernel,
-        out_shape=jax.ShapeDtypeStruct((rows_here, width), first.dtype),
-        in_specs=[in_vmem] * 3,
+        functools.partial(combine_kernel, (len(own), len(other))),
+        out_shape=jax.ShapeDtypeStruct((rows_here, width), jnp.bfloat16),
+        in_specs=[in_vmem] * (1 + len(parts)),
         out_specs=in_vmem,
-        compiler_params=pltpu.CompilerParams(vmem_limit_bytes=4 * 1024 * 1024),
-    )(coefficient, first, second)
+        compiler_params=pltpu.CompilerParams(vmem_limit_bytes=6 * 1024 * 1024),
+    )(coefficient, *parts)
 
 
 def feed_forward_kernel(count, capacity, *refs):
@@ -150,55 +180,59 @@
 
 def make_per_device(ring):
     count = len(ring)
-    forward = [(ring[i], ring[(i + 1) % count]) for i in range(count)]
-    backward = [(b, a) for a, b in forward]
+    near, opposite = (count - 1) // 2, count // 2
+    hop, cross = {}, {}
+    for way in (1, -1):
+        links = [(ring[i], ring[(i + way) % count]) for i in range(count)]
+        hop[way] = [(2 * a + core, 2 * b + core) for a, b in links for core in (0, 1)]
+        cross[way] = [(2 * a + core, 2 * b + 1 - core) for a, b in links for core in (0, 1)]
     swap = [(0, 1), (1, 0)]
-    longer, shorter = count // 2, (count - 1) // 2
-
-    def gather(block, forward_steps, backward_steps):
-        held = {0: block}
-        ahead = behind = block
-        for step in range(1, max(forward_steps, backward_steps) + 1):
-            if step <= forward_steps:
-                behind = lax.ppermute(behind, "tensor", forward)
-                held[-step] = behind
-            if step <= backward_steps:
-                ahead = lax.ppermute(ahead, "tensor", backward)
-                held[step] = ahead
+    steps = [(chain, -way * step, way) for step in range(1, near + 1) for chain in (0, 1) for way in (1, -1)]
+    if count % 2 == 0:
+        steps += [(0, -opposite, 1), (1, opposite, -1)]
+
+    def send(block, perm):
+        return lax.ppermute(block, ("tensor", "expert"), perm)
+
+    def gather(mine, theirs):
+        held = ({0: mine}, {0: lax.ppermute(theirs, "expert", swap)})
+        for chain, place, way in steps:
+            if place + way:
+                held[chain][place] = send(held[chain][place + way], hop[way])
+            elif chain:
+                held[chain][place] = send(theirs, cross[way])
+            else:
+                held[chain][place] = send(mine, hop[way])
         return held
 
-    def scatter_sum(terms, forward_steps, backward_steps):
-        def flow(steps, sign, perm):
-            running = None
-            for step in range(steps, 0, -1):
-                distance = sign * step
-                term = terms[distance] if distance in terms else terms[distance - sign * count]
-                total = term.astype(jnp.float32) + (0 if running is None else running.astype(jnp.float32))
-                running = lax.ppermute(total.astype(jnp.bfloat16), "tensor", perm)
-            return running
-
-        total = terms[0].astype(jnp.float32)
-        for part in (flow(forward_steps, 1, forward), flow(backward_steps, -1, backward)):
-            if part is not None:
-                total = total + part.astype(jnp.float32)
-        return total
+    def scatter(terms):
+        arrived = ({}, {})
+        other = lax.ppermute(terms[1][0].astype(jnp.bfloat16), "expert", swap)
+        for chain, place, way in reversed(steps):
+            place, far = -place, abs(place) == opposite and count % 2 == 0
+            term = terms[chain][-place if far else place].astype(jnp.float32)
+            parts = arrived[chain].pop(place, ())
+            for part in parts:
+                term = term + part.astype(jnp.float32)
+            term = term.astype(jnp.bfloat16)
+            last = place == way
+            got = send(term, cross[way] if last and chain else hop[way])
+            arrived[chain].setdefault(place - way, []).append(got)
+        late = [arrived[chain].get(0, [None])[(-1, 0)[chain]] for chain in (0, 1)]
+        soon = [[part for part in arrived[chain].get(0, ()) if part is not late[chain]] for chain in (0, 1)]
+        return presum([terms[0][0], *soon[0]], [other, *soon[1]]), late
 
     def per_device(tokens, expert_ids, gates, w_gate, w_up, w_down):
         own = lax.axis_index("expert").astype(jnp.int32).reshape(1)
         mine, theirs, coefficient = route(own, expert_ids.T, gates.T, tokens)
-        sibling = lax.ppermute(theirs, "expert", swap)
-        held_a = gather(mine, longer, shorter)
-        held_b = gather(sibling, shorter, longer)
-        keys = [("a", k) for k in held_a] + [("b", k) for k in held_b]
-        blocks = list(held_a.values()) + list(held_b.values())
-        parts = feed_forward(blocks, w_gate[0], w_up[0], w_down[0])
-        terms = {"a": {}, "b": {}}
-        for (chain, distance), part in zip(keys, parts):
-            terms[chain][distance] = part
-        sum_b = scatter_sum(terms["b"], shorter, longer)
-        other = lax.ppermute(sum_b.astype(jnp.bfloat16), "expert", swap)
-        sum_a = scatter_sum(terms["a"], longer, shorter).astype(jnp.bfloat16)
-        return combine(coefficient, sum_a, other)
+        held = gather(mine, theirs)
+        places = [(chain, place) for chain in (0, 1) for place in held[chain]]
+        parts = feed_forward([held[c][p] for c, p in places], w_gate[0], w_up[0], w_down[0])
+        terms = ({}, {})
+        for (chain, place), part in zip(places, parts):
+            terms[chain][place] = part
+        (first, second), late = scatter(terms)
+        return combine(coefficient, [p for p in (first, late[0]) if p is not None], [p for p in (second, late[1]) if p is not None])
 
     return per_device
 

time: 55.4 us -> 53.7 us (0.969)
  starting transfers between devices: 32.8 us -> 28.7 us
  waiting for transfers between devices: 14.1 us -> 16.7 us
    ppermute x30, starting transfers between devices: 32.8 us -> 28.7 us  [the longest x28 28.6 us: send(): return lax.ppermute(block, ('tensor', 'expert'), perm)]
    ppermute x30, waiting for transfers between devices: 14.1 us -> 16.7 us  [the longest x28 16.7 us: send(): return lax.ppermute(block, ('tensor', 'expert'), perm)]
  transfers between devices with their start and end apart: 30 -> 30, of which waited for: 17 -> 19; matrix products, arithmetic and copies ran while one was open for 1% -> 0% of each run, Pallas kernels for 0% -> 0%
where the time goes in v4:
time: 53.7 us; the launch traced here: 53.5 us
  starting transfers between devices  28.7 us (53%)
  waiting for transfers between devices  16.7 us (31%)
  Pallas kernels  7.74 us (14%)
    ppermute x28, starting transfers between devices, send(): return lax.ppermute(block, ('tensor', 'expert'), perm)  28.6 us
    ppermute x28, waiting for transfers between devices, send(): return lax.ppermute(block, ('tensor', 'expert'), perm)  16.7 us
    pallas_call x1, Pallas kernels, feed_forward(): pl.pallas_call(functools.partial(feed_forward_kernel, count, capacity), o...  5.14 us
    pallas_call x1, Pallas kernels, route(): pl.pallas_call(route_kernel, out_shape=[pltpu.VMEM((capacity, width), tok...  1.51 us
  transfers between devices with their start and end apart: 30, of which 19 were waited for; matrix products, arithmetic and copies ran while one was open for 0% of the time, Pallas kernels for 0%

profile of v4, /device:TPU:0, one launch (start us, length us, event | category | flops | bytes accessed | tf_op | source)
XLA Modules:
  0.0 53.5 jit_solution(2321264836873310545)
XLA Ops:
  0.0 1.5 %shard_map.64 = (bf16[8,6144]{1,0:T(8,128)(2,1)S(1)}, bf16[8,6144]{1,0:T(8,128)(2,1)S(1)}, f32[16,32]{1,0:T(8,128)S(1)}) custom-call(s32[1]{0:T(128)} %bitcast.own, s32[2,32]{1,0:T(2,128)} %bitcast.9, f32[2,32]{1,0:T(2,128)} %bitcast.10, bf16[32,6144]{1,0:T(8,128)(2,1)} %refs_2_.1), custom_call_target="tpu_custom_call" | custom-call | flops 30000001024 | tf_op jit(solution)/shard_map/pallas_call | solution.py:71
  1.5 3.1 %collective-permute-start = (bf16[8,6144]{1,0:T(8,128)(2,1)S(1)}, bf16[8,6144]{1,0:T(8,128)(2,1)S(1)}, u32[]{:S(2)}, u32[]{:S(2)}) collective-permute-start(bf16[8,6144]{1,0:T(8,128)(2,1)S(1)} %get-tuple-element.27.refs_0_), channel_id=1, source_target_pairs={{0,4},{1,5},{4,8},{5,9},{8,12},{9,13},{12,14},{13,15},{14,10},{15,... | collective-permute-start | bytes 294920 | tf_op jit(solution)/shard_map/ppermute | solution.py:195
  4.6 1.1 %collective-permute-start.1 = (bf16[8,6144]{1,0:T(8,128)(2,1)S(1)}, bf16[8,6144]{1,0:T(8,128)(2,1)S(1)}, u32[]{:S(2)}, u32[]{:S(2)}) collective-permute-start(bf16[8,6144]{1,0:T(8,128)(2,1)S(1)} %get-tuple-element.27.refs_0_), channel_id=1, source_target_pairs={{0,2},{1,3},{4,0},{5,1},{8,4},{9,5},{12,8},{13,9},{14,12},{15,13},... | collective-permute-start | bytes 294920 | tf_op jit(solution)/shard_map/ppermute | solution.py:195
  6.4 1.0 %collective-permute-done.refs_1_ = bf16[8,6144]{1,0:T(8,128)(2,1)S(1)} collective-permute-done((bf16[8,6144]{1,0:T(8,128)(2,1)S(1)}, bf16[8,6144]{1,0:T(8,128)(2,1)S(1)}, u32[]{:S(2)}, u32[]{:S(2)}) %collective-permute-start) | collective-permute-done | bytes 98336 | tf_op jit(solution)/shard_map/ppermute | solution.py:195
  7.3 1.9 %collective-permute-start.2 = (bf16[8,6144]{1,0:T(8,128)(2,1)S(1)}, bf16[8,6144]{1,0:T(8,128)(2,1)S(1)}, u32[]{:S(2)}, u32[]{:S(2)}) collective-permute-start(bf16[8,6144]{1,0:T(8,128)(2,1)S(1)} %collective-permute-done.refs_1_), channel_id=1, source_target_pairs={{0,4},{1,5},{4,8},{5,9},{8,12},{9,13},{12,14},{13,15},{14,10},{15,... | collective-permute-start | bytes 294920 | tf_op jit(solution)/shard_map/ppermute | solution.py:195
  9.6 2.2 %collective-permute-done.1.refs_2_ = bf16[8,6144]{1,0:T(8,128)(2,1)S(1)} collective-permute-done((bf16[8,6144]{1,0:T(8,128)(2,1)S(1)}, bf16[8,6144]{1,0:T(8,128)(2,1)S(1)}, u32[]{:S(2)}, u32[]{:S(2)}) %collective-permute-start.1) | collective-permute-done | bytes 98336 | tf_op jit(solution)/shard_map/ppermute | solution.py:195
  11.8 2.0 %collective-permute-start.10 = (bf16[8,6144]{1,0:T(8,128)(2,1)S(1)}, bf16[8,6144]{1,0:T(8,128)(2,1)S(1)}, u32[]{:S(2)}, u32[]{:S(2)}) collective-permute-start(bf16[8,6144]{1,0:T(8,128)(2,1)S(1)} %collective-permute-done.8.refs_9_), channel_id=1, source_target_pairs={{0,4},{1,5},{4,8},{5,9},{8,12},{9,13},{12,14},{13,15},{14,10},{15,... | collective-permute-start | bytes 294920 | tf_op jit(solution)/shard_map/ppermute | solution.py:195
  13.8 1.6 %collective-permute-start.4 = (bf16[8,6144]{1,0:T(8,128)(2,1)S(1)}, bf16[8,6144]{1,0:T(8,128)(2,1)S(1)}, u32[]{:S(2)}, u32[]{:S(2)}) collective-permute-start(bf16[8,6144]{1,0:T(8,128)(2,1)S(1)} %collective-permute-done.2.refs_3_), channel_id=1, source_target_pairs={{0,4},{1,5},{4,8},{5,9},{8,12},{9,13},{12,14},{13,15},{14,10},{15,... | collective-permute-start | bytes 294920 | tf_op jit(solution)/shard_map/ppermute | solution.py:195
  17.2 2.3 %collective-permute-start.12 = (bf16[8,6144]{1,0:T(8,128)(2,1)S(1)}, bf16[8,6144]{1,0:T(8,128)(2,1)S(1)}, u32[]{:S(2)}, u32[]{:S(2)}) collective-permute-start(bf16[8,6144]{1,0:T(8,128)(2,1)S(1)} %collective-permute-done.10.refs_11_), channel_id=1, source_target_pairs={{0,4},{1,5},{4,8},{5,9},{8,12},{9,13},{12,14},{13,15},{14,10},{15,... | collective-permute-start | bytes 294920 | tf_op jit(solution)/shard_map/ppermute | solution.py:195
  19.5 1.5 %collective-permute-start.6 = (bf16[8,6144]{1,0:T(8,128)(2,1)S(1)}, bf16[8,6144]{1,0:T(8,128)(2,1)S(1)}, u32[]{:S(2)}, u32[]{:S(2)}) collective-permute-start(bf16[8,6144]{1,0:T(8,128)(2,1)S(1)} %collective-permute-done.4.refs_5_), channel_id=1, source_target_pairs={{0,4},{1,5},{4,8},{5,9},{8,12},{9,13},{12,14},{13,15},{14,10},{15,... | collective-permute-start | bytes 294920 | tf_op jit(solution)/shard_map/ppermute | solution.py:195
  22.6 1.4 %collective-permute-done.6.refs_7_ = bf16[8,6144]{1,0:T(8,128)(2,1)S(1)} collective-permute-done((bf16[8,6144]{1,0:T(8,128)(2,1)S(1)}, bf16[8,6144]{1,0:T(8,128)(2,1)S(1)}, u32[]{:S(2)}, u32[]{:S(2)}) %collective-permute-start.6) | collective-permute-done | bytes 98336 | tf_op jit(solution)/shard_map/ppermute | solution.py:195
  24.1 1.6 %collective-permute-done.14.refs_15_ = bf16[8,6144]{1,0:T(8,128)(2,1)S(1)} collective-permute-done((bf16[8,6144]{1,0:T(8,128)(2,1)S(1)}, bf16[8,6144]{1,0:T(8,128)(2,1)S(1)}, u32[]{:S(2)}, u32[]{:S(2)}) %collective-permute-start.14) | collective-permute-done | bytes 98336 | tf_op jit(solution)/shard_map/ppermute | solution.py:195
  25.7 5.1 %shard_map.65 = (f32[8,6144]{1,0:T(8,128)S(1)}, f32[8,6144]{1,0:T(8,128)S(1)}, f32[8,6144]{1,0:T(8,128)S(1)}, f32[8,6144]{1,0:T(8,128)S(1)}, f32[8,6144]{1,0:T(8...) custom-call(bf16[8,6144]{1,0:T(8,128)(2,1)S(1)} %get-tuple-element.2, ...), custom_call_target="tpu_custom_call" | custom-call | flops 4831838208 | tf_op jit(solution)/shard_map/pallas_call | solution.py:162
  31.4 1.7 %collective-permute-start.22 = (bf16[8,6144]{1,0:T(8,128)(2,1)S(1)}, bf16[8,6144]{1,0:T(8,128)(2,1)S(1)}, u32[]{:S(2)}, u32[]{:S(2)}) collective-permute-start(bf16[8,6144]{1,0:T(8,128)(2,1)S(1)} %convert_element_type.86), channel_id=1, source_target_pairs={{0,4},{1,5},{4,8},{5,9},{8,12},{9,13},{12,14},{13,15},{14,10},{15,... | collective-permute-start | bytes 294920 | tf_op jit(solution)/shard_map/ppermute | solution.py:195
  33.1 1.6 %collective-permute-start.19 = (bf16[8,6144]{1,0:T(8,128)(2,1)S(1)}, bf16[8,6144]{1,0:T(8,128)(2,1)S(1)}, u32[]{:S(2)}, u32[]{:S(2)}) collective-permute-start(bf16[8,6144]{1,0:T(8,128)(2,1)S(1)} %convert_element_type.81), channel_id=1, source_target_pairs={{0,4},{1,5},{4,8},{5,9},{8,12},{9,13},{12,14},{13,15},{14,10},{15,... | collective-permute-start | bytes 294920 | tf_op jit(solution)/shard_map/ppermute | solution.py:195
  36.1 1.7 %collective-permute-start.23 = (bf16[8,6144]{1,0:T(8,128)(2,1)S(1)}, bf16[8,6144]{1,0:T(8,128)(2,1)S(1)}, u32[]{:S(2)}, u32[]{:S(2)}) collective-permute-start(bf16[8,6144]{1,0:T(8,128)(2,1)S(1)} %add_convert_fusion.5), channel_id=1, source_target_pairs={{0,4},{1,5},{4,8},{5,9},{8,12},{9,13},{12,14},{13,15},{14,10},{15,... | collective-permute-start | bytes 294920 | tf_op jit(solution)/shard_map/ppermute | solution.py:195
  37.8 1.6 %collective-permute-start.20 = (bf16[8,6144]{1,0:T(8,128)(2,1)S(1)}, bf16[8,6144]{1,0:T(8,128)(2,1)S(1)}, u32[]{:S(2)}, u32[]{:S(2)}) collective-permute-start(bf16[8,6144]{1,0:T(8,128)(2,1)S(1)} %add_convert_fusion.7), channel_id=1, source_target_pairs={{0,4},{1,5},{4,8},{5,9},{8,12},{9,13},{12,14},{13,15},{14,10},{15,... | collective-permute-start | bytes 294920 | tf_op jit(solution)/shard_map/ppermute | solution.py:195
  40.8 1.2 %collective-permute-done.27 = bf16[8,6144]{1,0:T(8,128)(2,1)S(1)} collective-permute-done((bf16[8,6144]{1,0:T(8,128)(2,1)S(1)}, bf16[8,6144]{1,0:T(8,128)(2,1)S(1)}, u32[]{:S(2)}, u32[]{:S(2)}) %collective-permute-start.27) | collective-permute-done | bytes 98336 | tf_op jit(solution)/shard_map/ppermute | solution.py:195
  42.5 1.6 %collective-permute-start.24 = (bf16[8,6144]{1,0:T(8,128)(2,1)S(1)}, bf16[8,6144]{1,0:T(8,128)(2,1)S(1)}, u32[]{:S(2)}, u32[]{:S(2)}) collective-permute-start(bf16[8,6144]{1,0:T(8,128)(2,1)S(1)} %add_convert_fusion.4), channel_id=1, source_target_pairs={{0,4},{1,5},{4,8},{5,9},{8,12},{9,13},{12,14},{13,15},{14,10},{15,... | collective-permute-start | bytes 294920 | tf_op jit(solution)/shard_map/ppermute | solution.py:195
  44.3 1.3 %collective-permute-done.16 = bf16[8,6144]{1,0:T(8,128)(2,1)S(1)} collective-permute-done((bf16[8,6144]{1,0:T(8,128)(2,1)S(1)}, bf16[8,6144]{1,0:T(8,128)(2,1)S(1)}, u32[]{:S(2)}, u32[]{:S(2)}) %collective-permute-start.16) | collective-permute-done | bytes 98336 | tf_op jit(solution)/shard_map/ppermute | solution.py:195
  47.2 2.2 %collective-permute-start.25 = (bf16[8,6144]{1,0:T(8,128)(2,1)S(1)}, bf16[8,6144]{1,0:T(8,128)(2,1)S(1)}, u32[]{:S(2)}, u32[]{:S(2)}) collective-permute-start(bf16[8,6144]{1,0:T(8,128)(2,1)S(1)} %add_convert_fusion.3), channel_id=1, source_target_pairs={{0,4},{1,5},{4,8},{5,9},{8,12},{9,13},{12,14},{13,15},{14,10},{15,... | collective-permute-start | bytes 294920 | tf_op jit(solution)/shard_map/ppermute | solution.py:195
  49.5 1.0 %collective-permute-done.17.refs_1_ = bf16[8,6144]{1,0:T(8,128)(2,1)S(1)} collective-permute-done((bf16[8,6144]{1,0:T(8,128)(2,1)S(1)}, bf16[8,6144]{1,0:T(8,128)(2,1)S(1)}, u32[]{:S(2)}, u32[]{:S(2)}) %collective-permute-start.17) | collective-permute-done | bytes 98336 | tf_op jit(solution)/shard_map/ppermute | solution.py:195
  50.5 1.7 %collective-permute-done.29.refs_3_ = bf16[8,6144]{1,0:T(8,128)(2,1)S(1)} collective-permute-done((bf16[8,6144]{1,0:T(8,128)(2,1)S(1)}, bf16[8,6144]{1,0:T(8,128)(2,1)S(1)}, u32[]{:S(2)}, u32[]{:S(2)}) %collective-permute-start.29) | collective-permute-done | bytes 98336 | tf_op jit(solution)/shard_map/ppermute | solution.py:195
  52.5 1.1 %shard_map.67 = bf16[32,6144]{1,0:T(8,128)(2,1)} custom-call(f32[16,32]{1,0:T(8,128)S(1)} %get-tuple-element.26.coefficient, f32[8,6144]{1,0:T(8,128)S(1)} %get-tuple-element.37.refs_0_, bf16[8,6144]{1,0:T(8,128)(2,1)S(1)} %collective-permute-done.25.refs_1_, f32[8,6144]{1,0:T(8,128)S(1)} %get-tuple-element.42.refs_2_, ...), custom_call_target="tpu_custom_call" | custom-call | tf_op jit(solution)/shard_map/pallas_call | solution.py:134
  (61 shorter events, 10.3 us)
Async XLA Ops:
  1.5 5.8 %collective-permute-start = (bf16[8,6144]{1,0:T(8,128)(2,1)S(1)}, bf16[8,6144]{1,0:T(8,128)(2,1)S(1)}, u32[]{:S(2)}, u32[]{:S(2)}) collective-permute-start(bf16[8,6144]{1,0:T(8,128)(2,1)S(1)} %get-tuple-element.27.refs_0_), channel_id=1, source_target_pairs={{0,4},{1,5},{4,8},{5,9},{8,12},{9,13},{12,14},{13,15},{14,10},{15,... | collective-permute-start | bytes 294920 | tf_op jit(solution)/shard_map/ppermute | solution.py:195
  4.6 5.0 %collective-permute-start.9 = (bf16[8,6144]{1,0:T(8,128)(2,1)S(1)}, bf16[8,6144]{1,0:T(8,128)(2,1)S(1)}, u32[]{:S(2)}, u32[]{:S(2)}) collective-permute-start(bf16[8,6144]{1,0:T(8,128)(2,1)S(1)} %get-tuple-element.28), channel_id=1, source_target_pairs={{0,3},{1,2},{4,1},{5,0},{8,5},{9,4},{12,9},{13,8},{14,13},{15,12},... | collective-permute-start | bytes 294920 | tf_op jit(solution)/shard_map/ppermute | solution.py:195
  4.6 7.2 %collective-permute-start.1 = (bf16[8,6144]{1,0:T(8,128)(2,1)S(1)}, bf16[8,6144]{1,0:T(8,128)(2,1)S(1)}, u32[]{:S(2)}, u32[]{:S(2)}) collective-permute-start(bf16[8,6144]{1,0:T(8,128)(2,1)S(1)} %get-tuple-element.27.refs_0_), channel_id=1, source_target_pairs={{0,2},{1,3},{4,0},{5,1},{8,4},{9,5},{12,8},{13,9},{14,12},{15,13},... | collective-permute-start | bytes 294920 | tf_op jit(solution)/shard_map/ppermute | solution.py:195
  5.7 6.1 %collective-permute-start.8 = (bf16[8,6144]{1,0:T(8,128)(2,1)S(1)}, bf16[8,6144]{1,0:T(8,128)(2,1)S(1)}, u32[]{:S(2)}, u32[]{:S(2)}) collective-permute-start(bf16[8,6144]{1,0:T(8,128)(2,1)S(1)} %get-tuple-element.28), channel_id=1, source_target_pairs={{0,5},{1,4},{4,9},{5,8},{8,13},{9,12},{12,15},{13,14},{14,11},{15,... | collective-permute-start | bytes 294920 | tf_op jit(solution)/shard_map/ppermute | solution.py:195
  7.3 6.5 %collective-permute-start.2 = (bf16[8,6144]{1,0:T(8,128)(2,1)S(1)}, bf16[8,6144]{1,0:T(8,128)(2,1)S(1)}, u32[]{:S(2)}, u32[]{:S(2)}) collective-permute-start(bf16[8,6144]{1,0:T(8,128)(2,1)S(1)} %collective-permute-done.refs_1_), channel_id=1, source_target_pairs={{0,4},{1,5},{4,8},{5,9},{8,12},{9,13},{12,14},{13,15},{14,10},{15,... | collective-permute-start | bytes 294920 | tf_op jit(solution)/shard_map/ppermute | solution.py:195
  9.6 5.9 %collective-permute-start.11 = (bf16[8,6144]{1,0:T(8,128)(2,1)S(1)}, bf16[8,6144]{1,0:T(8,128)(2,1)S(1)}, u32[]{:S(2)}, u32[]{:S(2)}) collective-permute-start(bf16[8,6144]{1,0:T(8,128)(2,1)S(1)} %collective-permute-done.9.refs_10_), channel_id=1, source_target_pairs={{0,2},{1,3},{4,0},{5,1},{8,4},{9,5},{12,8},{13,9},{14,12},{15,13},... | collective-permute-start | bytes 294920 | tf_op jit(solution)/shard_map/ppermute | solution.py:195
  11.8 4.9 %collective-permute-start.3 = (bf16[8,6144]{1,0:T(8,128)(2,1)S(1)}, bf16[8,6144]{1,0:T(8,128)(2,1)S(1)}, u32[]{:S(2)}, u32[]{:S(2)}) collective-permute-start(bf16[8,6144]{1,0:T(8,128)(2,1)S(1)} %collective-permute-done.1.refs_2_), channel_id=1, source_target_pairs={{0,2},{1,3},{4,0},{5,1},{8,4},{9,5},{12,8},{13,9},{14,12},{15,13},... | collective-permute-start | bytes 294920 | tf_op jit(solution)/shard_map/ppermute | solution.py:195
  11.8 5.4 %collective-permute-start.10 = (bf16[8,6144]{1,0:T(8,128)(2,1)S(1)}, bf16[8,6144]{1,0:T(8,128)(2,1)S(1)}, u32[]{:S(2)}, u32[]{:S(2)}) collective-permute-start(bf16[8,6144]{1,0:T(8,128)(2,1)S(1)} %collective-permute-done.8.refs_9_), channel_id=1, source_target_pairs={{0,4},{1,5},{4,8},{5,9},{8,12},{9,13},{12,14},{13,15},{14,10},{15,... | collective-permute-start | bytes 294920 | tf_op jit(solution)/shard_map/ppermute | solution.py:195
  13.8 5.6 %collective-permute-start.4 = (bf16[8,6144]{1,0:T(8,128)(2,1)S(1)}, bf16[8,6144]{1,0:T(8,128)(2,1)S(1)}, u32[]{:S(2)}, u32[]{:S(2)}) collective-permute-start(bf16[8,6144]{1,0:T(8,128)(2,1)S(1)} %collective-permute-done.2.refs_3_), channel_id=1, source_target_pairs={{0,4},{1,5},{4,8},{5,9},{8,12},{9,13},{12,14},{13,15},{14,10},{15,... | collective-permute-start | bytes 294920 | tf_op jit(solution)/shard_map/ppermute | solution.py:195
  15.4 5.7 %collective-permute-start.13 = (bf16[8,6144]{1,0:T(8,128)(2,1)S(1)}, bf16[8,6144]{1,0:T(8,128)(2,1)S(1)}, u32[]{:S(2)}, u32[]{:S(2)}) collective-permute-start(bf16[8,6144]{1,0:T(8,128)(2,1)S(1)} %collective-permute-done.11.refs_12_), channel_id=1, source_target_pairs={{0,2},{1,3},{4,0},{5,1},{8,4},{9,5},{12,8},{13,9},{14,12},{15,13},... | collective-permute-start | bytes 294920 | tf_op jit(solution)/shard_map/ppermute | solution.py:195
  15.9 5.6 %collective-permute-start.7 = (bf16[8,6144]{1,0:T(8,128)(2,1)S(1)}, bf16[8,6144]{1,0:T(8,128)(2,1)S(1)}, u32[]{:S(2)}, u32[]{:S(2)}) collective-permute-start(bf16[8,6144]{1,0:T(8,128)(2,1)S(1)} %get-tuple-element.28), channel_id=1, source_target_pairs={{0,1},{1,0},{2,3},{3,2},{4,5},{5,4},{6,7},{7,6},{8,9},{9,8},{10,11... | collective-permute-start | bytes 294920 | tf_op jit(solution)/shard_map/ppermute | solution.py:198
  16.7 5.5 %collective-permute-start.5 = (bf16[8,6144]{1,0:T(8,128)(2,1)S(1)}, bf16[8,6144]{1,0:T(8,128)(2,1)S(1)}, u32[]{:S(2)}, u32[]{:S(2)}) collective-permute-start(bf16[8,6144]{1,0:T(8,128)(2,1)S(1)} %collective-permute-done.3.refs_4_), channel_id=1, source_target_pairs={{0,2},{1,3},{4,0},{5,1},{8,4},{9,5},{12,8},{13,9},{14,12},{15,13},... | collective-permute-start | bytes 294920 | tf_op jit(solution)/shard_map/ppermute | solution.py:195
  17.2 5.4 %collective-permute-start.12 = (bf16[8,6144]{1,0:T(8,128)(2,1)S(1)}, bf16[8,6144]{1,0:T(8,128)(2,1)S(1)}, u32[]{:S(2)}, u32[]{:S(2)}) collective-permute-start(bf16[8,6144]{1,0:T(8,128)(2,1)S(1)} %collective-permute-done.10.refs_11_), channel_id=1, source_target_pairs={{0,4},{1,5},{4,8},{5,9},{8,12},{9,13},{12,14},{13,15},{14,10},{15,... | collective-permute-start | bytes 294920 | tf_op jit(solution)/shard_map/ppermute | solution.py:195
  34.7 14.8 %collective-permute-start.18 = (bf16[8,6144]{1,0:T(8,128)(2,1)S(1)}, bf16[8,6144]{1,0:T(8,128)(2,1)S(1)}, u32[]{:S(2)}, u32[]{:S(2)}) collective-permute-start(bf16[8,6144]{1,0:T(8,128)(2,1)S(1)} %convert_element_type.80), channel_id=1, source_target_pairs={{0,1},{1,0},{2,3},{3,2},{4,5},{5,4},{6,7},{7,6},{8,9},{9,8},{10,11... | collective-permute-start | bytes 294920 | tf_op jit(solution)/shard_map/ppermute | solution.py:210
  34.7 5.6 %collective-permute-start.15 = (bf16[8,6144]{1,0:T(8,128)(2,1)S(1)}, bf16[8,6144]{1,0:T(8,128)(2,1)S(1)}, u32[]{:S(2)}, u32[]{:S(2)}) collective-permute-start(bf16[8,6144]{1,0:T(8,128)(2,1)S(1)} %convert_element_type.75), channel_id=1, source_target_pairs={{0,2},{1,3},{4,0},{5,1},{8,4},{9,5},{12,8},{13,9},{14,12},{15,13},... | collective-permute-start | bytes 294920 | tf_op jit(solution)/shard_map/ppermute | solution.py:195
  35.6 6.4 %collective-permute-start.27 = (bf16[8,6144]{1,0:T(8,128)(2,1)S(1)}, bf16[8,6144]{1,0:T(8,128)(2,1)S(1)}, u32[]{:S(2)}, u32[]{:S(2)}) collective-permute-start(bf16[8,6144]{1,0:T(8,128)(2,1)S(1)} %add_convert_fusion.2), channel_id=1, source_target_pairs={{0,2},{1,3},{4,0},{5,1},{8,4},{9,5},{12,8},{13,9},{14,12},{15,13},... | collective-permute-start | bytes 294920 | tf_op jit(solution)/shard_map/ppermute | solution.py:195
  36.1 6.4 %collective-permute-start.23 = (bf16[8,6144]{1,0:T(8,128)(2,1)S(1)}, bf16[8,6144]{1,0:T(8,128)(2,1)S(1)}, u32[]{:S(2)}, u32[]{:S(2)}) collective-permute-start(bf16[8,6144]{1,0:T(8,128)(2,1)S(1)} %add_convert_fusion.5), channel_id=1, source_target_pairs={{0,4},{1,5},{4,8},{5,9},{8,12},{9,13},{12,14},{13,15},{14,10},{15,... | collective-permute-start | bytes 294920 | tf_op jit(solution)/shard_map/ppermute | solution.py:195
  37.8 6.4 %collective-permute-start.20 = (bf16[8,6144]{1,0:T(8,128)(2,1)S(1)}, bf16[8,6144]{1,0:T(8,128)(2,1)S(1)}, u32[]{:S(2)}, u32[]{:S(2)}) collective-permute-start(bf16[8,6144]{1,0:T(8,128)(2,1)S(1)} %add_convert_fusion.7), channel_id=1, source_target_pairs={{0,4},{1,5},{4,8},{5,9},{8,12},{9,13},{12,14},{13,15},{14,10},{15,... | collective-permute-start | bytes 294920 | tf_op jit(solution)/shard_map/ppermute | solution.py:195
  40.3 5.3 %collective-permute-start.16 = (bf16[8,6144]{1,0:T(8,128)(2,1)S(1)}, bf16[8,6144]{1,0:T(8,128)(2,1)S(1)}, u32[]{:S(2)}, u32[]{:S(2)}) collective-permute-start(bf16[8,6144]{1,0:T(8,128)(2,1)S(1)} %add_convert_fusion.9), channel_id=1, source_target_pairs={{0,2},{1,3},{4,0},{5,1},{8,4},{9,5},{12,8},{13,9},{14,12},{15,13},... | collective-permute-start | bytes 294920 | tf_op jit(solution)/shard_map/ppermute | solution.py:195
  42.0 5.1 %collective-permute-start.28 = (bf16[8,6144]{1,0:T(8,128)(2,1)S(1)}, bf16[8,6144]{1,0:T(8,128)(2,1)S(1)}, u32[]{:S(2)}, u32[]{:S(2)}) collective-permute-start(bf16[8,6144]{1,0:T(8,128)(2,1)S(1)} %add_convert_fusion.1), channel_id=1, source_target_pairs={{0,2},{1,3},{4,0},{5,1},{8,4},{9,5},{12,8},{13,9},{14,12},{15,13},... | collective-permute-start | bytes 294920 | tf_op jit(solution)/shard_map/ppermute | solution.py:195
  44.2 5.3 %collective-permute-start.21 = (bf16[8,6144]{1,0:T(8,128)(2,1)S(1)}, bf16[8,6144]{1,0:T(8,128)(2,1)S(1)}, u32[]{:S(2)}, u32[]{:S(2)}) collective-permute-start(bf16[8,6144]{1,0:T(8,128)(2,1)S(1)} %add_convert_fusion.6), channel_id=1, source_target_pairs={{0,5},{1,4},{4,9},{5,8},{8,13},{9,12},{12,15},{13,14},{14,11},{15,... | collective-permute-start | bytes 294920 | tf_op jit(solution)/shard_map/ppermute | solution.py:195
  45.6 4.8 %collective-permute-start.17 = (bf16[8,6144]{1,0:T(8,128)(2,1)S(1)}, bf16[8,6144]{1,0:T(8,128)(2,1)S(1)}, u32[]{:S(2)}, u32[]{:S(2)}) collective-permute-start(bf16[8,6144]{1,0:T(8,128)(2,1)S(1)} %add_convert_fusion.8), channel_id=1, source_target_pairs={{0,2},{1,3},{4,0},{5,1},{8,4},{9,5},{12,8},{13,9},{14,12},{15,13},... | collective-permute-start | bytes 294920 | tf_op jit(solution)/shard_map/ppermute | solution.py:195
  47.1 5.1 %collective-permute-start.29 = (bf16[8,6144]{1,0:T(8,128)(2,1)S(1)}, bf16[8,6144]{1,0:T(8,128)(2,1)S(1)}, u32[]{:S(2)}, u32[]{:S(2)}) collective-permute-start(bf16[8,6144]{1,0:T(8,128)(2,1)S(1)} %add_convert_fusion), channel_id=1, source_target_pairs={{0,3},{1,2},{4,1},{5,0},{8,5},{9,4},{12,9},{13,8},{14,13},{15,12},... | collective-permute-start | bytes 294920 | tf_op jit(solution)/shard_map/ppermute | solution.py:195
  47.2 5.3 %collective-permute-start.25 = (bf16[8,6144]{1,0:T(8,128)(2,1)S(1)}, bf16[8,6144]{1,0:T(8,128)(2,1)S(1)}, u32[]{:S(2)}, u32[]{:S(2)}) collective-permute-start(bf16[8,6144]{1,0:T(8,128)(2,1)S(1)} %add_convert_fusion.3), channel_id=1, source_target_pairs={{0,4},{1,5},{4,8},{5,9},{8,12},{9,13},{12,14},{13,15},{14,10},{15,... | collective-permute-start | bytes 294920 | tf_op jit(solution)/shard_map/ppermute | solution.py:195
  (9 other events, 105.1 us)

commit v5 on v4

--- a/solution.py
+++ b/solution.py
@@ -31,17 +31,27 @@
     return up + down
 
 
-def route_kernel(own, *refs):
-    sources, (mine, theirs, coefficient) = refs[:3], refs[3:6]
-    (ids, gates, tokens), arrived = refs[6:9], refs[9]
-    copies = [
-        pltpu.make_async_copy(source, target, arrived.at[i])
-        for i, (source, target) in enumerate(zip(sources, (ids, gates, tokens)))
-    ]
+def fetch_kernel(*refs):
+    count = (len(refs) - 1) // 2
+    copies = [pltpu.make_async_copy(refs[i], refs[count + i], refs[-1].at[i]) for i in range(count)]
     for copy in copies:
         copy.start()
     for copy in copies:
         copy.wait()
+
+
+def fetch(*arrays):
+    return pl.pallas_call(
+        fetch_kernel,
+        out_shape=[pltpu.VMEM(a.shape, a.dtype) for a in arrays],
+        in_specs=[pl.BlockSpec(memory_space=pl.ANY)] * len(arrays),
+        out_specs=[pl.BlockSpec(memory_space=pltpu.VMEM)] * len(arrays),
+        scratch_shapes=[pltpu.SemaphoreType.DMA((len(arrays),))],
+        compiler_params=pltpu.CompilerParams(vmem_limit_bytes=4 * 1024 * 1024),
+    )(*[pltpu.with_memory_space_constraint(a, pltpu.HBM) for a in arrays])
+
+
+def route_kernel(own, ids, gates, tokens, mine, theirs, coefficient):
     rows_here, capacity = tokens.shape[0], mine.shape[0]
     place = lax.broadcasted_iota(jnp.int32, (2 * capacity, rows_here), 0)
     expert = jnp.where(place < capacity, own[0], 1 - own[0])
@@ -75,13 +85,11 @@
             pltpu.VMEM((capacity, width), tokens.dtype),
             pltpu.VMEM((2 * capacity, rows_here), jnp.float32),
         ],
-        in_specs=[pl.BlockSpec(memory_space=pltpu.SMEM)] + [pl.BlockSpec(memory_space=pl.ANY)] * 3,
+        in_specs=[pl.BlockSpec(memory_space=pltpu.SMEM)] + [in_vmem] * 3,
         out_specs=[in_vmem] * 3,
-        scratch_shapes=[pltpu.VMEM(a.shape, a.dtype) for a in (ids, gates, tokens)]
-        + [pltpu.SemaphoreType.DMA((3,))],
         compiler_params=pltpu.CompilerParams(vmem_limit_bytes=4 * 1024 * 1024),
         cost_estimate=pl.CostEstimate(flops=30_000_000_000, bytes_accessed=0, transcendentals=0),
-    )(own, *[pltpu.with_memory_space_constraint(a, pltpu.HBM) for a in (ids, gates, tokens)])
+    )(own, *[pltpu.with_memory_space_constraint(a, pltpu.VMEM) for a in fetch(ids, gates, tokens)])
 
 
 def presum_kernel(counts, *refs):
@@ -181,46 +189,46 @@
 def make_per_device(ring):
     count = len(ring)
     near, opposite = (count - 1) // 2, count // 2
-    hop, cross = {}, {}
-    for way in (1, -1):
-        links = [(ring[i], ring[(i + way) % count]) for i in range(count)]
-        hop[way] = [(2 * a + core, 2 * b + core) for a, b in links for core in (0, 1)]
-        cross[way] = [(2 * a + core, 2 * b + 1 - core) for a, b in links for core in (0, 1)]
     swap = [(0, 1), (1, 0)]
+    long = (1, -1)
     steps = [(chain, -way * step, way) for step in range(1, near + 1) for chain in (0, 1) for way in (1, -1)]
     if count % 2 == 0:
-        steps += [(0, -opposite, 1), (1, opposite, -1)]
-
-    def send(block, perm):
+        steps += [(chain, -long[chain] * opposite, long[chain]) for chain in (0, 1)]
+
+    def send(block, hops, crossing=False):
+        perm = [
+            (2 * ring[i] + core, 2 * ring[(i + hops) % count] + (1 - core if crossing else core))
+            for i in range(count)
+            for core in (0, 1)
+        ]
         return lax.ppermute(block, ("tensor", "expert"), perm)
 
     def gather(mine, theirs):
         held = ({0: mine}, {0: lax.ppermute(theirs, "expert", swap)})
         for chain, place, way in steps:
+            if abs(place) == opposite and near and count % 2 == 0:
+                held[chain][place] = send(held[chain][place + 2 * way], 2 * way)
+            elif place + way:
+                held[chain][place] = send(held[chain][place + way], way)
+            else:
+                held[chain][place] = send(theirs if chain else mine, way, crossing=chain == 1)
+        return held
+
+    def scatter(terms):
+        arrived, early, last = {}, ([], []), [None, None]
+        for chain, place, way in reversed(steps):
+            term = terms[chain][place if abs(place) == opposite and count % 2 == 0 else -place].astype(jnp.float32)
+            if (chain, place, way) in arrived:
+                term = term + arrived[chain, place, way].astype(jnp.float32)
+            got = send(term.astype(jnp.bfloat16), way, crossing=chain == 1 and place + way == 0)
             if place + way:
-                held[chain][place] = send(held[chain][place + way], hop[way])
-            elif chain:
-                held[chain][place] = send(theirs, cross[way])
+                arrived[chain, place + way, way] = got
+            elif way == long[chain]:
+                last[chain] = got
             else:
-                held[chain][place] = send(mine, hop[way])
-        return held
-
-    def scatter(terms):
-        arrived = ({}, {})
+                early[chain].append(got)
         other = lax.ppermute(terms[1][0].astype(jnp.bfloat16), "expert", swap)
-        for chain, place, way in reversed(steps):
-            place, far = -place, abs(place) == opposite and count % 2 == 0
-            term = terms[chain][-place if far else place].astype(jnp.float32)
-            parts = arrived[chain].pop(place, ())
-            for part in parts:
-                term = term + part.astype(jnp.float32)
-            term = term.astype(jnp.bfloat16)
-            last = place == way
-            got = send(term, cross[way] if last and chain else hop[way])
-            arrived[chain].setdefault(place - way, []).append(got)
-        late = [arrived[chain].get(0, [None])[(-1, 0)[chain]] for chain in (0, 1)]
-        soon = [[part for part in arrived[chain].get(0, ()) if part is not late[chain]] for chain in (0, 1)]
-        return presum([terms[0][0], *soon[0]], [other, *soon[1]]), late
+        return presum([terms[0][0], *early[0]], [other, *early[1]]), last
 
     def per_device(tokens, expert_ids, gates, w_gate, w_up, w_down):
         own = lax.axis_index("expert").astype(jnp.int32).reshape(1)
@@ -231,8 +239,9 @@
         terms = ({}, {})
         for (chain, place), part in zip(places, parts):
             terms[chain][place] = part
-        (first, second), late = scatter(terms)
-        return combine(coefficient, [p for p in (first, late[0]) if p is not None], [p for p in (second, late[1]) if p is not None])
+        sums, last = scatter(terms)
+        own, other = ([first] if late is None else [first, late] for first, late in zip(sums, last))
+        return combine(coefficient, own, other)
 
     return per_device
 

time: 53.7 us -> 53.4 us (level)
    pallas_call x1, Pallas kernels: 1.51 us -> 0.3 us  [route(): pl.pallas_call(route_kernel, out_shape=[pltpu.VMEM((capacity, width), tok...]
    pallas_call x0 -> x1, Pallas kernels: none -> 1.05 us  [fetch(): pl.pallas_call(fetch_kernel, out_shape=[pltpu.VMEM(a.shape, a.dtype) for...]
    ppermute x28, waiting for transfers between devices: 16.7 us -> 16.1 us  [send(): return lax.ppermute(block, ('tensor', 'expert'), perm)]
  transfers between devices with their start and end apart: 30 -> 30, of which waited for: 19 -> 18; matrix products, arithmetic and copies ran while one was open for 0% -> 0% of each run, Pallas kernels for 0% -> 0%
where the time goes in v5:
time: 53.4 us; the launch traced here: 53.2 us
  starting transfers between devices  29 us (54%)
  waiting for transfers between devices  16.2 us (30%)
  Pallas kernels  7.58 us (14%)
    ppermute x28, starting transfers between devices, send(): return lax.ppermute(block, ('tensor', 'expert'), perm)  29 us
    ppermute x28, waiting for transfers between devices, send(): return lax.ppermute(block, ('tensor', 'expert'), perm)  16.1 us
    pallas_call x1, Pallas kernels, feed_forward(): pl.pallas_call(functools.partial(feed_forward_kernel, count, capacity), o...  5.14 us
  transfers between devices with their start and end apart: 30, of which 18 were waited for; matrix products, arithmetic and copies ran while one was open for 0% of the time, Pallas kernels for 0%

profile of v5, /device:TPU:0, one launch (start us, length us, event | category | flops | bytes accessed | tf_op | source)
XLA Modules:
  0.0 53.2 jit_solution(2257372565002542013)
XLA Ops:
  0.0 1.1 %shard_map.64 = (s32[2,32]{1,0:T(2,128)S(1)}, f32[2,32]{1,0:T(2,128)S(1)}, bf16[32,6144]{1,0:T(8,128)(2,1)S(1)}) custom-call(s32[2,32]{1,0:T(2,128)} %bitcast.9, f32[2,32]{1,0:T(2,128)} %bitcast.10, bf16[32,6144]{1,0:T(8,128)(2,1)} %refs_2_.1), custom_call_target="tpu_custom_call" | custom-call | tf_op jit(solution)/shard_map/pallas_call | solution.py:44
  1.4 3.0 %collective-permute-start.1 = (bf16[8,6144]{1,0:T(8,128)(2,1)S(1)}, bf16[8,6144]{1,0:T(8,128)(2,1)S(1)}, u32[]{:S(2)}, u32[]{:S(2)}) collective-permute-start(bf16[8,6144]{1,0:T(8,128)(2,1)S(1)} %get-tuple-element.33.refs_0_), channel_id=1, source_target_pairs={{0,2},{1,3},{4,0},{5,1},{8,4},{9,5},{12,8},{13,9},{14,12},{15,13},... | collective-permute-start | bytes 294920 | tf_op jit(solution)/shard_map/ppermute | solution.py:204
  5.3 1.0 %collective-permute-start.8 = (bf16[8,6144]{1,0:T(8,128)(2,1)S(1)}, bf16[8,6144]{1,0:T(8,128)(2,1)S(1)}, u32[]{:S(2)}, u32[]{:S(2)}) collective-permute-start(bf16[8,6144]{1,0:T(8,128)(2,1)S(1)} %get-tuple-element.34), channel_id=1, source_target_pairs={{0,5},{1,4},{4,9},{5,8},{8,13},{9,12},{12,15},{13,14},{14,11},{15,... | collective-permute-start | bytes 294920 | tf_op jit(solution)/shard_map/ppermute | solution.py:204
  6.3 1.0 %collective-permute-done.1.refs_2_ = bf16[8,6144]{1,0:T(8,128)(2,1)S(1)} collective-permute-done((bf16[8,6144]{1,0:T(8,128)(2,1)S(1)}, bf16[8,6144]{1,0:T(8,128)(2,1)S(1)}, u32[]{:S(2)}, u32[]{:S(2)}) %collective-permute-start.1) | collective-permute-done | bytes 98336 | tf_op jit(solution)/shard_map/ppermute | solution.py:204
  7.3 1.8 %collective-permute-start.3 = (bf16[8,6144]{1,0:T(8,128)(2,1)S(1)}, bf16[8,6144]{1,0:T(8,128)(2,1)S(1)}, u32[]{:S(2)}, u32[]{:S(2)}) collective-permute-start(bf16[8,6144]{1,0:T(8,128)(2,1)S(1)} %collective-permute-done.1.refs_2_), channel_id=1, source_target_pairs={{0,2},{1,3},{4,0},{5,1},{8,4},{9,5},{12,8},{13,9},{14,12},{15,13},... | collective-permute-start | bytes 294920 | tf_op jit(solution)/shard_map/ppermute | solution.py:204
  9.3 1.8 %collective-permute-start.11 = (bf16[8,6144]{1,0:T(8,128)(2,1)S(1)}, bf16[8,6144]{1,0:T(8,128)(2,1)S(1)}, u32[]{:S(2)}, u32[]{:S(2)}) collective-permute-start(bf16[8,6144]{1,0:T(8,128)(2,1)S(1)} %collective-permute-done.9.refs_10_), channel_id=1, source_target_pairs={{0,2},{1,3},{4,0},{5,1},{8,4},{9,5},{12,8},{13,9},{14,12},{15,13},... | collective-permute-start | bytes 294920 | tf_op jit(solution)/shard_map/ppermute | solution.py:204
  11.9 1.8 %collective-permute-start.5 = (bf16[8,6144]{1,0:T(8,128)(2,1)S(1)}, bf16[8,6144]{1,0:T(8,128)(2,1)S(1)}, u32[]{:S(2)}, u32[]{:S(2)}) collective-permute-start(bf16[8,6144]{1,0:T(8,128)(2,1)S(1)} %collective-permute-done.3.refs_4_), channel_id=1, source_target_pairs={{0,2},{1,3},{4,0},{5,1},{8,4},{9,5},{12,8},{13,9},{14,12},{15,13},... | collective-permute-start | bytes 294920 | tf_op jit(solution)/shard_map/ppermute | solution.py:204
  13.7 1.5 %collective-permute-start.6 = (bf16[8,6144]{1,0:T(8,128)(2,1)S(1)}, bf16[8,6144]{1,0:T(8,128)(2,1)S(1)}, u32[]{:S(2)}, u32[]{:S(2)}) collective-permute-start(bf16[8,6144]{1,0:T(8,128)(2,1)S(1)} %collective-permute-done.2.refs_3_), channel_id=1, source_target_pairs={{0,8},{1,9},{4,12},{5,13},{8,14},{9,15},{12,10},{13,11},{14,6},{15... | collective-permute-start | bytes 294920 | tf_op jit(solution)/shard_map/ppermute | solution.py:204
  15.2 1.6 %collective-permute-start.4 = (bf16[8,6144]{1,0:T(8,128)(2,1)S(1)}, bf16[8,6144]{1,0:T(8,128)(2,1)S(1)}, u32[]{:S(2)}, u32[]{:S(2)}) collective-permute-start(bf16[8,6144]{1,0:T(8,128)(2,1)S(1)} %collective-permute-done.2.refs_3_), channel_id=1, source_target_pairs={{0,4},{1,5},{4,8},{5,9},{8,12},{9,13},{12,14},{13,15},{14,10},{15,... | collective-permute-start | bytes 294920 | tf_op jit(solution)/shard_map/ppermute | solution.py:204
  17.3 2.1 %collective-permute-start.13 = (bf16[8,6144]{1,0:T(8,128)(2,1)S(1)}, bf16[8,6144]{1,0:T(8,128)(2,1)S(1)}, u32[]{:S(2)}, u32[]{:S(2)}) collective-permute-start(bf16[8,6144]{1,0:T(8,128)(2,1)S(1)} %collective-permute-done.11.refs_12_), channel_id=1, source_target_pairs={{0,2},{1,3},{4,0},{5,1},{8,4},{9,5},{12,8},{13,9},{14,12},{15,13},... | collective-permute-start | bytes 294920 | tf_op jit(solution)/shard_map/ppermute | solution.py:204
  19.4 2.3 %collective-permute-done.6.refs_7_ = bf16[8,6144]{1,0:T(8,128)(2,1)S(1)} collective-permute-done((bf16[8,6144]{1,0:T(8,128)(2,1)S(1)}, bf16[8,6144]{1,0:T(8,128)(2,1)S(1)}, u32[]{:S(2)}, u32[]{:S(2)}) %collective-permute-start.6) | collective-permute-done | bytes 98336 | tf_op jit(solution)/shard_map/ppermute | solution.py:204
  21.7 2.5 %collective-permute-done.14.refs_15_ = bf16[8,6144]{1,0:T(8,128)(2,1)S(1)} collective-permute-done((bf16[8,6144]{1,0:T(8,128)(2,1)S(1)}, bf16[8,6144]{1,0:T(8,128)(2,1)S(1)}, u32[]{:S(2)}, u32[]{:S(2)}) %collective-permute-start.14) | collective-permute-done | bytes 98336 | tf_op jit(solution)/shard_map/ppermute | solution.py:204
  24.6 5.1 %shard_map.66 = (f32[8,6144]{1,0:T(8,128)S(1)}, f32[8,6144]{1,0:T(8,128)S(1)}, f32[8,6144]{1,0:T(8,128)S(1)}, f32[8,6144]{1,0:T(8,128)S(1)}, f32[8,6144]{1,0:T(8...) custom-call(bf16[8,6144]{1,0:T(8,128)(2,1)S(1)} %get-tuple-element.3, ...), custom_call_target="tpu_custom_call" | custom-call | flops 4831838208 | tf_op jit(solution)/shard_map/pallas_call | solution.py:170
  29.8 2.0 %collective-permute-start.26 = (bf16[8,6144]{1,0:T(8,128)(2,1)S(1)}, bf16[8,6144]{1,0:T(8,128)(2,1)S(1)}, u32[]{:S(2)}, u32[]{:S(2)}) collective-permute-start(bf16[8,6144]{1,0:T(8,128)(2,1)S(1)} %convert_element_type.93), channel_id=1, source_target_pairs={{0,2},{1,3},{4,0},{5,1},{8,4},{9,5},{12,8},{13,9},{14,12},{15,13},... | collective-permute-start | bytes 294920 | tf_op jit(solution)/shard_map/ppermute | solution.py:204
  32.0 1.7 %collective-permute-start.19 = (bf16[8,6144]{1,0:T(8,128)(2,1)S(1)}, bf16[8,6144]{1,0:T(8,128)(2,1)S(1)}, u32[]{:S(2)}, u32[]{:S(2)}) collective-permute-start(bf16[8,6144]{1,0:T(8,128)(2,1)S(1)} %convert_element_type.81), channel_id=1, source_target_pairs={{0,4},{1,5},{4,8},{5,9},{8,12},{9,13},{12,14},{13,15},{14,10},{15,... | collective-permute-start | bytes 294920 | tf_op jit(solution)/shard_map/ppermute | solution.py:204
  34.5 2.0 %collective-permute-start.27 = (bf16[8,6144]{1,0:T(8,128)(2,1)S(1)}, bf16[8,6144]{1,0:T(8,128)(2,1)S(1)}, u32[]{:S(2)}, u32[]{:S(2)}) collective-permute-start(bf16[8,6144]{1,0:T(8,128)(2,1)S(1)} %add_convert_fusion.2), channel_id=1, source_target_pairs={{0,2},{1,3},{4,0},{5,1},{8,4},{9,5},{12,8},{13,9},{14,12},{15,13},... | collective-permute-start | bytes 294920 | tf_op jit(solution)/shard_map/ppermute | solution.py:204
  40.1 0.9 %collective-permute-done.27 = bf16[8,6144]{1,0:T(8,128)(2,1)S(1)} collective-permute-done((bf16[8,6144]{1,0:T(8,128)(2,1)S(1)}, bf16[8,6144]{1,0:T(8,128)(2,1)S(1)}, u32[]{:S(2)}, u32[]{:S(2)}) %collective-permute-start.27) | collective-permute-done | bytes 98336 | tf_op jit(solution)/shard_map/ppermute | solution.py:204
  41.9 1.3 %collective-permute-start.24 = (bf16[8,6144]{1,0:T(8,128)(2,1)S(1)}, bf16[8,6144]{1,0:T(8,128)(2,1)S(1)}, u32[]{:S(2)}, u32[]{:S(2)}) collective-permute-start(bf16[8,6144]{1,0:T(8,128)(2,1)S(1)} %add_convert_fusion.4), channel_id=1, source_target_pairs={{0,4},{1,5},{4,8},{5,9},{8,12},{9,13},{12,14},{13,15},{14,10},{15,... | collective-permute-start | bytes 294920 | tf_op jit(solution)/shard_map/ppermute | solution.py:204
  43.7 1.0 %collective-permute-done.16 = bf16[8,6144]{1,0:T(8,128)(2,1)S(1)} collective-permute-done((bf16[8,6144]{1,0:T(8,128)(2,1)S(1)}, bf16[8,6144]{1,0:T(8,128)(2,1)S(1)}, u32[]{:S(2)}, u32[]{:S(2)}) %collective-permute-start.16) | collective-permute-done | bytes 98336 | tf_op jit(solution)/shard_map/ppermute | solution.py:204
  44.7 1.2 %collective-permute-start.17 = (bf16[8,6144]{1,0:T(8,128)(2,1)S(1)}, bf16[8,6144]{1,0:T(8,128)(2,1)S(1)}, u32[]{:S(2)}, u32[]{:S(2)}) collective-permute-start(bf16[8,6144]{1,0:T(8,128)(2,1)S(1)} %add_convert_fusion.8), channel_id=1, source_target_pairs={{0,2},{1,3},{4,0},{5,1},{8,4},{9,5},{12,8},{13,9},{14,12},{15,13},... | collective-permute-start | bytes 294920 | tf_op jit(solution)/shard_map/ppermute | solution.py:204
  47.0 0.9 %collective-permute-start.25 = (bf16[8,6144]{1,0:T(8,128)(2,1)S(1)}, bf16[8,6144]{1,0:T(8,128)(2,1)S(1)}, u32[]{:S(2)}, u32[]{:S(2)}) collective-permute-start(bf16[8,6144]{1,0:T(8,128)(2,1)S(1)} %add_convert_fusion.3), channel_id=1, source_target_pairs={{0,4},{1,5},{4,8},{5,9},{8,12},{9,13},{12,14},{13,15},{14,10},{15,... | collective-permute-start | bytes 294920 | tf_op jit(solution)/shard_map/ppermute | solution.py:204
  48.3 2.0 %collective-permute-done.17.refs_1_ = bf16[8,6144]{1,0:T(8,128)(2,1)S(1)} collective-permute-done((bf16[8,6144]{1,0:T(8,128)(2,1)S(1)}, bf16[8,6144]{1,0:T(8,128)(2,1)S(1)}, u32[]{:S(2)}, u32[]{:S(2)}) %collective-permute-start.17) | collective-permute-done | bytes 98336 | tf_op jit(solution)/shard_map/ppermute | solution.py:204
  50.4 1.0 %collective-permute-done.29.refs_3_ = bf16[8,6144]{1,0:T(8,128)(2,1)S(1)} collective-permute-done((bf16[8,6144]{1,0:T(8,128)(2,1)S(1)}, bf16[8,6144]{1,0:T(8,128)(2,1)S(1)}, u32[]{:S(2)}, u32[]{:S(2)}) %collective-permute-start.29) | collective-permute-done | bytes 98336 | tf_op jit(solution)/shard_map/ppermute | solution.py:204
  52.2 1.0 %shard_map.68 = bf16[32,6144]{1,0:T(8,128)(2,1)} custom-call(f32[16,32]{1,0:T(8,128)S(1)} %get-tuple-element.32.coefficient, f32[8,6144]{1,0:T(8,128)S(1)} %get-tuple-element.43.refs_0_, bf16[8,6144]{1,0:T(8,128)(2,1)S(1)} %collective-permute-done.25.refs_1_, f32[8,6144]{1,0:T(8,128)S(1)} %get-tuple-element.48.refs_2_, ...), custom_call_target="tpu_custom_call" | custom-call | tf_op jit(solution)/shard_map/pallas_call | solution.py:142
  (62 shorter events, 11.5 us)
Async XLA Ops:
  1.4 5.9 %collective-permute-start.1 = (bf16[8,6144]{1,0:T(8,128)(2,1)S(1)}, bf16[8,6144]{1,0:T(8,128)(2,1)S(1)}, u32[]{:S(2)}, u32[]{:S(2)}) collective-permute-start(bf16[8,6144]{1,0:T(8,128)(2,1)S(1)} %get-tuple-element.33.refs_0_), channel_id=1, source_target_pairs={{0,2},{1,3},{4,0},{5,1},{8,4},{9,5},{12,8},{13,9},{14,12},{15,13},... | collective-permute-start | bytes 294920 | tf_op jit(solution)/shard_map/ppermute | solution.py:204
  5.3 5.8 %collective-permute-start.8 = (bf16[8,6144]{1,0:T(8,128)(2,1)S(1)}, bf16[8,6144]{1,0:T(8,128)(2,1)S(1)}, u32[]{:S(2)}, u32[]{:S(2)}) collective-permute-start(bf16[8,6144]{1,0:T(8,128)(2,1)S(1)} %get-tuple-element.34), channel_id=1, source_target_pairs={{0,5},{1,4},{4,9},{5,8},{8,13},{9,12},{12,15},{13,14},{14,11},{15,... | collective-permute-start | bytes 294920 | tf_op jit(solution)/shard_map/ppermute | solution.py:204
  9.3 5.9 %collective-permute-start.7 = (bf16[8,6144]{1,0:T(8,128)(2,1)S(1)}, bf16[8,6144]{1,0:T(8,128)(2,1)S(1)}, u32[]{:S(2)}, u32[]{:S(2)}) collective-permute-start(bf16[8,6144]{1,0:T(8,128)(2,1)S(1)} %get-tuple-element.34), channel_id=1, source_target_pairs={{0,1},{1,0},{2,3},{3,2},{4,5},{5,4},{6,7},{7,6},{8,9},{9,8},{10,11... | collective-permute-start | bytes 294920 | tf_op jit(solution)/shard_map/ppermute | solution.py:207
  9.3 7.5 %collective-permute-start.11 = (bf16[8,6144]{1,0:T(8,128)(2,1)S(1)}, bf16[8,6144]{1,0:T(8,128)(2,1)S(1)}, u32[]{:S(2)}, u32[]{:S(2)}) collective-permute-start(bf16[8,6144]{1,0:T(8,128)(2,1)S(1)} %collective-permute-done.9.refs_10_), channel_id=1, source_target_pairs={{0,2},{1,3},{4,0},{5,1},{8,4},{9,5},{12,8},{13,9},{14,12},{15,13},... | collective-permute-start | bytes 294920 | tf_op jit(solution)/shard_map/ppermute | solution.py:204
  11.2 6.2 %collective-permute-start.10 = (bf16[8,6144]{1,0:T(8,128)(2,1)S(1)}, bf16[8,6144]{1,0:T(8,128)(2,1)S(1)}, u32[]{:S(2)}, u32[]{:S(2)}) collective-permute-start(bf16[8,6144]{1,0:T(8,128)(2,1)S(1)} %collective-permute-done.8.refs_9_), channel_id=1, source_target_pairs={{0,4},{1,5},{4,8},{5,9},{8,12},{9,13},{12,14},{13,15},{14,10},{15,... | collective-permute-start | bytes 294920 | tf_op jit(solution)/shard_map/ppermute | solution.py:204
  11.9 7.5 %collective-permute-start.5 = (bf16[8,6144]{1,0:T(8,128)(2,1)S(1)}, bf16[8,6144]{1,0:T(8,128)(2,1)S(1)}, u32[]{:S(2)}, u32[]{:S(2)}) collective-permute-start(bf16[8,6144]{1,0:T(8,128)(2,1)S(1)} %collective-permute-done.3.refs_4_), channel_id=1, source_target_pairs={{0,2},{1,3},{4,0},{5,1},{8,4},{9,5},{12,8},{13,9},{14,12},{15,13},... | collective-permute-start | bytes 294920 | tf_op jit(solution)/shard_map/ppermute | solution.py:204
  13.7 8.0 %collective-permute-start.6 = (bf16[8,6144]{1,0:T(8,128)(2,1)S(1)}, bf16[8,6144]{1,0:T(8,128)(2,1)S(1)}, u32[]{:S(2)}, u32[]{:S(2)}) collective-permute-start(bf16[8,6144]{1,0:T(8,128)(2,1)S(1)} %collective-permute-done.2.refs_3_), channel_id=1, source_target_pairs={{0,8},{1,9},{4,12},{5,13},{8,14},{9,15},{12,10},{13,11},{14,6},{15... | collective-permute-start | bytes 294920 | tf_op jit(solution)/shard_map/ppermute | solution.py:204
  15.2 6.5 %collective-permute-start.4 = (bf16[8,6144]{1,0:T(8,128)(2,1)S(1)}, bf16[8,6144]{1,0:T(8,128)(2,1)S(1)}, u32[]{:S(2)}, u32[]{:S(2)}) collective-permute-start(bf16[8,6144]{1,0:T(8,128)(2,1)S(1)} %collective-permute-done.2.refs_3_), channel_id=1, source_target_pairs={{0,4},{1,5},{4,8},{5,9},{8,12},{9,13},{12,14},{13,15},{14,10},{15,... | collective-permute-start | bytes 294920 | tf_op jit(solution)/shard_map/ppermute | solution.py:204
  16.8 7.5 %collective-permute-start.14 = (bf16[8,6144]{1,0:T(8,128)(2,1)S(1)}, bf16[8,6144]{1,0:T(8,128)(2,1)S(1)}, u32[]{:S(2)}, u32[]{:S(2)}) collective-permute-start(bf16[8,6144]{1,0:T(8,128)(2,1)S(1)} %collective-permute-done.11.refs_12_), channel_id=1, source_target_pairs={{0,6},{1,7},{4,2},{5,3},{8,0},{9,1},{12,4},{13,5},{14,8},{15,9},{1... | collective-permute-start | bytes 294920 | tf_op jit(solution)/shard_map/ppermute | solution.py:204
  17.3 7.3 %collective-permute-start.13 = (bf16[8,6144]{1,0:T(8,128)(2,1)S(1)}, bf16[8,6144]{1,0:T(8,128)(2,1)S(1)}, u32[]{:S(2)}, u32[]{:S(2)}) collective-permute-start(bf16[8,6144]{1,0:T(8,128)(2,1)S(1)} %collective-permute-done.11.refs_12_), channel_id=1, source_target_pairs={{0,2},{1,3},{4,0},{5,1},{8,4},{9,5},{12,8},{13,9},{14,12},{15,13},... | collective-permute-start | bytes 294920 | tf_op jit(solution)/shard_map/ppermute | solution.py:204
  19.4 5.2 %collective-permute-start.12 = (bf16[8,6144]{1,0:T(8,128)(2,1)S(1)}, bf16[8,6144]{1,0:T(8,128)(2,1)S(1)}, u32[]{:S(2)}, u32[]{:S(2)}) collective-permute-start(bf16[8,6144]{1,0:T(8,128)(2,1)S(1)} %collective-permute-done.10.refs_11_), channel_id=1, source_target_pairs={{0,4},{1,5},{4,8},{5,9},{8,12},{9,13},{12,14},{13,15},{14,10},{15,... | collective-permute-start | bytes 294920 | tf_op jit(solution)/shard_map/ppermute | solution.py:204
  32.0 5.9 %collective-permute-start.19 = (bf16[8,6144]{1,0:T(8,128)(2,1)S(1)}, bf16[8,6144]{1,0:T(8,128)(2,1)S(1)}, u32[]{:S(2)}, u32[]{:S(2)}) collective-permute-start(bf16[8,6144]{1,0:T(8,128)(2,1)S(1)} %convert_element_type.81), channel_id=1, source_target_pairs={{0,4},{1,5},{4,8},{5,9},{8,12},{9,13},{12,14},{13,15},{14,10},{15,... | collective-permute-start | bytes 294920 | tf_op jit(solution)/shard_map/ppermute | solution.py:204
  33.7 14.2 %collective-permute-start.18 = (bf16[8,6144]{1,0:T(8,128)(2,1)S(1)}, bf16[8,6144]{1,0:T(8,128)(2,1)S(1)}, u32[]{:S(2)}, u32[]{:S(2)}) collective-permute-start(bf16[8,6144]{1,0:T(8,128)(2,1)S(1)} %convert_element_type.80), channel_id=1, source_target_pairs={{0,1},{1,0},{2,3},{3,2},{4,5},{5,4},{6,7},{7,6},{8,9},{9,8},{10,11... | collective-permute-start | bytes 294920 | tf_op jit(solution)/shard_map/ppermute | solution.py:230
  33.7 5.6 %collective-permute-start.15 = (bf16[8,6144]{1,0:T(8,128)(2,1)S(1)}, bf16[8,6144]{1,0:T(8,128)(2,1)S(1)}, u32[]{:S(2)}, u32[]{:S(2)}) collective-permute-start(bf16[8,6144]{1,0:T(8,128)(2,1)S(1)} %convert_element_type.75), channel_id=1, source_target_pairs={{0,2},{1,3},{4,0},{5,1},{8,4},{9,5},{12,8},{13,9},{14,12},{15,13},... | collective-permute-start | bytes 294920 | tf_op jit(solution)/shard_map/ppermute | solution.py:204
  34.5 6.5 %collective-permute-start.27 = (bf16[8,6144]{1,0:T(8,128)(2,1)S(1)}, bf16[8,6144]{1,0:T(8,128)(2,1)S(1)}, u32[]{:S(2)}, u32[]{:S(2)}) collective-permute-start(bf16[8,6144]{1,0:T(8,128)(2,1)S(1)} %add_convert_fusion.2), channel_id=1, source_target_pairs={{0,2},{1,3},{4,0},{5,1},{8,4},{9,5},{12,8},{13,9},{14,12},{15,13},... | collective-permute-start | bytes 294920 | tf_op jit(solution)/shard_map/ppermute | solution.py:204
  36.9 5.0 %collective-permute-start.23 = (bf16[8,6144]{1,0:T(8,128)(2,1)S(1)}, bf16[8,6144]{1,0:T(8,128)(2,1)S(1)}, u32[]{:S(2)}, u32[]{:S(2)}) collective-permute-start(bf16[8,6144]{1,0:T(8,128)(2,1)S(1)} %add_convert_fusion.5), channel_id=1, source_target_pairs={{0,4},{1,5},{4,8},{5,9},{8,12},{9,13},{12,14},{13,15},{14,10},{15,... | collective-permute-start | bytes 294920 | tf_op jit(solution)/shard_map/ppermute | solution.py:204
  38.0 5.2 %collective-permute-start.20 = (bf16[8,6144]{1,0:T(8,128)(2,1)S(1)}, bf16[8,6144]{1,0:T(8,128)(2,1)S(1)}, u32[]{:S(2)}, u32[]{:S(2)}) collective-permute-start(bf16[8,6144]{1,0:T(8,128)(2,1)S(1)} %add_convert_fusion.7), channel_id=1, source_target_pairs={{0,4},{1,5},{4,8},{5,9},{8,12},{9,13},{12,14},{13,15},{14,10},{15,... | collective-permute-start | bytes 294920 | tf_op jit(solution)/shard_map/ppermute | solution.py:204
  39.3 5.3 %collective-permute-start.16 = (bf16[8,6144]{1,0:T(8,128)(2,1)S(1)}, bf16[8,6144]{1,0:T(8,128)(2,1)S(1)}, u32[]{:S(2)}, u32[]{:S(2)}) collective-permute-start(bf16[8,6144]{1,0:T(8,128)(2,1)S(1)} %add_convert_fusion.9), channel_id=1, source_target_pairs={{0,2},{1,3},{4,0},{5,1},{8,4},{9,5},{12,8},{13,9},{14,12},{15,13},... | collective-permute-start | bytes 294920 | tf_op jit(solution)/shard_map/ppermute | solution.py:204
  41.1 5.1 %collective-permute-start.28 = (bf16[8,6144]{1,0:T(8,128)(2,1)S(1)}, bf16[8,6144]{1,0:T(8,128)(2,1)S(1)}, u32[]{:S(2)}, u32[]{:S(2)}) collective-permute-start(bf16[8,6144]{1,0:T(8,128)(2,1)S(1)} %add_convert_fusion.1), channel_id=1, source_target_pairs={{0,2},{1,3},{4,0},{5,1},{8,4},{9,5},{12,8},{13,9},{14,12},{15,13},... | collective-permute-start | bytes 294920 | tf_op jit(solution)/shard_map/ppermute | solution.py:204
  41.9 5.0 %collective-permute-start.24 = (bf16[8,6144]{1,0:T(8,128)(2,1)S(1)}, bf16[8,6144]{1,0:T(8,128)(2,1)S(1)}, u32[]{:S(2)}, u32[]{:S(2)}) collective-permute-start(bf16[8,6144]{1,0:T(8,128)(2,1)S(1)} %add_convert_fusion.4), channel_id=1, source_target_pairs={{0,4},{1,5},{4,8},{5,9},{8,12},{9,13},{12,14},{13,15},{14,10},{15,... | collective-permute-start | bytes 294920 | tf_op jit(solution)/shard_map/ppermute | solution.py:204
  43.2 5.1 %collective-permute-start.21 = (bf16[8,6144]{1,0:T(8,128)(2,1)S(1)}, bf16[8,6144]{1,0:T(8,128)(2,1)S(1)}, u32[]{:S(2)}, u32[]{:S(2)}) collective-permute-start(bf16[8,6144]{1,0:T(8,128)(2,1)S(1)} %add_convert_fusion.6), channel_id=1, source_target_pairs={{0,5},{1,4},{4,9},{5,8},{8,13},{9,12},{12,15},{13,14},{14,11},{15,... | collective-permute-start | bytes 294920 | tf_op jit(solution)/shard_map/ppermute | solution.py:204
  44.7 5.7 %collective-permute-start.17 = (bf16[8,6144]{1,0:T(8,128)(2,1)S(1)}, bf16[8,6144]{1,0:T(8,128)(2,1)S(1)}, u32[]{:S(2)}, u32[]{:S(2)}) collective-permute-start(bf16[8,6144]{1,0:T(8,128)(2,1)S(1)} %add_convert_fusion.8), channel_id=1, source_target_pairs={{0,2},{1,3},{4,0},{5,1},{8,4},{9,5},{12,8},{13,9},{14,12},{15,13},... | collective-permute-start | bytes 294920 | tf_op jit(solution)/shard_map/ppermute | solution.py:204
  46.1 5.2 %collective-permute-start.29 = (bf16[8,6144]{1,0:T(8,128)(2,1)S(1)}, bf16[8,6144]{1,0:T(8,128)(2,1)S(1)}, u32[]{:S(2)}, u32[]{:S(2)}) collective-permute-start(bf16[8,6144]{1,0:T(8,128)(2,1)S(1)} %add_convert_fusion), channel_id=1, source_target_pairs={{0,3},{1,2},{4,1},{5,0},{8,5},{9,4},{12,9},{13,8},{14,13},{15,12},... | collective-permute-start | bytes 294920 | tf_op jit(solution)/shard_map/ppermute | solution.py:204
  47.0 5.2 %collective-permute-start.25 = (bf16[8,6144]{1,0:T(8,128)(2,1)S(1)}, bf16[8,6144]{1,0:T(8,128)(2,1)S(1)}, u32[]{:S(2)}, u32[]{:S(2)}) collective-permute-start(bf16[8,6144]{1,0:T(8,128)(2,1)S(1)} %add_convert_fusion.3), channel_id=1, source_target_pairs={{0,4},{1,5},{4,8},{5,9},{8,12},{9,13},{12,14},{13,15},{14,10},{15,... | collective-permute-start | bytes 294920 | tf_op jit(solution)/shard_map/ppermute | solution.py:204
  (9 other events, 99.0 us)

commit v6 on v5

--- a/solution.py
+++ b/solution.py
@@ -190,10 +190,11 @@
     count = len(ring)
     near, opposite = (count - 1) // 2, count // 2
     swap = [(0, 1), (1, 0)]
-    long = (1, -1)
-    steps = [(chain, -way * step, way) for step in range(1, near + 1) for chain in (0, 1) for way in (1, -1)]
-    if count % 2 == 0:
-        steps += [(chain, -long[chain] * opposite, long[chain]) for chain in (0, 1)]
+    def outwards(long):
+        steps = [(chain, -way * step, way) for step in range(1, near + 1) for way in (1, -1) for chain in (0, 1)]
+        if count % 2 == 0:
+            steps += [(chain, -long[chain] * opposite, long[chain]) for chain in (0, 1)]
+        return steps
 
     def send(block, hops, crossing=False):
         perm = [
@@ -205,7 +206,7 @@
 
     def gather(mine, theirs):
         held = ({0: mine}, {0: lax.ppermute(theirs, "expert", swap)})
-        for chain, place, way in steps:
+        for chain, place, way in outwards((1, -1)):
             if abs(place) == opposite and near and count % 2 == 0:
                 held[chain][place] = send(held[chain][place + 2 * way], 2 * way)
             elif place + way:
@@ -215,9 +216,10 @@
         return held
 
     def scatter(terms):
+        long = (-1, 1)
         arrived, early, last = {}, ([], []), [None, None]
-        for chain, place, way in reversed(steps):
-            term = terms[chain][place if abs(place) == opposite and count % 2 == 0 else -place].astype(jnp.float32)
+        for chain, place, way in reversed(outwards(long)):
+            term = terms[chain][-place if -place in terms[chain] else place].astype(jnp.float32)
             if (chain, place, way) in arrived:
                 term = term + arrived[chain, place, way].astype(jnp.float32)
             got = send(term.astype(jnp.bfloat16), way, crossing=chain == 1 and place + way == 0)

time: 53.4 us -> 53 us (level)
  waiting for transfers between devices: 16.2 us -> 14.9 us
  starting transfers between devices: 29 us -> 29.9 us
    ppermute x28, waiting for transfers between devices: 16.1 us -> 14.9 us  [send(): return lax.ppermute(block, ('tensor', 'expert'), perm)]
    ppermute x28, starting transfers between devices: 29 us -> 29.9 us  [send(): return lax.ppermute(block, ('tensor', 'expert'), perm)]
  transfers between devices with their start and end apart: 30 -> 30, of which waited for: 18 -> 14; matrix products, arithmetic and copies ran while one was open for 0% -> 0% of each run, Pallas kernels for 0% -> 0%
where the time goes in v6:
time: 53 us; the launch traced here: 52.9 us
  starting transfers between devices  29.9 us (56%)
  waiting for transfers between devices  14.9 us (28%)
  Pallas kernels  7.59 us (14%)
    ppermute x28, starting transfers between devices, send(): return lax.ppermute(block, ('tensor', 'expert'), perm)  29.9 us
    ppermute x28, waiting for transfers between devices, send(): return lax.ppermute(block, ('tensor', 'expert'), perm)  14.9 us
    pallas_call x1, Pallas kernels, feed_forward(): pl.pallas_call(functools.partial(feed_forward_kernel, count, capacity), o...  5.14 us
  transfers between devices with their start and end apart: 30, of which 14 were waited for; matrix products, arithmetic and copies ran while one was open for 0% of the time, Pallas kernels for 0%

profile of v6, /device:TPU:0, one launch (start us, length us, event | category | flops | bytes accessed | tf_op | source)
XLA Modules:
  0.0 52.9 jit_solution(5212752429624472031)
XLA Ops:
  0.0 1.1 %shard_map.64 = (s32[2,32]{1,0:T(2,128)S(1)}, f32[2,32]{1,0:T(2,128)S(1)}, bf16[32,6144]{1,0:T(8,128)(2,1)S(1)}) custom-call(s32[2,32]{1,0:T(2,128)} %bitcast.9, f32[2,32]{1,0:T(2,128)} %bitcast.10, bf16[32,6144]{1,0:T(8,128)(2,1)} %refs_2_.1), custom_call_target="tpu_custom_call" | custom-call | tf_op jit(solution)/shard_map/pallas_call | solution.py:44
  1.4 3.0 %collective-permute-start.1 = (bf16[8,6144]{1,0:T(8,128)(2,1)S(1)}, bf16[8,6144]{1,0:T(8,128)(2,1)S(1)}, u32[]{:S(2)}, u32[]{:S(2)}) collective-permute-start(bf16[8,6144]{1,0:T(8,128)(2,1)S(1)} %get-tuple-element.33.refs_0_), channel_id=1, source_target_pairs={{0,2},{1,3},{4,0},{5,1},{8,4},{9,5},{12,8},{13,9},{14,12},{15,13},... | collective-permute-start | bytes 294920 | tf_op jit(solution)/shard_map/ppermute | solution.py:205
  6.3 1.0 %collective-permute-done.1.refs_2_ = bf16[8,6144]{1,0:T(8,128)(2,1)S(1)} collective-permute-done((bf16[8,6144]{1,0:T(8,128)(2,1)S(1)}, bf16[8,6144]{1,0:T(8,128)(2,1)S(1)}, u32[]{:S(2)}, u32[]{:S(2)}) %collective-permute-start.1) | collective-permute-done | bytes 98336 | tf_op jit(solution)/shard_map/ppermute | solution.py:205
  7.3 1.8 %collective-permute-start.3 = (bf16[8,6144]{1,0:T(8,128)(2,1)S(1)}, bf16[8,6144]{1,0:T(8,128)(2,1)S(1)}, u32[]{:S(2)}, u32[]{:S(2)}) collective-permute-start(bf16[8,6144]{1,0:T(8,128)(2,1)S(1)} %collective-permute-done.1.refs_2_), channel_id=1, source_target_pairs={{0,2},{1,3},{4,0},{5,1},{8,4},{9,5},{12,8},{13,9},{14,12},{15,13},... | collective-permute-start | bytes 294920 | tf_op jit(solution)/shard_map/ppermute | solution.py:205
  9.3 1.8 %collective-permute-start.11 = (bf16[8,6144]{1,0:T(8,128)(2,1)S(1)}, bf16[8,6144]{1,0:T(8,128)(2,1)S(1)}, u32[]{:S(2)}, u32[]{:S(2)}) collective-permute-start(bf16[8,6144]{1,0:T(8,128)(2,1)S(1)} %collective-permute-done.9.refs_10_), channel_id=1, source_target_pairs={{0,2},{1,3},{4,0},{5,1},{8,4},{9,5},{12,8},{13,9},{14,12},{15,13},... | collective-permute-start | bytes 294920 | tf_op jit(solution)/shard_map/ppermute | solution.py:205
  11.9 1.8 %collective-permute-start.5 = (bf16[8,6144]{1,0:T(8,128)(2,1)S(1)}, bf16[8,6144]{1,0:T(8,128)(2,1)S(1)}, u32[]{:S(2)}, u32[]{:S(2)}) collective-permute-start(bf16[8,6144]{1,0:T(8,128)(2,1)S(1)} %collective-permute-done.3.refs_4_), channel_id=1, source_target_pairs={{0,2},{1,3},{4,0},{5,1},{8,4},{9,5},{12,8},{13,9},{14,12},{15,13},... | collective-permute-start | bytes 294920 | tf_op jit(solution)/shard_map/ppermute | solution.py:205
  13.7 1.5 %collective-permute-start.6 = (bf16[8,6144]{1,0:T(8,128)(2,1)S(1)}, bf16[8,6144]{1,0:T(8,128)(2,1)S(1)}, u32[]{:S(2)}, u32[]{:S(2)}) collective-permute-start(bf16[8,6144]{1,0:T(8,128)(2,1)S(1)} %collective-permute-done.2.refs_3_), channel_id=1, source_target_pairs={{0,8},{1,9},{4,12},{5,13},{8,14},{9,15},{12,10},{13,11},{14,6},{15... | collective-permute-start | bytes 294920 | tf_op jit(solution)/shard_map/ppermute | solution.py:205
  15.2 1.6 %collective-permute-start.4 = (bf16[8,6144]{1,0:T(8,128)(2,1)S(1)}, bf16[8,6144]{1,0:T(8,128)(2,1)S(1)}, u32[]{:S(2)}, u32[]{:S(2)}) collective-permute-start(bf16[8,6144]{1,0:T(8,128)(2,1)S(1)} %collective-permute-done.2.refs_3_), channel_id=1, source_target_pairs={{0,4},{1,5},{4,8},{5,9},{8,12},{9,13},{12,14},{13,15},{14,10},{15,... | collective-permute-start | bytes 294920 | tf_op jit(solution)/shard_map/ppermute | solution.py:205
  17.3 2.1 %collective-permute-start.13 = (bf16[8,6144]{1,0:T(8,128)(2,1)S(1)}, bf16[8,6144]{1,0:T(8,128)(2,1)S(1)}, u32[]{:S(2)}, u32[]{:S(2)}) collective-permute-start(bf16[8,6144]{1,0:T(8,128)(2,1)S(1)} %collective-permute-done.11.refs_12_), channel_id=1, source_target_pairs={{0,2},{1,3},{4,0},{5,1},{8,4},{9,5},{12,8},{13,9},{14,12},{15,13},... | collective-permute-start | bytes 294920 | tf_op jit(solution)/shard_map/ppermute | solution.py:205
  19.4 2.3 %collective-permute-done.6.refs_7_ = bf16[8,6144]{1,0:T(8,128)(2,1)S(1)} collective-permute-done((bf16[8,6144]{1,0:T(8,128)(2,1)S(1)}, bf16[8,6144]{1,0:T(8,128)(2,1)S(1)}, u32[]{:S(2)}, u32[]{:S(2)}) %collective-permute-start.6) | collective-permute-done | bytes 98336 | tf_op jit(solution)/shard_map/ppermute | solution.py:205
  21.7 2.5 %collective-permute-done.14.refs_15_ = bf16[8,6144]{1,0:T(8,128)(2,1)S(1)} collective-permute-done((bf16[8,6144]{1,0:T(8,128)(2,1)S(1)}, bf16[8,6144]{1,0:T(8,128)(2,1)S(1)}, u32[]{:S(2)}, u32[]{:S(2)}) %collective-permute-start.14) | collective-permute-done | bytes 98336 | tf_op jit(solution)/shard_map/ppermute | solution.py:205
  24.6 5.1 %shard_map.66 = (f32[8,6144]{1,0:T(8,128)S(1)}, f32[8,6144]{1,0:T(8,128)S(1)}, f32[8,6144]{1,0:T(8,128)S(1)}, f32[8,6144]{1,0:T(8,128)S(1)}, f32[8,6144]{1,0:T(8...) custom-call(bf16[8,6144]{1,0:T(8,128)(2,1)S(1)} %get-tuple-element.3, ...), custom_call_target="tpu_custom_call" | custom-call | flops 4831838208 | tf_op jit(solution)/shard_map/pallas_call | solution.py:170
  29.8 1.7 %collective-permute-start.26 = (bf16[8,6144]{1,0:T(8,128)(2,1)S(1)}, bf16[8,6144]{1,0:T(8,128)(2,1)S(1)}, u32[]{:S(2)}, u32[]{:S(2)}) collective-permute-start(bf16[8,6144]{1,0:T(8,128)(2,1)S(1)} %convert_element_type.93), channel_id=1, source_target_pairs={{0,4},{1,5},{4,8},{5,9},{8,12},{9,13},{12,14},{13,15},{14,10},{15,... | collective-permute-start | bytes 294920 | tf_op jit(solution)/shard_map/ppermute | solution.py:205
  32.0 2.0 %collective-permute-start.19 = (bf16[8,6144]{1,0:T(8,128)(2,1)S(1)}, bf16[8,6144]{1,0:T(8,128)(2,1)S(1)}, u32[]{:S(2)}, u32[]{:S(2)}) collective-permute-start(bf16[8,6144]{1,0:T(8,128)(2,1)S(1)} %convert_element_type.81), channel_id=1, source_target_pairs={{0,2},{1,3},{4,0},{5,1},{8,4},{9,5},{12,8},{13,9},{14,12},{15,13},... | collective-permute-start | bytes 294920 | tf_op jit(solution)/shard_map/ppermute | solution.py:205
  34.5 1.7 %collective-permute-start.27 = (bf16[8,6144]{1,0:T(8,128)(2,1)S(1)}, bf16[8,6144]{1,0:T(8,128)(2,1)S(1)}, u32[]{:S(2)}, u32[]{:S(2)}) collective-permute-start(bf16[8,6144]{1,0:T(8,128)(2,1)S(1)} %add_convert_fusion.2), channel_id=1, source_target_pairs={{0,4},{1,5},{4,8},{5,9},{8,12},{9,13},{12,14},{13,15},{14,10},{15,... | collective-permute-start | bytes 294920 | tf_op jit(solution)/shard_map/ppermute | solution.py:205
  36.3 1.3 %collective-permute-start.23 = (bf16[8,6144]{1,0:T(8,128)(2,1)S(1)}, bf16[8,6144]{1,0:T(8,128)(2,1)S(1)}, u32[]{:S(2)}, u32[]{:S(2)}) collective-permute-start(bf16[8,6144]{1,0:T(8,128)(2,1)S(1)} %add_convert_fusion.5), channel_id=1, source_target_pairs={{0,2},{1,3},{4,0},{5,1},{8,4},{9,5},{12,8},{13,9},{14,12},{15,13},... | collective-permute-start | bytes 294920 | tf_op jit(solution)/shard_map/ppermute | solution.py:205
  37.7 1.6 %collective-permute-start.20 = (bf16[8,6144]{1,0:T(8,128)(2,1)S(1)}, bf16[8,6144]{1,0:T(8,128)(2,1)S(1)}, u32[]{:S(2)}, u32[]{:S(2)}) collective-permute-start(bf16[8,6144]{1,0:T(8,128)(2,1)S(1)} %add_convert_fusion.7), channel_id=1, source_target_pairs={{0,2},{1,3},{4,0},{5,1},{8,4},{9,5},{12,8},{13,9},{14,12},{15,13},... | collective-permute-start | bytes 294920 | tf_op jit(solution)/shard_map/ppermute | solution.py:205
  39.9 1.5 %collective-permute-done.27 = bf16[8,6144]{1,0:T(8,128)(2,1)S(1)} collective-permute-done((bf16[8,6144]{1,0:T(8,128)(2,1)S(1)}, bf16[8,6144]{1,0:T(8,128)(2,1)S(1)}, u32[]{:S(2)}, u32[]{:S(2)}) %collective-permute-start.27) | collective-permute-done | bytes 98336 | tf_op jit(solution)/shard_map/ppermute | solution.py:205
  41.7 1.8 %collective-permute-start.24 = (bf16[8,6144]{1,0:T(8,128)(2,1)S(1)}, bf16[8,6144]{1,0:T(8,128)(2,1)S(1)}, u32[]{:S(2)}, u32[]{:S(2)}) collective-permute-start(bf16[8,6144]{1,0:T(8,128)(2,1)S(1)} %add_convert_fusion.4), channel_id=1, source_target_pairs={{0,2},{1,3},{4,0},{5,1},{8,4},{9,5},{12,8},{13,9},{14,12},{15,13},... | collective-permute-start | bytes 294920 | tf_op jit(solution)/shard_map/ppermute | solution.py:205
  43.9 1.0 %collective-permute-done.16 = bf16[8,6144]{1,0:T(8,128)(2,1)S(1)} collective-permute-done((bf16[8,6144]{1,0:T(8,128)(2,1)S(1)}, bf16[8,6144]{1,0:T(8,128)(2,1)S(1)}, u32[]{:S(2)}, u32[]{:S(2)}) %collective-permute-start.16) | collective-permute-done | bytes 98336 | tf_op jit(solution)/shard_map/ppermute | solution.py:205
  45.1 1.4 %collective-permute-done.28 = bf16[8,6144]{1,0:T(8,128)(2,1)S(1)} collective-permute-done((bf16[8,6144]{1,0:T(8,128)(2,1)S(1)}, bf16[8,6144]{1,0:T(8,128)(2,1)S(1)}, u32[]{:S(2)}, u32[]{:S(2)}) %collective-permute-start.28) | collective-permute-done | bytes 98336 | tf_op jit(solution)/shard_map/ppermute | solution.py:205
  46.5 1.7 %collective-permute-start.25 = (bf16[8,6144]{1,0:T(8,128)(2,1)S(1)}, bf16[8,6144]{1,0:T(8,128)(2,1)S(1)}, u32[]{:S(2)}, u32[]{:S(2)}) collective-permute-start(bf16[8,6144]{1,0:T(8,128)(2,1)S(1)} %add_convert_fusion.3), channel_id=1, source_target_pairs={{0,2},{1,3},{4,0},{5,1},{8,4},{9,5},{12,8},{13,9},{14,12},{15,13},... | collective-permute-start | bytes 294920 | tf_op jit(solution)/shard_map/ppermute | solution.py:205
  48.5 2.1 %collective-permute-done.17.refs_1_ = bf16[8,6144]{1,0:T(8,128)(2,1)S(1)} collective-permute-done((bf16[8,6144]{1,0:T(8,128)(2,1)S(1)}, bf16[8,6144]{1,0:T(8,128)(2,1)S(1)}, u32[]{:S(2)}, u32[]{:S(2)}) %collective-permute-start.17) | collective-permute-done | bytes 98336 | tf_op jit(solution)/shard_map/ppermute | solution.py:205
  51.8 1.1 %shard_map.68 = bf16[32,6144]{1,0:T(8,128)(2,1)} custom-call(f32[16,32]{1,0:T(8,128)S(1)} %get-tuple-element.32.coefficient, f32[8,6144]{1,0:T(8,128)S(1)} %get-tuple-element.43.refs_0_, bf16[8,6144]{1,0:T(8,128)(2,1)S(1)} %collective-permute-done.25.refs_1_, f32[8,6144]{1,0:T(8,128)S(1)} %get-tuple-element.48.refs_2_, ...), custom_call_target="tpu_custom_call" | custom-call | tf_op jit(solution)/shard_map/pallas_call | solution.py:142
  (62 shorter events, 8.2 us)
Async XLA Ops:
  1.4 5.9 %collective-permute-start.1 = (bf16[8,6144]{1,0:T(8,128)(2,1)S(1)}, bf16[8,6144]{1,0:T(8,128)(2,1)S(1)}, u32[]{:S(2)}, u32[]{:S(2)}) collective-permute-start(bf16[8,6144]{1,0:T(8,128)(2,1)S(1)} %get-tuple-element.33.refs_0_), channel_id=1, source_target_pairs={{0,2},{1,3},{4,0},{5,1},{8,4},{9,5},{12,8},{13,9},{14,12},{15,13},... | collective-permute-start | bytes 294920 | tf_op jit(solution)/shard_map/ppermute | solution.py:205
  5.3 5.8 %collective-permute-start.8 = (bf16[8,6144]{1,0:T(8,128)(2,1)S(1)}, bf16[8,6144]{1,0:T(8,128)(2,1)S(1)}, u32[]{:S(2)}, u32[]{:S(2)}) collective-permute-start(bf16[8,6144]{1,0:T(8,128)(2,1)S(1)} %get-tuple-element.34), channel_id=1, source_target_pairs={{0,5},{1,4},{4,9},{5,8},{8,13},{9,12},{12,15},{13,14},{14,11},{15,... | collective-permute-start | bytes 294920 | tf_op jit(solution)/shard_map/ppermute | solution.py:205
  9.3 5.9 %collective-permute-start.7 = (bf16[8,6144]{1,0:T(8,128)(2,1)S(1)}, bf16[8,6144]{1,0:T(8,128)(2,1)S(1)}, u32[]{:S(2)}, u32[]{:S(2)}) collective-permute-start(bf16[8,6144]{1,0:T(8,128)(2,1)S(1)} %get-tuple-element.34), channel_id=1, source_target_pairs={{0,1},{1,0},{2,3},{3,2},{4,5},{5,4},{6,7},{7,6},{8,9},{9,8},{10,11... | collective-permute-start | bytes 294920 | tf_op jit(solution)/shard_map/ppermute | solution.py:208
  9.3 7.5 %collective-permute-start.11 = (bf16[8,6144]{1,0:T(8,128)(2,1)S(1)}, bf16[8,6144]{1,0:T(8,128)(2,1)S(1)}, u32[]{:S(2)}, u32[]{:S(2)}) collective-permute-start(bf16[8,6144]{1,0:T(8,128)(2,1)S(1)} %collective-permute-done.9.refs_10_), channel_id=1, source_target_pairs={{0,2},{1,3},{4,0},{5,1},{8,4},{9,5},{12,8},{13,9},{14,12},{15,13},... | collective-permute-start | bytes 294920 | tf_op jit(solution)/shard_map/ppermute | solution.py:205
  11.2 6.2 %collective-permute-start.10 = (bf16[8,6144]{1,0:T(8,128)(2,1)S(1)}, bf16[8,6144]{1,0:T(8,128)(2,1)S(1)}, u32[]{:S(2)}, u32[]{:S(2)}) collective-permute-start(bf16[8,6144]{1,0:T(8,128)(2,1)S(1)} %collective-permute-done.8.refs_9_), channel_id=1, source_target_pairs={{0,4},{1,5},{4,8},{5,9},{8,12},{9,13},{12,14},{13,15},{14,10},{15,... | collective-permute-start | bytes 294920 | tf_op jit(solution)/shard_map/ppermute | solution.py:205
  11.9 7.5 %collective-permute-start.5 = (bf16[8,6144]{1,0:T(8,128)(2,1)S(1)}, bf16[8,6144]{1,0:T(8,128)(2,1)S(1)}, u32[]{:S(2)}, u32[]{:S(2)}) collective-permute-start(bf16[8,6144]{1,0:T(8,128)(2,1)S(1)} %collective-permute-done.3.refs_4_), channel_id=1, source_target_pairs={{0,2},{1,3},{4,0},{5,1},{8,4},{9,5},{12,8},{13,9},{14,12},{15,13},... | collective-permute-start | bytes 294920 | tf_op jit(solution)/shard_map/ppermute | solution.py:205
  13.7 8.0 %collective-permute-start.6 = (bf16[8,6144]{1,0:T(8,128)(2,1)S(1)}, bf16[8,6144]{1,0:T(8,128)(2,1)S(1)}, u32[]{:S(2)}, u32[]{:S(2)}) collective-permute-start(bf16[8,6144]{1,0:T(8,128)(2,1)S(1)} %collective-permute-done.2.refs_3_), channel_id=1, source_target_pairs={{0,8},{1,9},{4,12},{5,13},{8,14},{9,15},{12,10},{13,11},{14,6},{15... | collective-permute-start | bytes 294920 | tf_op jit(solution)/shard_map/ppermute | solution.py:205
  15.2 6.5 %collective-permute-start.4 = (bf16[8,6144]{1,0:T(8,128)(2,1)S(1)}, bf16[8,6144]{1,0:T(8,128)(2,1)S(1)}, u32[]{:S(2)}, u32[]{:S(2)}) collective-permute-start(bf16[8,6144]{1,0:T(8,128)(2,1)S(1)} %collective-permute-done.2.refs_3_), channel_id=1, source_target_pairs={{0,4},{1,5},{4,8},{5,9},{8,12},{9,13},{12,14},{13,15},{14,10},{15,... | collective-permute-start | bytes 294920 | tf_op jit(solution)/shard_map/ppermute | solution.py:205
  16.8 7.5 %collective-permute-start.14 = (bf16[8,6144]{1,0:T(8,128)(2,1)S(1)}, bf16[8,6144]{1,0:T(8,128)(2,1)S(1)}, u32[]{:S(2)}, u32[]{:S(2)}) collective-permute-start(bf16[8,6144]{1,0:T(8,128)(2,1)S(1)} %collective-permute-done.11.refs_12_), channel_id=1, source_target_pairs={{0,6},{1,7},{4,2},{5,3},{8,0},{9,1},{12,4},{13,5},{14,8},{15,9},{1... | collective-permute-start | bytes 294920 | tf_op jit(solution)/shard_map/ppermute | solution.py:205
  17.3 7.3 %collective-permute-start.13 = (bf16[8,6144]{1,0:T(8,128)(2,1)S(1)}, bf16[8,6144]{1,0:T(8,128)(2,1)S(1)}, u32[]{:S(2)}, u32[]{:S(2)}) collective-permute-start(bf16[8,6144]{1,0:T(8,128)(2,1)S(1)} %collective-permute-done.11.refs_12_), channel_id=1, source_target_pairs={{0,2},{1,3},{4,0},{5,1},{8,4},{9,5},{12,8},{13,9},{14,12},{15,13},... | collective-permute-start | bytes 294920 | tf_op jit(solution)/shard_map/ppermute | solution.py:205
  19.4 5.2 %collective-permute-start.12 = (bf16[8,6144]{1,0:T(8,128)(2,1)S(1)}, bf16[8,6144]{1,0:T(8,128)(2,1)S(1)}, u32[]{:S(2)}, u32[]{:S(2)}) collective-permute-start(bf16[8,6144]{1,0:T(8,128)(2,1)S(1)} %collective-permute-done.10.refs_11_), channel_id=1, source_target_pairs={{0,4},{1,5},{4,8},{5,9},{8,12},{9,13},{12,14},{13,15},{14,10},{15,... | collective-permute-start | bytes 294920 | tf_op jit(solution)/shard_map/ppermute | solution.py:205
  32.0 5.6 %collective-permute-start.19 = (bf16[8,6144]{1,0:T(8,128)(2,1)S(1)}, bf16[8,6144]{1,0:T(8,128)(2,1)S(1)}, u32[]{:S(2)}, u32[]{:S(2)}) collective-permute-start(bf16[8,6144]{1,0:T(8,128)(2,1)S(1)} %convert_element_type.81), channel_id=1, source_target_pairs={{0,2},{1,3},{4,0},{5,1},{8,4},{9,5},{12,8},{13,9},{14,12},{15,13},... | collective-permute-start | bytes 294920 | tf_op jit(solution)/shard_map/ppermute | solution.py:205
  34.0 14.2 %collective-permute-start.18 = (bf16[8,6144]{1,0:T(8,128)(2,1)S(1)}, bf16[8,6144]{1,0:T(8,128)(2,1)S(1)}, u32[]{:S(2)}, u32[]{:S(2)}) collective-permute-start(bf16[8,6144]{1,0:T(8,128)(2,1)S(1)} %convert_element_type.80), channel_id=1, source_target_pairs={{0,1},{1,0},{2,3},{3,2},{4,5},{5,4},{6,7},{7,6},{8,9},{9,8},{10,11... | collective-permute-start | bytes 294920 | tf_op jit(solution)/shard_map/ppermute | solution.py:232
  34.0 5.6 %collective-permute-start.15 = (bf16[8,6144]{1,0:T(8,128)(2,1)S(1)}, bf16[8,6144]{1,0:T(8,128)(2,1)S(1)}, u32[]{:S(2)}, u32[]{:S(2)}) collective-permute-start(bf16[8,6144]{1,0:T(8,128)(2,1)S(1)} %convert_element_type.75), channel_id=1, source_target_pairs={{0,4},{1,5},{4,8},{5,9},{8,12},{9,13},{12,14},{13,15},{14,10},{15,... | collective-permute-start | bytes 294920 | tf_op jit(solution)/shard_map/ppermute | solution.py:205
  34.5 6.8 %collective-permute-start.27 = (bf16[8,6144]{1,0:T(8,128)(2,1)S(1)}, bf16[8,6144]{1,0:T(8,128)(2,1)S(1)}, u32[]{:S(2)}, u32[]{:S(2)}) collective-permute-start(bf16[8,6144]{1,0:T(8,128)(2,1)S(1)} %add_convert_fusion.2), channel_id=1, source_target_pairs={{0,4},{1,5},{4,8},{5,9},{8,12},{9,13},{12,14},{13,15},{14,10},{15,... | collective-permute-start | bytes 294920 | tf_op jit(solution)/shard_map/ppermute | solution.py:205
  36.3 5.4 %collective-permute-start.23 = (bf16[8,6144]{1,0:T(8,128)(2,1)S(1)}, bf16[8,6144]{1,0:T(8,128)(2,1)S(1)}, u32[]{:S(2)}, u32[]{:S(2)}) collective-permute-start(bf16[8,6144]{1,0:T(8,128)(2,1)S(1)} %add_convert_fusion.5), channel_id=1, source_target_pairs={{0,2},{1,3},{4,0},{5,1},{8,4},{9,5},{12,8},{13,9},{14,12},{15,13},... | collective-permute-start | bytes 294920 | tf_op jit(solution)/shard_map/ppermute | solution.py:205
  37.7 5.8 %collective-permute-start.20 = (bf16[8,6144]{1,0:T(8,128)(2,1)S(1)}, bf16[8,6144]{1,0:T(8,128)(2,1)S(1)}, u32[]{:S(2)}, u32[]{:S(2)}) collective-permute-start(bf16[8,6144]{1,0:T(8,128)(2,1)S(1)} %add_convert_fusion.7), channel_id=1, source_target_pairs={{0,2},{1,3},{4,0},{5,1},{8,4},{9,5},{12,8},{13,9},{14,12},{15,13},... | collective-permute-start | bytes 294920 | tf_op jit(solution)/shard_map/ppermute | solution.py:205
  39.6 5.3 %collective-permute-start.16 = (bf16[8,6144]{1,0:T(8,128)(2,1)S(1)}, bf16[8,6144]{1,0:T(8,128)(2,1)S(1)}, u32[]{:S(2)}, u32[]{:S(2)}) collective-permute-start(bf16[8,6144]{1,0:T(8,128)(2,1)S(1)} %add_convert_fusion.9), channel_id=1, source_target_pairs={{0,4},{1,5},{4,8},{5,9},{8,12},{9,13},{12,14},{13,15},{14,10},{15,... | collective-permute-start | bytes 294920 | tf_op jit(solution)/shard_map/ppermute | solution.py:205
  41.4 5.1 %collective-permute-start.28 = (bf16[8,6144]{1,0:T(8,128)(2,1)S(1)}, bf16[8,6144]{1,0:T(8,128)(2,1)S(1)}, u32[]{:S(2)}, u32[]{:S(2)}) collective-permute-start(bf16[8,6144]{1,0:T(8,128)(2,1)S(1)} %add_convert_fusion.1), channel_id=1, source_target_pairs={{0,4},{1,5},{4,8},{5,9},{8,12},{9,13},{12,14},{13,15},{14,10},{15,... | collective-permute-start | bytes 294920 | tf_op jit(solution)/shard_map/ppermute | solution.py:205
  41.7 4.8 %collective-permute-start.24 = (bf16[8,6144]{1,0:T(8,128)(2,1)S(1)}, bf16[8,6144]{1,0:T(8,128)(2,1)S(1)}, u32[]{:S(2)}, u32[]{:S(2)}) collective-permute-start(bf16[8,6144]{1,0:T(8,128)(2,1)S(1)} %add_convert_fusion.4), channel_id=1, source_target_pairs={{0,2},{1,3},{4,0},{5,1},{8,4},{9,5},{12,8},{13,9},{14,12},{15,13},... | collective-permute-start | bytes 294920 | tf_op jit(solution)/shard_map/ppermute | solution.py:205
  43.5 5.0 %collective-permute-start.21 = (bf16[8,6144]{1,0:T(8,128)(2,1)S(1)}, bf16[8,6144]{1,0:T(8,128)(2,1)S(1)}, u32[]{:S(2)}, u32[]{:S(2)}) collective-permute-start(bf16[8,6144]{1,0:T(8,128)(2,1)S(1)} %add_convert_fusion.6), channel_id=1, source_target_pairs={{0,3},{1,2},{4,1},{5,0},{8,5},{9,4},{12,9},{13,8},{14,13},{15,12},... | collective-permute-start | bytes 294920 | tf_op jit(solution)/shard_map/ppermute | solution.py:205
  45.0 5.7 %collective-permute-start.17 = (bf16[8,6144]{1,0:T(8,128)(2,1)S(1)}, bf16[8,6144]{1,0:T(8,128)(2,1)S(1)}, u32[]{:S(2)}, u32[]{:S(2)}) collective-permute-start(bf16[8,6144]{1,0:T(8,128)(2,1)S(1)} %add_convert_fusion.8), channel_id=1, source_target_pairs={{0,4},{1,5},{4,8},{5,9},{8,12},{9,13},{12,14},{13,15},{14,10},{15,... | collective-permute-start | bytes 294920 | tf_op jit(solution)/shard_map/ppermute | solution.py:205
  46.4 5.2 %collective-permute-start.29 = (bf16[8,6144]{1,0:T(8,128)(2,1)S(1)}, bf16[8,6144]{1,0:T(8,128)(2,1)S(1)}, u32[]{:S(2)}, u32[]{:S(2)}) collective-permute-start(bf16[8,6144]{1,0:T(8,128)(2,1)S(1)} %add_convert_fusion), channel_id=1, source_target_pairs={{0,5},{1,4},{4,9},{5,8},{8,13},{9,12},{12,15},{13,14},{14,11},{15,... | collective-permute-start | bytes 294920 | tf_op jit(solution)/shard_map/ppermute | solution.py:205
  46.5 5.3 %collective-permute-start.25 = (bf16[8,6144]{1,0:T(8,128)(2,1)S(1)}, bf16[8,6144]{1,0:T(8,128)(2,1)S(1)}, u32[]{:S(2)}, u32[]{:S(2)}) collective-permute-start(bf16[8,6144]{1,0:T(8,128)(2,1)S(1)} %add_convert_fusion.3), channel_id=1, source_target_pairs={{0,2},{1,3},{4,0},{5,1},{8,4},{9,5},{12,8},{13,9},{14,12},{15,13},... | collective-permute-start | bytes 294920 | tf_op jit(solution)/shard_map/ppermute | solution.py:205
  (9 other events, 98.7 us)

commit v7 on v6

--- a/solution.py
+++ b/solution.py
@@ -110,7 +110,7 @@
         in_specs=[in_vmem] * len(parts),
         out_specs=[in_vmem] * 2,
         compiler_params=pltpu.CompilerParams(vmem_limit_bytes=4 * 1024 * 1024),
-        cost_estimate=pl.CostEstimate(flops=4_000_000_000, bytes_accessed=0, transcendentals=0),
+        cost_estimate=pl.CostEstimate(flops=9_000_000_000, bytes_accessed=0, transcendentals=0),
     )(*parts)
 
 

time: 53 us -> 53 us (level)
  no operation moved by 1% of the time
where the time goes in v7:
time: 53 us; the launch traced here: 52.9 us
  starting transfers between devices  29.9 us (56%)
  waiting for transfers between devices  14.9 us (28%)
  Pallas kernels  7.59 us (14%)
    ppermute x28, starting transfers between devices, send(): return lax.ppermute(block, ('tensor', 'expert'), perm)  29.9 us
    ppermute x28, waiting for transfers between devices, send(): return lax.ppermute(block, ('tensor', 'expert'), perm)  14.9 us
    pallas_call x1, Pallas kernels, feed_forward(): pl.pallas_call(functools.partial(feed_forward_kernel, count, capacity), o...  5.14 us
  transfers between devices with their start and end apart: 30, of which 14 were waited for; matrix products, arithmetic and copies ran while one was open for 0% of the time, Pallas kernels for 0%

profile of v7, /device:TPU:0, one launch (start us, length us, event | category | flops | bytes accessed | tf_op | source)
XLA Modules:
  0.0 52.9 jit_solution(5212752429624472031)
XLA Ops:
  0.0 1.1 %shard_map.64 = (s32[2,32]{1,0:T(2,128)S(1)}, f32[2,32]{1,0:T(2,128)S(1)}, bf16[32,6144]{1,0:T(8,128)(2,1)S(1)}) custom-call(s32[2,32]{1,0:T(2,128)} %bitcast.9, f32[2,32]{1,0:T(2,128)} %bitcast.10, bf16[32,6144]{1,0:T(8,128)(2,1)} %refs_2_.1), custom_call_target="tpu_custom_call" | custom-call | tf_op jit(solution)/shard_map/pallas_call | solution.py:44
  1.4 3.0 %collective-permute-start.1 = (bf16[8,6144]{1,0:T(8,128)(2,1)S(1)}, bf16[8,6144]{1,0:T(8,128)(2,1)S(1)}, u32[]{:S(2)}, u32[]{:S(2)}) collective-permute-start(bf16[8,6144]{1,0:T(8,128)(2,1)S(1)} %get-tuple-element.33.refs_0_), channel_id=1, source_target_pairs={{0,2},{1,3},{4,0},{5,1},{8,4},{9,5},{12,8},{13,9},{14,12},{15,13},... | collective-permute-start | bytes 294920 | tf_op jit(solution)/shard_map/ppermute | solution.py:205
  6.3 1.0 %collective-permute-done.1.refs_2_ = bf16[8,6144]{1,0:T(8,128)(2,1)S(1)} collective-permute-done((bf16[8,6144]{1,0:T(8,128)(2,1)S(1)}, bf16[8,6144]{1,0:T(8,128)(2,1)S(1)}, u32[]{:S(2)}, u32[]{:S(2)}) %collective-permute-start.1) | collective-permute-done | bytes 98336 | tf_op jit(solution)/shard_map/ppermute | solution.py:205
  7.3 1.8 %collective-permute-start.3 = (bf16[8,6144]{1,0:T(8,128)(2,1)S(1)}, bf16[8,6144]{1,0:T(8,128)(2,1)S(1)}, u32[]{:S(2)}, u32[]{:S(2)}) collective-permute-start(bf16[8,6144]{1,0:T(8,128)(2,1)S(1)} %collective-permute-done.1.refs_2_), channel_id=1, source_target_pairs={{0,2},{1,3},{4,0},{5,1},{8,4},{9,5},{12,8},{13,9},{14,12},{15,13},... | collective-permute-start | bytes 294920 | tf_op jit(solution)/shard_map/ppermute | solution.py:205
  9.3 1.8 %collective-permute-start.11 = (bf16[8,6144]{1,0:T(8,128)(2,1)S(1)}, bf16[8,6144]{1,0:T(8,128)(2,1)S(1)}, u32[]{:S(2)}, u32[]{:S(2)}) collective-permute-start(bf16[8,6144]{1,0:T(8,128)(2,1)S(1)} %collective-permute-done.9.refs_10_), channel_id=1, source_target_pairs={{0,2},{1,3},{4,0},{5,1},{8,4},{9,5},{12,8},{13,9},{14,12},{15,13},... | collective-permute-start | bytes 294920 | tf_op jit(solution)/shard_map/ppermute | solution.py:205
  11.9 1.8 %collective-permute-start.5 = (bf16[8,6144]{1,0:T(8,128)(2,1)S(1)}, bf16[8,6144]{1,0:T(8,128)(2,1)S(1)}, u32[]{:S(2)}, u32[]{:S(2)}) collective-permute-start(bf16[8,6144]{1,0:T(8,128)(2,1)S(1)} %collective-permute-done.3.refs_4_), channel_id=1, source_target_pairs={{0,2},{1,3},{4,0},{5,1},{8,4},{9,5},{12,8},{13,9},{14,12},{15,13},... | collective-permute-start | bytes 294920 | tf_op jit(solution)/shard_map/ppermute | solution.py:205
  13.7 1.5 %collective-permute-start.6 = (bf16[8,6144]{1,0:T(8,128)(2,1)S(1)}, bf16[8,6144]{1,0:T(8,128)(2,1)S(1)}, u32[]{:S(2)}, u32[]{:S(2)}) collective-permute-start(bf16[8,6144]{1,0:T(8,128)(2,1)S(1)} %collective-permute-done.2.refs_3_), channel_id=1, source_target_pairs={{0,8},{1,9},{4,12},{5,13},{8,14},{9,15},{12,10},{13,11},{14,6},{15... | collective-permute-start | bytes 294920 | tf_op jit(solution)/shard_map/ppermute | solution.py:205
  15.2 1.6 %collective-permute-start.4 = (bf16[8,6144]{1,0:T(8,128)(2,1)S(1)}, bf16[8,6144]{1,0:T(8,128)(2,1)S(1)}, u32[]{:S(2)}, u32[]{:S(2)}) collective-permute-start(bf16[8,6144]{1,0:T(8,128)(2,1)S(1)} %collective-permute-done.2.refs_3_), channel_id=1, source_target_pairs={{0,4},{1,5},{4,8},{5,9},{8,12},{9,13},{12,14},{13,15},{14,10},{15,... | collective-permute-start | bytes 294920 | tf_op jit(solution)/shard_map/ppermute | solution.py:205
  17.3 2.1 %collective-permute-start.13 = (bf16[8,6144]{1,0:T(8,128)(2,1)S(1)}, bf16[8,6144]{1,0:T(8,128)(2,1)S(1)}, u32[]{:S(2)}, u32[]{:S(2)}) collective-permute-start(bf16[8,6144]{1,0:T(8,128)(2,1)S(1)} %collective-permute-done.11.refs_12_), channel_id=1, source_target_pairs={{0,2},{1,3},{4,0},{5,1},{8,4},{9,5},{12,8},{13,9},{14,12},{15,13},... | collective-permute-start | bytes 294920 | tf_op jit(solution)/shard_map/ppermute | solution.py:205
  19.4 2.3 %collective-permute-done.6.refs_7_ = bf16[8,6144]{1,0:T(8,128)(2,1)S(1)} collective-permute-done((bf16[8,6144]{1,0:T(8,128)(2,1)S(1)}, bf16[8,6144]{1,0:T(8,128)(2,1)S(1)}, u32[]{:S(2)}, u32[]{:S(2)}) %collective-permute-start.6) | collective-permute-done | bytes 98336 | tf_op jit(solution)/shard_map/ppermute | solution.py:205
  21.7 2.5 %collective-permute-done.14.refs_15_ = bf16[8,6144]{1,0:T(8,128)(2,1)S(1)} collective-permute-done((bf16[8,6144]{1,0:T(8,128)(2,1)S(1)}, bf16[8,6144]{1,0:T(8,128)(2,1)S(1)}, u32[]{:S(2)}, u32[]{:S(2)}) %collective-permute-start.14) | collective-permute-done | bytes 98336 | tf_op jit(solution)/shard_map/ppermute | solution.py:205
  24.6 5.1 %shard_map.66 = (f32[8,6144]{1,0:T(8,128)S(1)}, f32[8,6144]{1,0:T(8,128)S(1)}, f32[8,6144]{1,0:T(8,128)S(1)}, f32[8,6144]{1,0:T(8,128)S(1)}, f32[8,6144]{1,0:T(8...) custom-call(bf16[8,6144]{1,0:T(8,128)(2,1)S(1)} %get-tuple-element.3, ...), custom_call_target="tpu_custom_call" | custom-call | flops 4831838208 | tf_op jit(solution)/shard_map/pallas_call | solution.py:170
  29.8 1.7 %collective-permute-start.26 = (bf16[8,6144]{1,0:T(8,128)(2,1)S(1)}, bf16[8,6144]{1,0:T(8,128)(2,1)S(1)}, u32[]{:S(2)}, u32[]{:S(2)}) collective-permute-start(bf16[8,6144]{1,0:T(8,128)(2,1)S(1)} %convert_element_type.93), channel_id=1, source_target_pairs={{0,4},{1,5},{4,8},{5,9},{8,12},{9,13},{12,14},{13,15},{14,10},{15,... | collective-permute-start | bytes 294920 | tf_op jit(solution)/shard_map/ppermute | solution.py:205
  32.0 2.0 %collective-permute-start.19 = (bf16[8,6144]{1,0:T(8,128)(2,1)S(1)}, bf16[8,6144]{1,0:T(8,128)(2,1)S(1)}, u32[]{:S(2)}, u32[]{:S(2)}) collective-permute-start(bf16[8,6144]{1,0:T(8,128)(2,1)S(1)} %convert_element_type.81), channel_id=1, source_target_pairs={{0,2},{1,3},{4,0},{5,1},{8,4},{9,5},{12,8},{13,9},{14,12},{15,13},... | collective-permute-start | bytes 294920 | tf_op jit(solution)/shard_map/ppermute | solution.py:205
  34.5 1.7 %collective-permute-start.27 = (bf16[8,6144]{1,0:T(8,128)(2,1)S(1)}, bf16[8,6144]{1,0:T(8,128)(2,1)S(1)}, u32[]{:S(2)}, u32[]{:S(2)}) collective-permute-start(bf16[8,6144]{1,0:T(8,128)(2,1)S(1)} %add_convert_fusion.2), channel_id=1, source_target_pairs={{0,4},{1,5},{4,8},{5,9},{8,12},{9,13},{12,14},{13,15},{14,10},{15,... | collective-permute-start | bytes 294920 | tf_op jit(solution)/shard_map/ppermute | solution.py:205
  36.3 1.3 %collective-permute-start.23 = (bf16[8,6144]{1,0:T(8,128)(2,1)S(1)}, bf16[8,6144]{1,0:T(8,128)(2,1)S(1)}, u32[]{:S(2)}, u32[]{:S(2)}) collective-permute-start(bf16[8,6144]{1,0:T(8,128)(2,1)S(1)} %add_convert_fusion.5), channel_id=1, source_target_pairs={{0,2},{1,3},{4,0},{5,1},{8,4},{9,5},{12,8},{13,9},{14,12},{15,13},... | collective-permute-start | bytes 294920 | tf_op jit(solution)/shard_map/ppermute | solution.py:205
  37.7 1.6 %collective-permute-start.20 = (bf16[8,6144]{1,0:T(8,128)(2,1)S(1)}, bf16[8,6144]{1,0:T(8,128)(2,1)S(1)}, u32[]{:S(2)}, u32[]{:S(2)}) collective-permute-start(bf16[8,6144]{1,0:T(8,128)(2,1)S(1)} %add_convert_fusion.7), channel_id=1, source_target_pairs={{0,2},{1,3},{4,0},{5,1},{8,4},{9,5},{12,8},{13,9},{14,12},{15,13},... | collective-permute-start | bytes 294920 | tf_op jit(solution)/shard_map/ppermute | solution.py:205
  39.9 1.5 %collective-permute-done.27 = bf16[8,6144]{1,0:T(8,128)(2,1)S(1)} collective-permute-done((bf16[8,6144]{1,0:T(8,128)(2,1)S(1)}, bf16[8,6144]{1,0:T(8,128)(2,1)S(1)}, u32[]{:S(2)}, u32[]{:S(2)}) %collective-permute-start.27) | collective-permute-done | bytes 98336 | tf_op jit(solution)/shard_map/ppermute | solution.py:205
  41.7 1.8 %collective-permute-start.24 = (bf16[8,6144]{1,0:T(8,128)(2,1)S(1)}, bf16[8,6144]{1,0:T(8,128)(2,1)S(1)}, u32[]{:S(2)}, u32[]{:S(2)}) collective-permute-start(bf16[8,6144]{1,0:T(8,128)(2,1)S(1)} %add_convert_fusion.4), channel_id=1, source_target_pairs={{0,2},{1,3},{4,0},{5,1},{8,4},{9,5},{12,8},{13,9},{14,12},{15,13},... | collective-permute-start | bytes 294920 | tf_op jit(solution)/shard_map/ppermute | solution.py:205
  43.9 1.0 %collective-permute-done.16 = bf16[8,6144]{1,0:T(8,128)(2,1)S(1)} collective-permute-done((bf16[8,6144]{1,0:T(8,128)(2,1)S(1)}, bf16[8,6144]{1,0:T(8,128)(2,1)S(1)}, u32[]{:S(2)}, u32[]{:S(2)}) %collective-permute-start.16) | collective-permute-done | bytes 98336 | tf_op jit(solution)/shard_map/ppermute | solution.py:205
  45.1 1.4 %collective-permute-done.28 = bf16[8,6144]{1,0:T(8,128)(2,1)S(1)} collective-permute-done((bf16[8,6144]{1,0:T(8,128)(2,1)S(1)}, bf16[8,6144]{1,0:T(8,128)(2,1)S(1)}, u32[]{:S(2)}, u32[]{:S(2)}) %collective-permute-start.28) | collective-permute-done | bytes 98336 | tf_op jit(solution)/shard_map/ppermute | solution.py:205
  46.5 1.7 %collective-permute-start.25 = (bf16[8,6144]{1,0:T(8,128)(2,1)S(1)}, bf16[8,6144]{1,0:T(8,128)(2,1)S(1)}, u32[]{:S(2)}, u32[]{:S(2)}) collective-permute-start(bf16[8,6144]{1,0:T(8,128)(2,1)S(1)} %add_convert_fusion.3), channel_id=1, source_target_pairs={{0,2},{1,3},{4,0},{5,1},{8,4},{9,5},{12,8},{13,9},{14,12},{15,13},... | collective-permute-start | bytes 294920 | tf_op jit(solution)/shard_map/ppermute | solution.py:205
  48.5 2.1 %collective-permute-done.17.refs_1_ = bf16[8,6144]{1,0:T(8,128)(2,1)S(1)} collective-permute-done((bf16[8,6144]{1,0:T(8,128)(2,1)S(1)}, bf16[8,6144]{1,0:T(8,128)(2,1)S(1)}, u32[]{:S(2)}, u32[]{:S(2)}) %collective-permute-start.17) | collective-permute-done | bytes 98336 | tf_op jit(solution)/shard_map/ppermute | solution.py:205
  51.8 1.1 %shard_map.68 = bf16[32,6144]{1,0:T(8,128)(2,1)} custom-call(f32[16,32]{1,0:T(8,128)S(1)} %get-tuple-element.32.coefficient, f32[8,6144]{1,0:T(8,128)S(1)} %get-tuple-element.43.refs_0_, bf16[8,6144]{1,0:T(8,128)(2,1)S(1)} %collective-permute-done.25.refs_1_, f32[8,6144]{1,0:T(8,128)S(1)} %get-tuple-element.48.refs_2_, ...), custom_call_target="tpu_custom_call" | custom-call | tf_op jit(solution)/shard_map/pallas_call | solution.py:142
  (62 shorter events, 8.2 us)
Async XLA Ops:
  1.4 5.9 %collective-permute-start.1 = (bf16[8,6144]{1,0:T(8,128)(2,1)S(1)}, bf16[8,6144]{1,0:T(8,128)(2,1)S(1)}, u32[]{:S(2)}, u32[]{:S(2)}) collective-permute-start(bf16[8,6144]{1,0:T(8,128)(2,1)S(1)} %get-tuple-element.33.refs_0_), channel_id=1, source_target_pairs={{0,2},{1,3},{4,0},{5,1},{8,4},{9,5},{12,8},{13,9},{14,12},{15,13},... | collective-permute-start | bytes 294920 | tf_op jit(solution)/shard_map/ppermute | solution.py:205
  5.3 5.8 %collective-permute-start.8 = (bf16[8,6144]{1,0:T(8,128)(2,1)S(1)}, bf16[8,6144]{1,0:T(8,128)(2,1)S(1)}, u32[]{:S(2)}, u32[]{:S(2)}) collective-permute-start(bf16[8,6144]{1,0:T(8,128)(2,1)S(1)} %get-tuple-element.34), channel_id=1, source_target_pairs={{0,5},{1,4},{4,9},{5,8},{8,13},{9,12},{12,15},{13,14},{14,11},{15,... | collective-permute-start | bytes 294920 | tf_op jit(solution)/shard_map/ppermute | solution.py:205
  9.3 5.9 %collective-permute-start.7 = (bf16[8,6144]{1,0:T(8,128)(2,1)S(1)}, bf16[8,6144]{1,0:T(8,128)(2,1)S(1)}, u32[]{:S(2)}, u32[]{:S(2)}) collective-permute-start(bf16[8,6144]{1,0:T(8,128)(2,1)S(1)} %get-tuple-element.34), channel_id=1, source_target_pairs={{0,1},{1,0},{2,3},{3,2},{4,5},{5,4},{6,7},{7,6},{8,9},{9,8},{10,11... | collective-permute-start | bytes 294920 | tf_op jit(solution)/shard_map/ppermute | solution.py:208
  9.3 7.5 %collective-permute-start.11 = (bf16[8,6144]{1,0:T(8,128)(2,1)S(1)}, bf16[8,6144]{1,0:T(8,128)(2,1)S(1)}, u32[]{:S(2)}, u32[]{:S(2)}) collective-permute-start(bf16[8,6144]{1,0:T(8,128)(2,1)S(1)} %collective-permute-done.9.refs_10_), channel_id=1, source_target_pairs={{0,2},{1,3},{4,0},{5,1},{8,4},{9,5},{12,8},{13,9},{14,12},{15,13},... | collective-permute-start | bytes 294920 | tf_op jit(solution)/shard_map/ppermute | solution.py:205
  11.2 6.2 %collective-permute-start.10 = (bf16[8,6144]{1,0:T(8,128)(2,1)S(1)}, bf16[8,6144]{1,0:T(8,128)(2,1)S(1)}, u32[]{:S(2)}, u32[]{:S(2)}) collective-permute-start(bf16[8,6144]{1,0:T(8,128)(2,1)S(1)} %collective-permute-done.8.refs_9_), channel_id=1, source_target_pairs={{0,4},{1,5},{4,8},{5,9},{8,12},{9,13},{12,14},{13,15},{14,10},{15,... | collective-permute-start | bytes 294920 | tf_op jit(solution)/shard_map/ppermute | solution.py:205
  11.9 7.5 %collective-permute-start.5 = (bf16[8,6144]{1,0:T(8,128)(2,1)S(1)}, bf16[8,6144]{1,0:T(8,128)(2,1)S(1)}, u32[]{:S(2)}, u32[]{:S(2)}) collective-permute-start(bf16[8,6144]{1,0:T(8,128)(2,1)S(1)} %collective-permute-done.3.refs_4_), channel_id=1, source_target_pairs={{0,2},{1,3},{4,0},{5,1},{8,4},{9,5},{12,8},{13,9},{14,12},{15,13},... | collective-permute-start | bytes 294920 | tf_op jit(solution)/shard_map/ppermute | solution.py:205
  13.7 8.0 %collective-permute-start.6 = (bf16[8,6144]{1,0:T(8,128)(2,1)S(1)}, bf16[8,6144]{1,0:T(8,128)(2,1)S(1)}, u32[]{:S(2)}, u32[]{:S(2)}) collective-permute-start(bf16[8,6144]{1,0:T(8,128)(2,1)S(1)} %collective-permute-done.2.refs_3_), channel_id=1, source_target_pairs={{0,8},{1,9},{4,12},{5,13},{8,14},{9,15},{12,10},{13,11},{14,6},{15... | collective-permute-start | bytes 294920 | tf_op jit(solution)/shard_map/ppermute | solution.py:205
  15.2 6.5 %collective-permute-start.4 = (bf16[8,6144]{1,0:T(8,128)(2,1)S(1)}, bf16[8,6144]{1,0:T(8,128)(2,1)S(1)}, u32[]{:S(2)}, u32[]{:S(2)}) collective-permute-start(bf16[8,6144]{1,0:T(8,128)(2,1)S(1)} %collective-permute-done.2.refs_3_), channel_id=1, source_target_pairs={{0,4},{1,5},{4,8},{5,9},{8,12},{9,13},{12,14},{13,15},{14,10},{15,... | collective-permute-start | bytes 294920 | tf_op jit(solution)/shard_map/ppermute | solution.py:205
  16.8 7.5 %collective-permute-start.14 = (bf16[8,6144]{1,0:T(8,128)(2,1)S(1)}, bf16[8,6144]{1,0:T(8,128)(2,1)S(1)}, u32[]{:S(2)}, u32[]{:S(2)}) collective-permute-start(bf16[8,6144]{1,0:T(8,128)(2,1)S(1)} %collective-permute-done.11.refs_12_), channel_id=1, source_target_pairs={{0,6},{1,7},{4,2},{5,3},{8,0},{9,1},{12,4},{13,5},{14,8},{15,9},{1... | collective-permute-start | bytes 294920 | tf_op jit(solution)/shard_map/ppermute | solution.py:205
  17.3 7.3 %collective-permute-start.13 = (bf16[8,6144]{1,0:T(8,128)(2,1)S(1)}, bf16[8,6144]{1,0:T(8,128)(2,1)S(1)}, u32[]{:S(2)}, u32[]{:S(2)}) collective-permute-start(bf16[8,6144]{1,0:T(8,128)(2,1)S(1)} %collective-permute-done.11.refs_12_), channel_id=1, source_target_pairs={{0,2},{1,3},{4,0},{5,1},{8,4},{9,5},{12,8},{13,9},{14,12},{15,13},... | collective-permute-start | bytes 294920 | tf_op jit(solution)/shard_map/ppermute | solution.py:205
  19.4 5.2 %collective-permute-start.12 = (bf16[8,6144]{1,0:T(8,128)(2,1)S(1)}, bf16[8,6144]{1,0:T(8,128)(2,1)S(1)}, u32[]{:S(2)}, u32[]{:S(2)}) collective-permute-start(bf16[8,6144]{1,0:T(8,128)(2,1)S(1)} %collective-permute-done.10.refs_11_), channel_id=1, source_target_pairs={{0,4},{1,5},{4,8},{5,9},{8,12},{9,13},{12,14},{13,15},{14,10},{15,... | collective-permute-start | bytes 294920 | tf_op jit(solution)/shard_map/ppermute | solution.py:205
  32.0 5.6 %collective-permute-start.19 = (bf16[8,6144]{1,0:T(8,128)(2,1)S(1)}, bf16[8,6144]{1,0:T(8,128)(2,1)S(1)}, u32[]{:S(2)}, u32[]{:S(2)}) collective-permute-start(bf16[8,6144]{1,0:T(8,128)(2,1)S(1)} %convert_element_type.81), channel_id=1, source_target_pairs={{0,2},{1,3},{4,0},{5,1},{8,4},{9,5},{12,8},{13,9},{14,12},{15,13},... | collective-permute-start | bytes 294920 | tf_op jit(solution)/shard_map/ppermute | solution.py:205
  34.0 14.2 %collective-permute-start.18 = (bf16[8,6144]{1,0:T(8,128)(2,1)S(1)}, bf16[8,6144]{1,0:T(8,128)(2,1)S(1)}, u32[]{:S(2)}, u32[]{:S(2)}) collective-permute-start(bf16[8,6144]{1,0:T(8,128)(2,1)S(1)} %convert_element_type.80), channel_id=1, source_target_pairs={{0,1},{1,0},{2,3},{3,2},{4,5},{5,4},{6,7},{7,6},{8,9},{9,8},{10,11... | collective-permute-start | bytes 294920 | tf_op jit(solution)/shard_map/ppermute | solution.py:232
  34.0 5.6 %collective-permute-start.15 = (bf16[8,6144]{1,0:T(8,128)(2,1)S(1)}, bf16[8,6144]{1,0:T(8,128)(2,1)S(1)}, u32[]{:S(2)}, u32[]{:S(2)}) collective-permute-start(bf16[8,6144]{1,0:T(8,128)(2,1)S(1)} %convert_element_type.75), channel_id=1, source_target_pairs={{0,4},{1,5},{4,8},{5,9},{8,12},{9,13},{12,14},{13,15},{14,10},{15,... | collective-permute-start | bytes 294920 | tf_op jit(solution)/shard_map/ppermute | solution.py:205
  34.5 6.8 %collective-permute-start.27 = (bf16[8,6144]{1,0:T(8,128)(2,1)S(1)}, bf16[8,6144]{1,0:T(8,128)(2,1)S(1)}, u32[]{:S(2)}, u32[]{:S(2)}) collective-permute-start(bf16[8,6144]{1,0:T(8,128)(2,1)S(1)} %add_convert_fusion.2), channel_id=1, source_target_pairs={{0,4},{1,5},{4,8},{5,9},{8,12},{9,13},{12,14},{13,15},{14,10},{15,... | collective-permute-start | bytes 294920 | tf_op jit(solution)/shard_map/ppermute | solution.py:205
  36.3 5.4 %collective-permute-start.23 = (bf16[8,6144]{1,0:T(8,128)(2,1)S(1)}, bf16[8,6144]{1,0:T(8,128)(2,1)S(1)}, u32[]{:S(2)}, u32[]{:S(2)}) collective-permute-start(bf16[8,6144]{1,0:T(8,128)(2,1)S(1)} %add_convert_fusion.5), channel_id=1, source_target_pairs={{0,2},{1,3},{4,0},{5,1},{8,4},{9,5},{12,8},{13,9},{14,12},{15,13},... | collective-permute-start | bytes 294920 | tf_op jit(solution)/shard_map/ppermute | solution.py:205
  37.7 5.8 %collective-permute-start.20 = (bf16[8,6144]{1,0:T(8,128)(2,1)S(1)}, bf16[8,6144]{1,0:T(8,128)(2,1)S(1)}, u32[]{:S(2)}, u32[]{:S(2)}) collective-permute-start(bf16[8,6144]{1,0:T(8,128)(2,1)S(1)} %add_convert_fusion.7), channel_id=1, source_target_pairs={{0,2},{1,3},{4,0},{5,1},{8,4},{9,5},{12,8},{13,9},{14,12},{15,13},... | collective-permute-start | bytes 294920 | tf_op jit(solution)/shard_map/ppermute | solution.py:205
  39.6 5.3 %collective-permute-start.16 = (bf16[8,6144]{1,0:T(8,128)(2,1)S(1)}, bf16[8,6144]{1,0:T(8,128)(2,1)S(1)}, u32[]{:S(2)}, u32[]{:S(2)}) collective-permute-start(bf16[8,6144]{1,0:T(8,128)(2,1)S(1)} %add_convert_fusion.9), channel_id=1, source_target_pairs={{0,4},{1,5},{4,8},{5,9},{8,12},{9,13},{12,14},{13,15},{14,10},{15,... | collective-permute-start | bytes 294920 | tf_op jit(solution)/shard_map/ppermute | solution.py:205
  41.4 5.1 %collective-permute-start.28 = (bf16[8,6144]{1,0:T(8,128)(2,1)S(1)}, bf16[8,6144]{1,0:T(8,128)(2,1)S(1)}, u32[]{:S(2)}, u32[]{:S(2)}) collective-permute-start(bf16[8,6144]{1,0:T(8,128)(2,1)S(1)} %add_convert_fusion.1), channel_id=1, source_target_pairs={{0,4},{1,5},{4,8},{5,9},{8,12},{9,13},{12,14},{13,15},{14,10},{15,... | collective-permute-start | bytes 294920 | tf_op jit(solution)/shard_map/ppermute | solution.py:205
  41.7 4.8 %collective-permute-start.24 = (bf16[8,6144]{1,0:T(8,128)(2,1)S(1)}, bf16[8,6144]{1,0:T(8,128)(2,1)S(1)}, u32[]{:S(2)}, u32[]{:S(2)}) collective-permute-start(bf16[8,6144]{1,0:T(8,128)(2,1)S(1)} %add_convert_fusion.4), channel_id=1, source_target_pairs={{0,2},{1,3},{4,0},{5,1},{8,4},{9,5},{12,8},{13,9},{14,12},{15,13},... | collective-permute-start | bytes 294920 | tf_op jit(solution)/shard_map/ppermute | solution.py:205
  43.5 5.0 %collective-permute-start.21 = (bf16[8,6144]{1,0:T(8,128)(2,1)S(1)}, bf16[8,6144]{1,0:T(8,128)(2,1)S(1)}, u32[]{:S(2)}, u32[]{:S(2)}) collective-permute-start(bf16[8,6144]{1,0:T(8,128)(2,1)S(1)} %add_convert_fusion.6), channel_id=1, source_target_pairs={{0,3},{1,2},{4,1},{5,0},{8,5},{9,4},{12,9},{13,8},{14,13},{15,12},... | collective-permute-start | bytes 294920 | tf_op jit(solution)/shard_map/ppermute | solution.py:205
  45.0 5.7 %collective-permute-start.17 = (bf16[8,6144]{1,0:T(8,128)(2,1)S(1)}, bf16[8,6144]{1,0:T(8,128)(2,1)S(1)}, u32[]{:S(2)}, u32[]{:S(2)}) collective-permute-start(bf16[8,6144]{1,0:T(8,128)(2,1)S(1)} %add_convert_fusion.8), channel_id=1, source_target_pairs={{0,4},{1,5},{4,8},{5,9},{8,12},{9,13},{12,14},{13,15},{14,10},{15,... | collective-permute-start | bytes 294920 | tf_op jit(solution)/shard_map/ppermute | solution.py:205
  46.4 5.2 %collective-permute-start.29 = (bf16[8,6144]{1,0:T(8,128)(2,1)S(1)}, bf16[8,6144]{1,0:T(8,128)(2,1)S(1)}, u32[]{:S(2)}, u32[]{:S(2)}) collective-permute-start(bf16[8,6144]{1,0:T(8,128)(2,1)S(1)} %add_convert_fusion), channel_id=1, source_target_pairs={{0,5},{1,4},{4,9},{5,8},{8,13},{9,12},{12,15},{13,14},{14,11},{15,... | collective-permute-start | bytes 294920 | tf_op jit(solution)/shard_map/ppermute | solution.py:205
  46.5 5.3 %collective-permute-start.25 = (bf16[8,6144]{1,0:T(8,128)(2,1)S(1)}, bf16[8,6144]{1,0:T(8,128)(2,1)S(1)}, u32[]{:S(2)}, u32[]{:S(2)}) collective-permute-start(bf16[8,6144]{1,0:T(8,128)(2,1)S(1)} %add_convert_fusion.3), channel_id=1, source_target_pairs={{0,2},{1,3},{4,0},{5,1},{8,4},{9,5},{12,8},{13,9},{14,12},{15,13},... | collective-permute-start | bytes 294920 | tf_op jit(solution)/shard_map/ppermute | solution.py:205
  (9 other events, 98.7 us)
